TPU v7x, 32 devices: a whole 2x2x4 slice. The times are simulated.
32 devices in a mesh: dp: 8 (over z, y), tensor: 4 (over x, core).
Axes of the slice: x: 2, y: 2, z: 4, core: 2. Of those that a mesh axis runs over, the one named last changes fastest.
Arguments:
- latents: bfloat16 [8192, 1536], P(('dp', 'tensor')), may hold values from -6 to 6
- cotangent: float32 [8192, 1536], P(('dp', 'tensor')), may hold values from -6 to 6
- captions: bfloat16 [16384, 4096], P('dp', 'tensor'), may hold values from -17 to 17, as said below
- conditions: float32 [64, 1024], replicated, may hold values from -6 to 6
- image_ids: int32 [8, 1024], P('dp'), may hold values from 0 to 7, never falling along the last dimension, each value on 1 to 512 neighbouring positions
- rope_rows: int32 [8, 1024], P('dp'), may hold values from 0 to 47
- rope_cols: int32 [8, 1024], P('dp'), may hold values from 0 to 47
- caption_lengths: int32 [8, 8], P('dp'), may hold values from 1 to 256
- attention_in: float32 [3, 1536, 1536], P(None, 'dp', 'tensor'), may hold values from -0.15625 to 0.15625
- attention_out: float32 [1536, 1536], P('tensor', 'dp'), may hold values from -0.15625 to 0.15625
- feed_in: float32 [2, 1536, 4096], P(None, 'dp', 'tensor'), may hold values from -0.15625 to 0.15625
- feed_out: float32 [4096, 1536], P('tensor', 'dp'), may hold values from -0.09375 to 0.09375
- caption_in: float32 [2, 4096, 1536], P(None, 'tensor', 'dp'), may hold values from -0.09375 to 0.09375
- modulator: float32 [1025, 6144], P(None, ('dp', 'tensor')), may hold values from -0.1875 to 0.1875
- channels: float32 [8, 1536], P(None, 'dp'), may hold values from 0.2 to 2.3, as said below
- moment_attention_in: float32 [3, 1536, 1536], P(None, 'dp', 'tensor'), may hold values from -9.1552734e-05 to 9.1552734e-05
- square_attention_in: float32 [3, 1536, 1536], P(None, 'dp', 'tensor'), may hold values from 1.1227779e-09 to 4.4487423e-09
- moment_attention_out: float32 [1536, 1536], P('tensor', 'dp'), may hold values from -9.1552734e-05 to 9.1552734e-05
- square_attention_out: float32 [1536, 1536], P('tensor', 'dp'), may hold values from 1.1227779e-09 to 4.4487423e-09
- moment_feed_in: float32 [2, 1536, 4096], P(None, 'dp', 'tensor'), may hold values from -9.1552734e-05 to 9.1552734e-05
- square_feed_in: float32 [2, 1536, 4096], P(None, 'dp', 'tensor'), may hold values from 1.1227779e-09 to 4.4487423e-09
- moment_feed_out: float32 [4096, 1536], P('tensor', 'dp'), may hold values from -9.1552734e-05 to 9.1552734e-05
- square_feed_out: float32 [4096, 1536], P('tensor', 'dp'), may hold values from 1.1227779e-09 to 4.4487423e-09
- moment_caption_in: float32 [2, 4096, 1536], P(None, 'tensor', 'dp'), may hold values from -9.1552734e-05 to 9.1552734e-05
- square_caption_in: float32 [2, 4096, 1536], P(None, 'tensor', 'dp'), may hold values from 1.1227779e-09 to 4.4487423e-09
- moment_modulator: float32 [1025, 6144], P(None, ('dp', 'tensor')), may hold values from -9.1552734e-05 to 9.1552734e-05
- square_modulator: float32 [1025, 6144], P(None, ('dp', 'tensor')), may hold values from 1.1227779e-09 to 4.4487423e-09
- moment_channels: float32 [8, 1536], P(None, 'dp'), may hold values from -0.00036621094 to 0.00036621094
- square_channels: float32 [8, 1536], P(None, 'dp'), may hold values from 3.389518e-09 to 1.3558072e-08
Outputs:
- block_out: float32 [8192, 1536], P(('dp', 'tensor'))
- latent_grad: float32 [8192, 1536], P(('dp', 'tensor'))
- grad_norm: float32 [], replicated
- moment_attention_in_new: float32 [3, 1536, 1536], P(None, 'dp', 'tensor')
- square_attention_in_new: float32 [3, 1536, 1536], P(None, 'dp', 'tensor')
- attention_in_new: float32 [3, 1536, 1536], P(None, 'dp', 'tensor')
- moment_attention_out_new: float32 [1536, 1536], P('tensor', 'dp')
- square_attention_out_new: float32 [1536, 1536], P('tensor', 'dp')
- attention_out_new: float32 [1536, 1536], P('tensor', 'dp')
- moment_feed_in_new: float32 [2, 1536, 4096], P(None, 'dp', 'tensor')
- square_feed_in_new: float32 [2, 1536, 4096], P(None, 'dp', 'tensor')
- feed_in_new: float32 [2, 1536, 4096], P(None, 'dp', 'tensor')
- moment_feed_out_new: float32 [4096, 1536], P('tensor', 'dp')
- square_feed_out_new: float32 [4096, 1536], P('tensor', 'dp')
- feed_out_new: float32 [4096, 1536], P('tensor', 'dp')
- moment_caption_in_new: float32 [2, 4096, 1536], P(None, 'tensor', 'dp')
- square_caption_in_new: float32 [2, 4096, 1536], P(None, 'tensor', 'dp')
- caption_in_new: float32 [2, 4096, 1536], P(None, 'tensor', 'dp')
- moment_modulator_new: float32 [1025, 6144], P(None, ('dp', 'tensor'))
- square_modulator_new: float32 [1025, 6144], P(None, ('dp', 'tensor'))
- modulator_new: float32 [1025, 6144], P(None, ('dp', 'tensor'))
- moment_channels_new: float32 [8, 1536], P(None, 'dp')
- square_channels_new: float32 [8, 1536], P(None, 'dp')
- channels_new: float32 [8, 1536], P(None, 'dp')
Inputs may be any that keep to these rules, and one draw needn't show every extreme that they name: `image_ids`: each row holds all 8 images as runs of consecutive tokens numbered in order, none longer than 512 tokens. `captions`: caption features of order one. `channels`: positive gains and gate values of order one.
All inputs are finite; a program needn't handle non-finite values.
Results may differ from a plain program's by a relative error of at most 0.015.
The roundings to bfloat16 on the way count: a program that leaves them out, or rounds other values in their place, can miss the bound.
Values may be sent and summed in bfloat16 or wider, within the bound.
A program may use at most 320 MiB of HBM per device.

v0:
```python
import jax
import jax.numpy as jnp
from jax import lax
from jax.sharding import PartitionSpec as P

HEAD = 64
CAP = 256
STEP = 10


EPS = 1e-06
NEG = -1e30
THETA = 10000.0
BETA1 = 0.9
BETA2 = 0.95
RATE = 0.05
GAIN_RATE = 0.8
DECAY = 0.1
ADAM_EPS = 1e-08
CLIP = 1.0
HIGH = lax.Precision.HIGHEST


def half(value):
    return value.astype(jnp.bfloat16)


def rms_parts(value):
    inverse = lax.rsqrt(jnp.mean(value * value, axis=-1, keepdims=True) + EPS)
    return (value * inverse, inverse)


def rms_back(normed, inverse, grad):
    return inverse * (grad - normed * jnp.mean(grad * normed, axis=-1, keepdims=True))


def rope_tables(rows, columns, head):
    quarter = head // 4
    frequency = THETA ** (-jnp.arange(quarter, dtype=jnp.float32) / quarter)
    angles = jnp.concatenate(
        [
            rows.astype(jnp.float32)[:, None] * frequency[None, :],
            columns.astype(jnp.float32)[:, None] * frequency[None, :],
        ],
        axis=1,
    )
    return (jnp.cos(angles)[:, None, :], jnp.sin(angles)[:, None, :])


def rotate(value, cosine, sine):
    middle = value.shape[-1] // 2
    first = value[..., :middle]
    second = value[..., middle:]
    return jnp.concatenate(
        [first * cosine - second * sine, second * cosine + first * sine], axis=-1
    )


def spread_rows(value):
    return lax.all_gather(value, "tensor", axis=0, tiled=True)


def collect_rows(value):
    return lax.psum_scatter(value, "tensor", scatter_dimension=0, tiled=True)


def attend(query, keys, values, allowed, scale):
    scores = jnp.einsum("qhd,khd->hqk", query, keys, preferred_element_type=jnp.float32) * scale
    scores = jnp.where(allowed[None], scores, NEG)
    top = jnp.max(scores, axis=-1, keepdims=True)
    expo = jnp.exp(scores - top)
    total = jnp.sum(expo, axis=-1, keepdims=True)
    output = jnp.einsum(
        "hqk,khd->qhd", half(expo / total), values, preferred_element_type=jnp.float32
    )
    return (output, (top + jnp.log(total))[..., 0])


def attend_back(query, keys, values, allowed, scale, logsum, out_grad):
    scores = jnp.einsum("qhd,khd->hqk", query, keys, preferred_element_type=jnp.float32) * scale
    scores = jnp.where(allowed[None], scores, NEG)
    probs = jnp.exp(scores - logsum[..., None])
    prob_grad = jnp.einsum("qhd,khd->hqk", out_grad, values, preferred_element_type=jnp.float32)
    centre = jnp.sum(probs * prob_grad, axis=-1, keepdims=True)
    score_grad = half(probs * (prob_grad - centre))
    query_grad = (
        jnp.einsum("hqk,khd->qhd", score_grad, keys, preferred_element_type=jnp.float32) * scale
    )
    key_grad = (
        jnp.einsum("hqk,qhd->khd", score_grad, query, preferred_element_type=jnp.float32) * scale
    )
    value_grad = jnp.einsum(
        "hqk,qhd->khd", half(probs), out_grad, preferred_element_type=jnp.float32
    )
    return (query_grad, key_grad, value_grad)


def adamw(grad, weight, moment, square, decay, rate):
    moment_new = BETA1 * moment + (1.0 - BETA1) * grad
    square_new = BETA2 * square + (1.0 - BETA2) * grad * grad
    step_size = (
        moment_new / (1.0 - BETA1**STEP) / (jnp.sqrt(square_new / (1.0 - BETA2**STEP)) + ADAM_EPS)
    )
    return (moment_new, square_new, weight - rate * (step_size + decay * weight))


def body(
    latents,
    cotangent,
    captions,
    conditions,
    image_ids,
    rope_rows,
    rope_cols,
    caption_lengths,
    attention_in,
    attention_out,
    feed_in,
    feed_out,
    caption_in,
    modulator,
    channels,
    moment_attention_in,
    square_attention_in,
    moment_attention_out,
    square_attention_out,
    moment_feed_in,
    square_feed_in,
    moment_feed_out,
    square_feed_out,
    moment_caption_in,
    square_caption_in,
    moment_modulator,
    square_modulator,
    moment_channels,
    square_channels,
):
    tensor_size = lax.axis_size("tensor")
    tensor_index = lax.axis_index("tensor")
    row_index = lax.axis_index("dp")
    shard_rows, width = latents.shape
    local = attention_in.shape[2]
    local_heads = local // HEAD
    segment = image_ids[0]
    row_tokens = segment.shape[0]
    images = conditions.shape[0]
    per_row = caption_lengths.shape[1]
    slots = captions.shape[0]
    scale = HEAD ** (-0.5)
    offset = tensor_index * local
    own_ids = lax.dynamic_slice_in_dim(segment, tensor_index * shard_rows, shard_rows)
    in_full, out_full, feed_full, down_full, caption_full, channel_half = (
        lax.all_gather(half(attention_in), "dp", axis=1, tiled=True),
        lax.all_gather(half(attention_out), "dp", axis=1, tiled=True),
        lax.all_gather(half(feed_in), "dp", axis=1, tiled=True),
        lax.all_gather(half(feed_out), "dp", axis=1, tiled=True),
        lax.all_gather(half(caption_in), "dp", axis=2, tiled=True),
        lax.all_gather(half(channels), "dp", axis=1, tiled=True),
    )
    gains = channel_half.astype(jnp.float32)
    local_gains = lax.dynamic_slice_in_dim(gains, offset, local, 1).reshape(8, local_heads, HEAD)
    augmented = half(
        jnp.concatenate([jax.nn.silu(conditions), jnp.ones((images, 1), jnp.float32)], axis=1)
    )
    factor_part = jnp.dot(augmented, half(modulator), preferred_element_type=jnp.float32)
    factor_all = lax.all_gather(factor_part, ("dp", "tensor"), axis=1, tiled=True)
    factor_row = lax.dynamic_slice_in_dim(factor_all, row_index * per_row, per_row, 0)
    chooser = (own_ids[:, None] == jnp.arange(per_row, dtype=jnp.int32)[None, :]).astype(
        jnp.float32
    )
    token_factor = jnp.dot(chooser, factor_row, precision=HIGH)
    scale_attn = token_factor[:, :width]
    gate_attn = token_factor[:, width : 2 * width]
    scale_feed = token_factor[:, 2 * width : 3 * width]
    gate_feed = token_factor[:, 3 * width :]
    caption_part = jnp.einsum(
        "ct,ktd->ckd", captions, caption_full, preferred_element_type=jnp.float32
    )
    caption_pair = lax.psum_scatter(caption_part, "tensor", scatter_dimension=2, tiled=True)
    text_key_norm, text_key_inv = rms_parts(caption_pair[:, 0].reshape(slots, local_heads, HEAD))
    text_keys = half(text_key_norm * local_gains[6])
    text_values = half(caption_pair[:, 1].reshape(slots, local_heads, HEAD))
    source = latents.astype(jnp.float32)
    attn_norm, attn_inv = rms_parts(source)
    attn_full = spread_rows(half(attn_norm * gains[0] * (1.0 + scale_attn)))
    projected = jnp.einsum("td,kde->kte", attn_full, in_full, preferred_element_type=jnp.float32)
    query_norm, query_inv = rms_parts(projected[0].reshape(row_tokens, local_heads, HEAD))
    key_norm, key_inv = rms_parts(projected[1].reshape(row_tokens, local_heads, HEAD))
    cosine, sine = rope_tables(rope_rows[0], rope_cols[0], HEAD)
    queries = half(rotate(query_norm * local_gains[4], cosine, sine))
    keys = half(rotate(key_norm * local_gains[5], cosine, sine))
    values = half(projected[2].reshape(row_tokens, local_heads, HEAD))
    slot_ids = jnp.arange(slots, dtype=jnp.int32)
    slot_image = slot_ids // CAP
    slot_limit = jnp.sum(
        jnp.where(
            slot_image[:, None] == jnp.arange(per_row, dtype=jnp.int32)[None, :],
            caption_lengths[0][None, :],
            0,
        ),
        axis=1,
    )
    slot_live = slot_ids % CAP < slot_limit
    block = min(512, row_tokens)
    count = row_tokens // block
    query_blocks = queries.reshape(count, block, local_heads, HEAD)
    id_blocks = segment.reshape(count, block)

    def forward_block(carry, inputs):
        query, ids = inputs
        own, own_sum = attend(query, keys, values, ids[:, None] == segment[None, :], scale)
        cross_mask = (ids[:, None] == slot_image[None, :]) & slot_live[None, :]
        other, other_sum = attend(query, text_keys, text_values, cross_mask, scale)
        return (carry, (own, other, own_sum, other_sum))

    unused, (own_out, other_out, own_lse, other_lse) = lax.scan(
        forward_block, jnp.zeros((), jnp.float32), (query_blocks, id_blocks)
    )
    own_out = own_out.reshape(row_tokens, local_heads, HEAD)
    other_out = other_out.reshape(row_tokens, local_heads, HEAD)
    cross_gate = jnp.tanh(local_gains[7])
    mixed = half(own_out + cross_gate * other_out).reshape(row_tokens, local)
    attn_sum = collect_rows(jnp.dot(mixed, out_full, preferred_element_type=jnp.float32))
    first_norm, first_inv = rms_parts(attn_sum)
    branch_attn = first_norm * gains[1]
    tanh_attn = jnp.tanh(gate_attn)
    middle = source + tanh_attn * branch_attn
    feed_norm, feed_inv = rms_parts(middle)
    feed_all = spread_rows(half(feed_norm * gains[2] * (1.0 + scale_feed)))
    gate_up = jnp.einsum("td,kdf->ktf", feed_all, feed_full, preferred_element_type=jnp.float32)
    sigmoid_gate = jax.nn.sigmoid(gate_up[0])
    silu_gate = gate_up[0] * sigmoid_gate
    hidden = half(jax.nn.silu(gate_up[0]) * gate_up[1])
    feed_sum = collect_rows(jnp.dot(hidden, down_full, preferred_element_type=jnp.float32))
    second_norm, second_inv = rms_parts(feed_sum)
    branch_feed = second_norm * gains[3]
    tanh_feed = jnp.tanh(gate_feed)
    block_out = middle + tanh_feed * branch_feed
    branch_feed_grad = tanh_feed * cotangent
    gate_feed_grad = cotangent * branch_feed * (1.0 - tanh_feed * tanh_feed)
    feed_sum_grad = spread_rows(
        half(rms_back(second_norm, second_inv, branch_feed_grad * gains[3]))
    )
    feed_out_grad = jnp.dot(hidden.T, feed_sum_grad, preferred_element_type=jnp.float32)
    hidden_grad = jnp.dot(feed_sum_grad, down_full.T, preferred_element_type=jnp.float32)
    gate_grad = (
        hidden_grad * gate_up[1] * (sigmoid_gate + gate_up[0] * sigmoid_gate * (1.0 - sigmoid_gate))
    )
    up_grad = hidden_grad * silu_gate
    pair_grad = half(jnp.stack([gate_grad, up_grad]))
    feed_in_grad = jnp.einsum(
        "td,ktf->kdf", feed_all, pair_grad, preferred_element_type=jnp.float32
    )
    feed_input_grad = collect_rows(
        jnp.einsum("ktf,kdf->td", pair_grad, feed_full, preferred_element_type=jnp.float32)
    )
    scale_feed_grad = feed_input_grad * feed_norm * gains[2]
    middle_grad = cotangent + rms_back(
        feed_norm, feed_inv, feed_input_grad * gains[2] * (1.0 + scale_feed)
    )
    branch_attn_grad = tanh_attn * middle_grad
    gate_attn_grad = middle_grad * branch_attn * (1.0 - tanh_attn * tanh_attn)
    attn_sum_grad = spread_rows(half(rms_back(first_norm, first_inv, branch_attn_grad * gains[1])))
    attention_out_grad = jnp.dot(mixed.T, attn_sum_grad, preferred_element_type=jnp.float32)
    mixed_grad = jnp.dot(attn_sum_grad, out_full.T, preferred_element_type=jnp.float32).reshape(
        row_tokens, local_heads, HEAD
    )
    gate_channel_grad = jnp.sum(mixed_grad * other_out * (1.0 - cross_gate * cross_gate), axis=0)
    own_grad = half(mixed_grad)
    other_grad = half(cross_gate * mixed_grad)

    def backward_block(carry, inputs):
        key_acc, value_acc, text_key_acc, text_value_acc = carry
        query, ids, own_sum, other_sum, own_back, other_back = inputs
        query_one, key_one, value_one = attend_back(
            query, keys, values, ids[:, None] == segment[None, :], scale, own_sum, own_back
        )
        cross_mask = (ids[:, None] == slot_image[None, :]) & slot_live[None, :]
        query_two, key_two, value_two = attend_back(
            query, text_keys, text_values, cross_mask, scale, other_sum, other_back
        )
        return (
            (
                key_acc + key_one,
                value_acc + value_one,
                text_key_acc + key_two,
                text_value_acc + value_two,
            ),
            query_one + query_two,
        )

    zeros_rows = jnp.zeros((row_tokens, local_heads, HEAD), jnp.float32)
    zeros_text = jnp.zeros((slots, local_heads, HEAD), jnp.float32)
    (key_rot_grad, value_grad, text_key_grad, text_value_grad), query_rot_grad = lax.scan(
        backward_block,
        (zeros_rows, zeros_rows, zeros_text, zeros_text),
        (
            query_blocks,
            id_blocks,
            own_lse,
            other_lse,
            own_grad.reshape(count, block, local_heads, HEAD),
            other_grad.reshape(count, block, local_heads, HEAD),
        ),
    )
    query_rot_grad = query_rot_grad.reshape(row_tokens, local_heads, HEAD)
    query_turn = rotate(query_rot_grad, cosine, -sine)
    key_turn = rotate(key_rot_grad, cosine, -sine)
    query_gain_grad = jnp.sum(query_turn * query_norm, axis=0)
    key_gain_grad = jnp.sum(key_turn * key_norm, axis=0)
    text_gain_grad = jnp.sum(text_key_grad * text_key_norm, axis=0)
    query_raw_grad = rms_back(query_norm, query_inv, query_turn * local_gains[4]).reshape(
        row_tokens, local
    )
    key_raw_grad = rms_back(key_norm, key_inv, key_turn * local_gains[5]).reshape(row_tokens, local)
    triple_grad = half(
        jnp.stack([query_raw_grad, key_raw_grad, value_grad.reshape(row_tokens, local)])
    )
    attention_in_grad = jnp.einsum(
        "td,kte->kde", attn_full, triple_grad, preferred_element_type=jnp.float32
    )
    text_raw_grad = rms_back(text_key_norm, text_key_inv, text_key_grad * local_gains[6]).reshape(
        slots, local
    )
    text_pair = half(jnp.stack([text_raw_grad, text_value_grad.reshape(slots, local)], axis=1))
    text_full = lax.all_gather(text_pair, "tensor", axis=2, tiled=True)
    caption_in_grad = jnp.einsum(
        "ct,ckd->ktd", captions, text_full, preferred_element_type=jnp.float32
    )
    attn_input_grad = collect_rows(
        jnp.einsum("kte,kde->td", triple_grad, in_full, preferred_element_type=jnp.float32)
    )
    scale_attn_grad = attn_input_grad * attn_norm * gains[0]
    latent_grad = middle_grad + rms_back(
        attn_norm, attn_inv, attn_input_grad * gains[0] * (1.0 + scale_attn)
    )
    shared_rows = jnp.stack(
        [
            jnp.sum(attn_input_grad * attn_norm * (1.0 + scale_attn), axis=0),
            jnp.sum(branch_attn_grad * first_norm, axis=0),
            jnp.sum(feed_input_grad * feed_norm * (1.0 + scale_feed), axis=0),
            jnp.sum(branch_feed_grad * second_norm, axis=0),
        ]
    )
    head_rows = jnp.stack(
        [query_gain_grad, key_gain_grad, text_gain_grad, gate_channel_grad]
    ).reshape(4, local)
    head_full = lax.dynamic_update_slice(
        jnp.zeros((4, width), jnp.float32), head_rows, (jnp.zeros((), jnp.int32), offset)
    )
    channel_total = lax.psum(jnp.concatenate([shared_rows, head_full], axis=0), "tensor")
    in_sum, out_sum, feed_in_sum, feed_out_sum, caption_sum, channel_sum = (
        lax.psum_scatter(attention_in_grad, "dp", scatter_dimension=1, tiled=True),
        lax.psum_scatter(attention_out_grad, "dp", scatter_dimension=1, tiled=True),
        lax.psum_scatter(feed_in_grad, "dp", scatter_dimension=1, tiled=True),
        lax.psum_scatter(feed_out_grad, "dp", scatter_dimension=1, tiled=True),
        lax.psum_scatter(caption_in_grad, "dp", scatter_dimension=2, tiled=True),
        lax.psum_scatter(channel_total, "dp", scatter_dimension=1, tiled=True),
    )
    factor_tokens = jnp.concatenate(
        [scale_attn_grad, gate_attn_grad, scale_feed_grad, gate_feed_grad], axis=1
    )
    factor_image = jnp.dot(chooser.T, factor_tokens, precision=HIGH)
    factor_place = lax.dynamic_update_slice(
        jnp.zeros((images, 4 * width), jnp.float32),
        factor_image,
        (row_index * per_row, jnp.zeros((), jnp.int32)),
    )
    factor_grad = lax.psum_scatter(factor_place, ("dp", "tensor"), scatter_dimension=1, tiled=True)
    modulator_sum = jnp.dot(augmented.astype(jnp.float32).T, factor_grad, precision=HIGH)
    squares = (
        jnp.sum(in_sum * in_sum)
        + jnp.sum(out_sum * out_sum)
        + jnp.sum(feed_in_sum * feed_in_sum)
        + jnp.sum(feed_out_sum * feed_out_sum)
        + jnp.sum(caption_sum * caption_sum)
        + jnp.sum(modulator_sum * modulator_sum)
        + jnp.sum(channel_sum * channel_sum) / tensor_size
    )
    grad_norm = jnp.sqrt(lax.psum(squares, ("dp", "tensor")))
    factor = CLIP / jnp.maximum(grad_norm, CLIP)
    first = adamw(
        in_sum * factor, attention_in, moment_attention_in, square_attention_in, DECAY, RATE
    )
    second = adamw(
        out_sum * factor, attention_out, moment_attention_out, square_attention_out, DECAY, RATE
    )
    third = adamw(feed_in_sum * factor, feed_in, moment_feed_in, square_feed_in, DECAY, RATE)
    fourth = adamw(feed_out_sum * factor, feed_out, moment_feed_out, square_feed_out, DECAY, RATE)
    fifth = adamw(
        caption_sum * factor, caption_in, moment_caption_in, square_caption_in, DECAY, RATE
    )
    sixth = adamw(
        modulator_sum * factor, modulator, moment_modulator, square_modulator, DECAY, RATE
    )
    seventh = adamw(
        channel_sum * factor, channels, moment_channels, square_channels, 0.0, GAIN_RATE
    )
    return (
        block_out,
        latent_grad,
        grad_norm,
        first[0],
        first[1],
        first[2],
        second[0],
        second[1],
        second[2],
        third[0],
        third[1],
        third[2],
        fourth[0],
        fourth[1],
        fourth[2],
        fifth[0],
        fifth[1],
        fifth[2],
        sixth[0],
        sixth[1],
        sixth[2],
        seventh[0],
        seventh[1],
        seventh[2],
    )


def solution(mesh):
    return jax.shard_map(
        body,
        mesh=mesh,
        in_specs=(
            P(("dp", "tensor"), None),
            P(("dp", "tensor"), None),
            P("dp", "tensor"),
            P(),
            P("dp", None),
            P("dp", None),
            P("dp", None),
            P("dp", None),
            P(None, "dp", "tensor"),
            P("tensor", "dp"),
            P(None, "dp", "tensor"),
            P("tensor", "dp"),
            P(None, "tensor", "dp"),
            P(None, ("dp", "tensor")),
            P(None, "dp"),
            P(None, "dp", "tensor"),
            P(None, "dp", "tensor"),
            P("tensor", "dp"),
            P("tensor", "dp"),
            P(None, "dp", "tensor"),
            P(None, "dp", "tensor"),
            P("tensor", "dp"),
            P("tensor", "dp"),
            P(None, "tensor", "dp"),
            P(None, "tensor", "dp"),
            P(None, ("dp", "tensor")),
            P(None, ("dp", "tensor")),
            P(None, "dp"),
            P(None, "dp"),
        ),
        out_specs=(
            P(("dp", "tensor"), None),
            P(("dp", "tensor"), None),
            P(),
            P(None, "dp", "tensor"),
            P(None, "dp", "tensor"),
            P(None, "dp", "tensor"),
            P("tensor", "dp"),
            P("tensor", "dp"),
            P("tensor", "dp"),
            P(None, "dp", "tensor"),
            P(None, "dp", "tensor"),
            P(None, "dp", "tensor"),
            P("tensor", "dp"),
            P("tensor", "dp"),
            P("tensor", "dp"),
            P(None, "tensor", "dp"),
            P(None, "tensor", "dp"),
            P(None, "tensor", "dp"),
            P(None, ("dp", "tensor")),
            P(None, ("dp", "tensor")),
            P(None, ("dp", "tensor")),
            P(None, "dp"),
            P(None, "dp"),
            P(None, "dp"),
        ),
        check_vma=False,
    )
```

profile of v0, /device:TPU:0, one launch (start us, length us, event | category | flops | bytes accessed | tf_op | source)
XLA Modules:
  0.0 2740.7 jit_solution(1303907720684474410)
XLA Ops:
  14.6 32.5 %all-gather.1 = bf16[8,192,8]{1,2,0:T(8,128)(2,1)S(1)} all-gather(bf16[1,192,8]{1,2,0:T(8,128)(2,1)S(1)} %convert_bitcast_fusion), channel_id=1, replica_groups=mesh['dp'=8,'tensor'=4] {'dp'}, dimensions={0}, use_global_device_ids=true | all-gather | bytes 27648 | tf_op jit(solution)/shard_map/all_gather | solution.py:158
  83.0 88.3 %all-gather.18.cloned.1.call-done = bf16[2,1024,1536]{1,2,0:T(8,128)(2,1)} async-done(((bf16[2,1024,192]{1,2,0:T(8,128)(2,1)}), bf16[2,1024,1536]{1,2,0:T(8,128)(2,1)}) %all-gather.18.cloned.1.call-update) | async-done | bytes 6291472 | tf_op jit(solution)/shard_map/all_gather | solution.py:157
  197.1 40.3 %all-gather.16.cloned.1.call-done = bf16[3,1536,384]{2,1,0:T(8,128)(2,1)} async-done(((bf16[3,192,384]{2,1,0:T(8,128)(2,1)}), bf16[3,1536,384]{2,1,0:T(8,128)(2,1)}) %all-gather.16.cloned.1.call-update) | async-done | bytes 3538960 | tf_op jit(solution)/shard_map/all_gather | solution.py:153
  237.4 29.0 %all-gather.14.cloned.1.call-done = bf16[1024,1536]{1,0:T(8,128)(2,1)} async-done(((bf16[256,1536]{1,0:T(8,128)(2,1)}), bf16[1024,1536]{1,0:T(8,128)(2,1)}) %all-gather.14.cloned.1.call-update) | async-done | bytes 3145744 | tf_op jit(solution)/shard_map/all_gather | solution.py:60
  281.1 168.3 %reduce-scatter.18.cloned.1.call-done = f32[2048,2,384]{2,0,1:T(8,128)} async-done(((f32[2048,2,1536]{2,0,1:T(8,128)}), f32[2048,2,384]{2,0,1:T(8,128)}) %reduce-scatter.18.cloned.1.call-update) | async-done | bytes 6291472 | tf_op jit(solution)/shard_map/reduce_scatter | solution.py:179
  467.0 160.1 %while.36 = (s32[]{:T(128)}, f32[2,512,6,64]{1,0,3,2:T(2,128)}, f32[2,512,6,64]{1,0,3,2:T(2,128)}, f32[2,6,512]{2,1,0:T(8,128)S(1)}, f32[2,6,512]{2,1,0:T(8,128)...) while((s32[]{:T(128)}, f32[2,512,6,64]{1,0,3,2:T(2,128)}, ...), condition=%wide.region_11.12_spmd.clone, body=%wide.region_6.11_spmd.clone.sunk | while | flops 2531796992 | bytes 142596336 | solution.py:216
  639.3 56.1 %reduce-scatter.20.cloned.1.call-done = f32[256,1536]{1,0:T(8,128)} async-done(((f32[1024,1536]{1,0:T(8,128)}), f32[256,1536]{1,0:T(8,128)}) %reduce-scatter.20.cloned.1.call-update) | async-done | bytes 1572880 | tf_op jit(solution)/shard_map/reduce_scatter | solution.py:64
  704.1 93.1 %all-gather.24.cloned.1.call-done = bf16[2,1536,1024]{2,1,0:T(8,128)(2,1)} async-done(((bf16[2,192,1024]{2,1,0:T(8,128)(2,1)}), bf16[2,1536,1024]{2,1,0:T(8,128)(2,1)}) %all-gather.24.cloned.1.call-update) | async-done | bytes 6291472 | tf_op jit(solution)/shard_map/all_gather | solution.py:155
  797.3 28.9 %all-gather.22.cloned.1.call-done = bf16[1024,1536]{1,0:T(8,128)(2,1)} async-done(((bf16[256,1536]{1,0:T(8,128)(2,1)}), bf16[1024,1536]{1,0:T(8,128)(2,1)}) %all-gather.22.cloned.1.call-update) | async-done | bytes 3145744 | tf_op jit(solution)/shard_map/all_gather | solution.py:60
  841.9 47.3 %all-gather.26.cloned.1.call-done = bf16[1024,1536]{0,1:T(8,128)(2,1)} async-done(((bf16[1024,192]{0,1:T(8,128)(2,1)}), bf16[1024,1536]{0,1:T(8,128)(2,1)}) %all-gather.26.cloned.1.call-update) | async-done | bytes 3145744 | tf_op jit(solution)/shard_map/all_gather | solution.py:156
  897.9 57.1 %reduce-scatter.22.cloned.1.call-done = f32[256,1536]{1,0:T(8,128)} async-done(((f32[1024,1536]{1,0:T(8,128)}), f32[256,1536]{1,0:T(8,128)}) %reduce-scatter.22.cloned.1.call-update) | async-done | bytes 1572880 | tf_op jit(solution)/shard_map/reduce_scatter | solution.py:64
  964.7 28.4 %all-gather.28.cloned.1.call-done = bf16[1024,1536]{1,0:T(8,128)(2,1)} async-done(((bf16[256,1536]{1,0:T(8,128)(2,1)}), bf16[1024,1536]{1,0:T(8,128)(2,1)}) %all-gather.28.cloned.1.call-update) | async-done | bytes 3145744 | tf_op jit(solution)/shard_map/all_gather | solution.py:60
  1015.5 58.5 %reduce-scatter.24.cloned.1.call-done = f32[256,1536]{1,0:T(8,128)} async-done(((f32[1024,1536]{1,0:T(8,128)}), f32[256,1536]{1,0:T(8,128)}) %reduce-scatter.24.cloned.1.call-update) | async-done | bytes 1572880 | tf_op jit(solution)/shard_map/reduce_scatter | solution.py:64
  1090.2 25.1 all-gather.30.cloned.1.call-done
  1134.4 262.9 %while.37 = (s32[]{:T(128)}, f32[1024,6,64]{0,2,1:T(8,128)}, f32[1024,6,64]{0,2,1:T(8,128)}, f32[2048,6,64]{0,2,1:T(8,128)}, f32[2048,6,64]{0,2,1:T(8,128)}, /*i...) while((s32[]{:T(128)}, f32[1024,6,64]{0,2,1:T(8,128)}, ...), condition=%wide.region_24.25_spmd.clone, body=%wide.region_21.24_spmd.clone.sunk | while | flops 6190278656 | bytes 412305984 | solution.py:294
  1513.3 43.6 %all-gather.32.cloned.1.call-done = bf16[2048,2,1536]{0,2,1:T(8,128)(2,1)} async-done(((bf16[2048,2,384]{0,2,1:T(8,128)(2,1)}), bf16[2048,2,1536]{0,2,1:T(8,128)(2,1)}) %all-gather.32.cloned.1.call-update) | async-done | bytes 12582928 | tf_op jit(solution)/shard_map/all_gather | solution.py:326
  1578.0 100.7 %reduce-scatter.30.cloned.1.call-done = f32[1024,192]{0,1:T(8,128)} async-done(((f32[1024,1536]{0,1:T(8,128)}), f32[1024,192]{0,1:T(8,128)}) %reduce-scatter.30.cloned.1.call-update) | async-done | bytes 786448 | tf_op jit(solution)/shard_map/reduce_scatter | solution.py:356
  1680.7 399.4 %all-reduce.4.cloned.1.call-done = f32[2,1536,1024]{2,0,1:T(2,128)} async-done(((f32[2,1536,1024]{2,0,1:T(2,128)}), f32[2,1536,1024]{2,0,1:T(2,128)}) %all-reduce.4.cloned.1.call-update) | async-done | bytes 12582928
  2084.7 66.8 %reduce-scatter.28.cloned.1.call-done = f32[384,192]{0,1:T(8,128)} async-done(((f32[384,1536]{0,1:T(8,128)}), f32[384,192]{0,1:T(8,128)}) %reduce-scatter.28.cloned.1.call-update) | async-done | bytes 294928 | tf_op jit(solution)/shard_map/reduce_scatter | solution.py:354
  2153.8 63.1 %reduce-scatter.38.cloned.1.call-done = f32[192,8]{1,0:T(8,128)} async-done(((f32[1536,8]{1,0:T(8,128)}), f32[192,8]{1,0:T(8,128)}) %reduce-scatter.38.cloned.1.call-update) | async-done | bytes 6160
  2224.9 124.1 %reduce-scatter.34.cloned.1.call-done = f32[192,1152]{1,0:T(8,128)} async-done(((f32[1536,1152]{1,0:T(8,128)}), f32[192,1152]{1,0:T(8,128)}) %reduce-scatter.34.cloned.1.call-update) | async-done | bytes 884752
  2354.8 100.2 %reduce-scatter.36.cloned.1.call-done = f32[192,64]{1,0:T(8,128)} async-done(((f32[6144,64]{1,0:T(8,128)}), f32[192,64]{1,0:T(8,128)}) %reduce-scatter.36.cloned.1.call-update) | async-done | bytes 49168
  2458.0 207.0 %reduce-scatter.32.cloned.1.call-done = f32[2,1024,192]{1,2,0:T(8,128)} async-done(((f32[2,1024,1536]{1,2,0:T(8,128)}), f32[2,1024,192]{1,2,0:T(8,128)}) %reduce-scatter.32.cloned.1.call-update) | async-done | bytes 1572880 | tf_op jit(solution)/shard_map/reduce_scatter | solution.py:357
  2672.2 39.6 %psum.15 = f32[]{:T(128)} all-reduce(f32[]{:T(128)S(6)} %add.370), channel_id=1, replica_groups=mesh['dp'=8,'tensor'=4] {'dp','tensor'}, use_global_device_ids=true, to_apply=%region_53.54 | all-reduce | flops 1 | bytes 8 | tf_op jit(solution)/shard_map/psum | solution.py:380
  (543 shorter events, 811.6 us)
Async XLA Ops:
  7.2 63.4 %all-gather.34.cloned.1.call-start = ((), (), s32[]{:S(2)}) async-start(), calls=%async_computation.29 | async-start | bytes 2162688 | tf_op jit(solution)/shard_map/all_gather | solution.py:166
  11.1 160.2 %all-gather.18.cloned.1.call-start = ((), (), s32[]{:S(2)}) async-start(), calls=%async_computation.13 | async-start | bytes 7077888 | tf_op jit(solution)/shard_map/all_gather | solution.py:157
  13.6 223.8 %all-gather.16.cloned.1.call-start = ((), (), s32[]{:S(2)}) async-start(), calls=%async_computation.12 | async-start | bytes 3981312 | tf_op jit(solution)/shard_map/all_gather | solution.py:153
  14.5 251.9 %all-gather.14.cloned.1.call-start = ((), (), s32[]{:S(2)}) async-start(), calls=%async_computation.11 | async-start | bytes 3932160 | tf_op jit(solution)/shard_map/all_gather | solution.py:60
  82.9 366.4 %reduce-scatter.18.cloned.1.call-start = ((), (), s32[]{:S(2)}) async-start(), calls=%async_computation.14 | async-start | bytes 31457280 | tf_op jit(solution)/shard_map/reduce_scatter | solution.py:179
  191.3 439.4 %all-gather.20.cloned.1.call-start = ((), (), s32[]{:S(2)}) async-start(), calls=%async_computation.15 | async-start | bytes 1327104 | tf_op jit(solution)/shard_map/all_gather | solution.py:154
  193.0 502.5 %reduce-scatter.20.cloned.1.call-start = ((), (), s32[]{:S(2)}) async-start(), calls=%async_computation.16 | async-start | bytes 7864320 | tf_op jit(solution)/shard_map/reduce_scatter | solution.py:64
  636.8 160.5 %all-gather.24.cloned.1.call-start = ((), (), s32[]{:S(2)}) async-start(), calls=%async_computation.18 | async-start | bytes 7077888 | tf_op jit(solution)/shard_map/all_gather | solution.py:155
  639.3 186.9 %all-gather.22.cloned.1.call-start = ((), (), s32[]{:S(2)}) async-start(), calls=%async_computation.17 | async-start | bytes 3932160 | tf_op jit(solution)/shard_map/all_gather | solution.py:60
  703.2 186.0 %all-gather.26.cloned.1.call-start = ((), (), s32[]{:S(2)}) async-start(), calls=%async_computation.19 | async-start | bytes 3538944 | tf_op jit(solution)/shard_map/all_gather | solution.py:156
  704.1 250.9 %reduce-scatter.22.cloned.1.call-start = ((), (), s32[]{:S(2)}) async-start(), calls=%async_computation.20 | async-start | bytes 7864320 | tf_op jit(solution)/shard_map/reduce_scatter | solution.py:64
  897.9 95.3 %all-gather.28.cloned.1.call-start = ((), (), s32[]{:S(2)}) async-start(), calls=%async_computation.21 | async-start | bytes 3932160 | tf_op jit(solution)/shard_map/all_gather | solution.py:60
  964.5 109.5 %reduce-scatter.24.cloned.1.call-start = ((), (), s32[]{:S(2)}) async-start(), calls=%async_computation.22 | async-start | bytes 7864320 | tf_op jit(solution)/shard_map/reduce_scatter | solution.py:64
  1015.5 99.8 %all-gather.30.cloned.1.call-start = ((), (), s32[]{:S(2)}) async-start(), calls=%async_computation.23 | async-start | bytes 3932160 | tf_op jit(solution)/shard_map/all_gather | solution.py:60
  1086.6 386.8 %reduce-scatter.26.cloned.1.call-start = ((), (), s32[]{:S(2)}) async-start(), calls=%async_computation.24 | async-start | bytes 7864320 | tf_op jit(solution)/shard_map/reduce_scatter | solution.py:64
  1414.7 142.1 %all-gather.32.cloned.1.call-start = ((), (), s32[]{:S(2)}) async-start(), calls=%async_computation.27 | async-start | bytes 15728640 | tf_op jit(solution)/shard_map/all_gather | solution.py:326
  1422.4 256.3 %reduce-scatter.30.cloned.1.call-start = ((), (), s32[]{:S(2)}) async-start(), calls=%async_computation.26 | async-start | bytes 7077888 | tf_op jit(solution)/shard_map/reduce_scatter | solution.py:356
  1432.3 647.7 %all-reduce.4.cloned.1.call-start = ((), (), s32[]{:S(2)}) async-start(), calls=%async_computation.33 | async-start | bytes 25165824
  1466.2 685.4 %reduce-scatter.28.cloned.1.call-start = ((), (), s32[]{:S(2)}) async-start(), calls=%async_computation.25 | async-start | bytes 2654208 | tf_op jit(solution)/shard_map/reduce_scatter | solution.py:354
  1472.5 744.4 %reduce-scatter.38.cloned.1.call-start = ((), (), s32[]{:S(2)}) async-start(), calls=%async_computation.32 | async-start | bytes 884736
  1478.8 870.2 %reduce-scatter.34.cloned.1.call-start = ((), (), s32[]{:S(2)}) async-start(), calls=%async_computation.30 | async-start | bytes 7962624
  1505.4 949.6 %reduce-scatter.36.cloned.1.call-start = ((), (), s32[]{:S(2)}) async-start(), calls=%async_computation.31 | async-start | bytes 3244032
  1513.2 1151.7 %reduce-scatter.32.cloned.1.call-start = ((), (), s32[]{:S(2)}) async-start(), calls=%async_computation.28 | async-start | bytes 14155776 | tf_op jit(solution)/shard_map/reduce_scatter | solution.py:357
  2352.1 316.6 %copy-start.20 = (f32[256,1536]{1,0:T(8,128)S(1)}, f32[256,1536]{1,0:T(8,128)}, u32[]{:S(2)}) copy-start(f32[256,1536]{1,0:T(8,128)} %copy-done.19) | copy-start | bytes 4718596
  (132 other events, 1454.1 us)
Sparse Core Ops, SparseCore 0:
  11.5 59.0 all-gather.33
  73.3 97.8 all-gather.17
  174.0 63.3 all-gather.15
  239.4 26.9 all-gather.13
  268.9 180.4 reduce-scatter.17
  452.2 41.0 all-gather.19
  636.9 58.4 reduce-scatter.19
  698.2 99.0 all-gather.23
  799.4 26.6 all-gather.21
  828.8 60.4 all-gather.25
  898.0 56.9 reduce-scatter.21
  964.6 28.5 all-gather.27
  1015.6 58.3 reduce-scatter.23
  1086.7 28.5 all-gather.29
  1414.8 58.3 reduce-scatter.25
  1474.7 82.0 all-gather.31
  1560.7 117.9 reduce-scatter.29
  1683.2 396.7 all-reduce.3
  2083.5 67.9 reduce-scatter.27
  2155.3 61.5 reduce-scatter.37
  2221.0 127.9 reduce-scatter.33
  2354.4 100.5 reduce-scatter.35
  2458.6 206.2 reduce-scatter.31
where the time goes:
time: 2760 us; the launch traced here: 2740 us
  waiting for transfers between devices  1850 us (67%)
  matrix products  375 us (14%)
  local copies, waits for them, and re-layouts  217 us (8%)
  other arithmetic  189 us (7%)
  blocking collectives  77.8 us (3%)
    unnamed x27, waiting for transfers between devices  687 us
    reduce_scatter x1, waiting for transfers between devices, body(): lax.psum_scatter(caption_in_grad, 'dp', scatter_dimension=2, tiled=True)  207 us
    reduce_scatter x4, waiting for transfers between devices, collect_rows(): return lax.psum_scatter(value, 'tensor', scatter_dimension=0, tiled=True)  172 us
    reduce_scatter x1, waiting for transfers between devices, body(): lax.psum_scatter(caption_part, 'tensor', scatter_dimension=2, tiled=True)  168 us
    all_gather x4, waiting for transfers between devices, spread_rows(): return lax.all_gather(value, 'tensor', axis=0, tiled=True)  111 us
    reduce_scatter x1, waiting for transfers between devices, body(): lax.psum_scatter(feed_out_grad, 'dp', scatter_dimension=1, tiled=True)  101 us
    dynamic_update_slice x12, local copies, waits for them, and re-layouts, body(): lax.scan(forward_block, jnp.zeros((), jnp.float32), (query_blocks, id_blo...  96.6 us
    all_gather x1, waiting for transfers between devices, body(): lax.all_gather(half(feed_in), 'dp', axis=1, tiled=True)  93.1 us
  transfers between devices with their start and end apart: 23, of which 21 were waited for; matrix products, arithmetic and copies ran while one was open for 14% of the time, Pallas kernels for 0%

commit v1 on v0

v1 whole, which is shorter than its diff:
```python
import functools
import math

import jax
import jax.numpy as jnp
from jax import lax
from jax.experimental import pallas as pl
from jax.experimental.pallas import tpu as pltpu
from jax.sharding import PartitionSpec as P

HEAD = 64
CAP = 256
STEP = 10


EPS = 1e-06
NEG = -1e30
THETA = 10000.0
BETA1 = 0.9
BETA2 = 0.95
RATE = 0.05
GAIN_RATE = 0.8
DECAY = 0.1
ADAM_EPS = 1e-08
CLIP = 1.0
HIGH = lax.Precision.HIGHEST


def half(value):
    return value.astype(jnp.bfloat16)


TILE = 256
LOG2E = 1.0 / math.log(2.0)


def dot(left, right, left_dim, right_dim):
    return lax.dot_general(
        left, right, (((left_dim,), (right_dim,)), ((), ())), preferred_element_type=jnp.float32
    )


def rms_parts(value, axis=-1):
    inverse = lax.rsqrt(jnp.mean(value * value, axis=axis, keepdims=True) + EPS)
    return (value * inverse, inverse)


def rms_back(normed, inverse, grad, axis=-1):
    return inverse * (grad - normed * jnp.mean(grad * normed, axis=axis, keepdims=True))


def rope_tables(rows, columns):
    quarter = HEAD // 4
    frequency = THETA ** (-jnp.arange(quarter, dtype=jnp.float32) / quarter)
    angles = jnp.concatenate(
        [
            frequency[:, None] * rows.astype(jnp.float32)[None, :],
            frequency[:, None] * columns.astype(jnp.float32)[None, :],
        ],
        axis=0,
    )
    return (jnp.cos(angles)[None], jnp.sin(angles)[None])


def rotate(value, cosine, sine):
    middle = value.shape[1] // 2
    first = value[:, :middle]
    second = value[:, middle:]
    return jnp.concatenate(
        [first * cosine - second * sine, second * cosine + first * sine], axis=1
    )


def near_swap(value):
    return lax.ppermute(value, "dp", [(i, i ^ 1) for i in range(lax.axis_size("dp"))])


def far_groups():
    count = lax.axis_size("dp")
    return [list(range(near, count, 2)) for near in range(2)]


def gather_dp(value, near_first=False):
    odd = lax.axis_index("dp") % 2
    groups = far_groups()
    if near_first:
        other = near_swap(value)
        pair = jnp.concatenate(
            [jnp.where(odd == 0, value, other), jnp.where(odd == 0, other, value)], axis=0
        )
        return lax.all_gather(pair, "dp", axis=0, tiled=True, axis_index_groups=groups)
    line = lax.all_gather(value, "dp", axis=0, tiled=True, axis_index_groups=groups)
    other = near_swap(line)
    rows, columns = value.shape
    line = line.reshape(-1, rows, columns)
    other = other.reshape(-1, rows, columns)
    both = jnp.stack(
        [jnp.where(odd == 0, line, other), jnp.where(odd == 0, other, line)], axis=1
    )
    return both.reshape(-1, columns)


def scatter_dp(value):
    count = lax.axis_size("dp")
    odd = lax.axis_index("dp") % 2
    rows, columns = value.shape[0] // count, value.shape[1]
    parts = value.reshape(count // 2, 2, rows, columns)
    keep = lax.dynamic_index_in_dim(parts, odd, 1, keepdims=False)
    send = lax.dynamic_index_in_dim(parts, 1 - odd, 1, keepdims=False)
    got = near_swap(send.reshape(-1, columns)).reshape(-1, rows, columns)
    summed = half(keep.astype(jnp.float32) + got.astype(jnp.float32)).reshape(-1, columns)
    return lax.psum_scatter(
        summed, "dp", scatter_dimension=0, tiled=True, axis_index_groups=far_groups()
    )


def swap_tensor(value, bits):
    return lax.ppermute(value, "tensor", [(i, i ^ bits) for i in range(lax.axis_size("tensor"))])


def owner(place):
    if lax.axis_size("tensor") == 4:
        return lax.axis_index("tensor") ^ place
    return jnp.int32(place)


def spread(value):
    count = lax.axis_size("tensor")
    if count == 4:
        near = swap_tensor(value, 1)
        far = swap_tensor(value, 2)
        return [value, near, far, swap_tensor(far, 1)]
    whole = lax.all_gather(value, "tensor", axis=0, tiled=False)
    return [whole[i] for i in range(count)]


def collect(parts):
    if len(parts) == 4:
        rows = parts[0].shape[0]
        sent = swap_tensor(half(jnp.concatenate([parts[3], parts[1]], axis=0)), 1)
        sent = sent.astype(jnp.float32)
        far = swap_tensor(half(parts[2] + sent[:rows]), 2)
        return parts[0] + sent[rows:] + far.astype(jnp.float32)
    return lax.psum_scatter(
        half(jnp.concatenate(parts, axis=0)), "tensor", scatter_dimension=0, tiled=True
    ).astype(jnp.float32)


def in_place(blocks):
    if len(blocks) == 4:
        stacked = jnp.stack(blocks)
        mine = lax.axis_index("tensor")
        blocks = [
            lax.dynamic_index_in_dim(stacked, mine ^ i, 0, keepdims=False)
            for i in range(len(blocks))
        ]
    return jnp.concatenate(blocks, axis=0)


def attention_bias(cross, step, ids_row, ids_column, lengths):
    if cross:
        slots = lax.broadcasted_iota(jnp.int32, (TILE, 1), 0) < lengths[step]
        return jnp.where(slots & (ids_row[...] == step), 0.0, NEG)
    start = pl.multiple_of(step * TILE, TILE)
    return jnp.where(ids_column[pl.ds(start, TILE), :] == ids_row[...], 0.0, NEG)


def attention_kernel(
    heads, cross, meta, lengths, ids_row, ids_column, q_ref, k_ref, v_ref, out_ref, inv_ref, total
):
    place = pl.program_id(0)
    base = 2 * place
    factor = HEAD ** (-0.5) * LOG2E
    out_ref[...] = jnp.zeros_like(out_ref)
    total[...] = jnp.zeros_like(total)

    def step(index, carry):
        bias = attention_bias(cross, index, ids_row, ids_column, lengths)
        rows = pl.ds(pl.multiple_of(index * TILE, TILE), TILE)
        for head in range(heads):
            span = slice(head * HEAD, (head + 1) * HEAD)
            scores = dot(k_ref[head, rows, :], q_ref[span, :], 1, 0)
            expo = jnp.exp2(scores * factor + bias)
            total[head] += jnp.sum(expo.reshape(TILE // 8, 8, TILE), axis=0)
            out_ref[span, :] += dot(v_ref[span, rows], half(expo), 1, 0)
        return carry

    lax.fori_loop(meta[base], meta[base + 1], step, 0)
    for head in range(heads):
        span = slice(head * HEAD, (head + 1) * HEAD)
        inverse = 1.0 / jnp.sum(total[head], axis=0, keepdims=True)
        inv_ref[head] = jnp.broadcast_to(inverse, (8, TILE))
        out_ref[span, :] = out_ref[span, :] * inverse


def attention_back_kernel(
    heads,
    cross,
    meta,
    lengths,
    ids_row,
    ids_column,
    q_ref,
    k_ref,
    kt_ref,
    v_ref,
    inv_ref,
    o_ref,
    do_ref,
    dq_ref,
    dk_ref,
    dv_ref,
    centre,
):
    place = pl.program_id(0)
    base = 2 * place
    scale = HEAD ** (-0.5)
    factor = scale * LOG2E

    @pl.when(place == 0)
    def _():
        dk_ref[...] = jnp.zeros_like(dk_ref)
        dv_ref[...] = jnp.zeros_like(dv_ref)

    dq_ref[...] = jnp.zeros_like(dq_ref)
    for head in range(heads):
        span = slice(head * HEAD, (head + 1) * HEAD)
        both = o_ref[span, :] * do_ref[span, :].astype(jnp.float32)
        centre[head] = jnp.broadcast_to(jnp.sum(both, axis=0, keepdims=True), (8, TILE))

    def step(index, carry):
        bias = attention_bias(cross, index, ids_row, ids_column, lengths)
        rows = pl.ds(pl.multiple_of(index * TILE, TILE), TILE)
        for head in range(heads):
            span = slice(head * HEAD, (head + 1) * HEAD)
            query = q_ref[span, :]
            back = do_ref[span, :]
            scores = dot(k_ref[head, rows, :], query, 1, 0)
            probs = jnp.exp2(scores * factor + bias) * inv_ref[head, 0:1, :]
            prob_grad = dot(v_ref[head, rows, :], back, 1, 0)
            score_grad = half(probs * (prob_grad - centre[head, 0:1, :]))
            dv_ref[span, rows] += dot(back, half(probs), 1, 1)
            dk_ref[span, rows] += dot(query, score_grad, 1, 1) * scale
            dq_ref[span, :] += dot(kt_ref[span, rows], score_grad, 1, 0) * scale
        return carry

    lax.fori_loop(meta[base], meta[base + 1], step, 0)


def whole_block(array):
    return pl.BlockSpec(array.shape, lambda i, *_: (0,) * array.ndim)


def tile_block(array):
    lead = array.shape[:-1]
    return pl.BlockSpec((*lead, TILE), lambda i, *_: (*([0] * len(lead)), i))


def attention(cross, meta, lengths, ids_row, ids_column, query, key_rows, value):
    local, tokens = query.shape
    heads = local // HEAD
    outs = (
        jax.ShapeDtypeStruct((local, tokens), jnp.float32),
        jax.ShapeDtypeStruct((heads, 8, tokens), jnp.float32),
    )
    return pl.pallas_call(
        functools.partial(attention_kernel, heads, cross),
        grid_spec=pltpu.PrefetchScalarGridSpec(
            num_scalar_prefetch=2,
            grid=(tokens // TILE,),
            in_specs=[
                tile_block(ids_row),
                whole_block(ids_column),
                tile_block(query),
                whole_block(key_rows),
                whole_block(value),
            ],
            out_specs=[tile_block(out) for out in outs],
            scratch_shapes=[pltpu.VMEM((heads, 8, TILE), jnp.float32)],
        ),
        out_shape=outs,
        compiler_params=pltpu.CompilerParams(
            vmem_limit_bytes=48 * 1024 * 1024, dimension_semantics=("arbitrary",)
        ),
        cost_estimate=pl.CostEstimate(
            flops=4 * tokens * 512 * local,
            bytes_accessed=16 * tokens * local,
            transcendentals=tokens * 512 * heads,
        ),
        name="cross_forward" if cross else "self_forward",
    )(meta, lengths, ids_row, ids_column, query, key_rows, value)


def attention_back(
    cross, meta, lengths, ids_row, ids_column, query, key_rows, key, value_rows, inverse, out, grad
):
    local, tokens = query.shape
    heads = local // HEAD
    outs = (
        jax.ShapeDtypeStruct((local, tokens), jnp.float32),
        jax.ShapeDtypeStruct(key.shape, jnp.float32),
        jax.ShapeDtypeStruct(key.shape, jnp.float32),
    )
    return pl.pallas_call(
        functools.partial(attention_back_kernel, heads, cross),
        grid_spec=pltpu.PrefetchScalarGridSpec(
            num_scalar_prefetch=2,
            grid=(tokens // TILE,),
            in_specs=[
                tile_block(ids_row),
                whole_block(ids_column),
                tile_block(query),
                whole_block(key_rows),
                whole_block(key),
                whole_block(value_rows),
                tile_block(inverse),
                tile_block(out),
                tile_block(grad),
            ],
            out_specs=[tile_block(outs[0]), whole_block(outs[1]), whole_block(outs[2])],
            scratch_shapes=[pltpu.VMEM((heads, 8, TILE), jnp.float32)],
        ),
        out_shape=outs,
        compiler_params=pltpu.CompilerParams(
            vmem_limit_bytes=56 * 1024 * 1024, dimension_semantics=("arbitrary",)
        ),
        cost_estimate=pl.CostEstimate(
            flops=10 * tokens * 512 * local,
            bytes_accessed=30 * tokens * local,
            transcendentals=tokens * 512 * heads,
        ),
        name="cross_backward" if cross else "self_backward",
    )(
        meta,
        lengths,
        ids_row,
        ids_column,
        query,
        key_rows,
        key,
        value_rows,
        inverse,
        out,
        grad,
    )


def rows_of(value):
    return jnp.transpose(value.reshape(-1, HEAD, value.shape[1]), (0, 2, 1))


def adamw(grad, weight, moment, square, decay, rate):
    moment_new = BETA1 * moment + (1.0 - BETA1) * grad
    square_new = BETA2 * square + (1.0 - BETA2) * grad * grad
    step_size = (
        moment_new / (1.0 - BETA1**STEP) / (jnp.sqrt(square_new / (1.0 - BETA2**STEP)) + ADAM_EPS)
    )
    return (moment_new, square_new, weight - rate * (step_size + decay * weight))


def body(
    latents,
    cotangent,
    captions,
    conditions,
    image_ids,
    rope_rows,
    rope_cols,
    caption_lengths,
    attention_in,
    attention_out,
    feed_in,
    feed_out,
    caption_in,
    modulator,
    channels,
    moment_attention_in,
    square_attention_in,
    moment_attention_out,
    square_attention_out,
    moment_feed_in,
    square_feed_in,
    moment_feed_out,
    square_feed_out,
    moment_caption_in,
    square_caption_in,
    moment_modulator,
    square_modulator,
    moment_channels,
    square_channels,
):
    tensor_size = lax.axis_size("tensor")
    tensor_index = lax.axis_index("tensor")
    dp_size = lax.axis_size("dp")
    dp_index = lax.axis_index("dp")
    shard_rows, width = latents.shape
    local = attention_in.shape[2]
    heads = local // HEAD
    units = feed_in.shape[2]
    segment = image_ids[0]
    row_tokens = segment.shape[0]
    images = conditions.shape[0]
    per_row = caption_lengths.shape[1]
    lengths = caption_lengths[0]
    slots = captions.shape[0]
    offset = tensor_index * local
    own_ids = lax.dynamic_slice_in_dim(segment, tensor_index * shard_rows, shard_rows)

    caption_half = half(caption_in)
    key_full = gather_dp(caption_half[0].T)
    value_full = gather_dp(caption_half[1].T)
    in_half = half(attention_in)
    in_full = gather_dp(jnp.concatenate([in_half[0], in_half[1], in_half[2]], axis=1))
    out_full = gather_dp(half(attention_out).T)
    feed_half = half(feed_in)
    feed_full = gather_dp(jnp.concatenate([feed_half[0], feed_half[1]], axis=1))
    down_full = gather_dp(half(feed_out).T, near_first=True)

    channel_half = lax.all_gather(half(channels), "dp", axis=1, tiled=True)
    gains = channel_half.astype(jnp.float32)
    local_gains = lax.dynamic_slice_in_dim(gains, offset, local, 1).reshape(8, heads, HEAD, 1)
    augmented = half(
        jnp.concatenate([jax.nn.silu(conditions), jnp.ones((images, 1), jnp.float32)], axis=1)
    )
    factor_part = jnp.dot(augmented, half(modulator), preferred_element_type=jnp.float32)
    own_columns = factor_part.shape[1]
    factor_moved = lax.all_to_all(
        factor_part.reshape(dp_size, per_row, own_columns), "dp", 0, 0, tiled=True
    )
    factor_row = lax.all_gather(factor_moved, "tensor", axis=0, tiled=False)
    factor_row = jnp.transpose(factor_row, (2, 1, 0, 3)).reshape(per_row, -1)
    chooser = (own_ids[:, None] == jnp.arange(per_row, dtype=jnp.int32)[None, :]).astype(
        jnp.float32
    )
    token_factor = jnp.dot(chooser, factor_row, precision=HIGH)
    scale_attn = token_factor[:, :width]
    gate_attn = token_factor[:, width : 2 * width]
    scale_feed = token_factor[:, 2 * width : 3 * width]
    gate_feed = token_factor[:, 3 * width :]

    def caption_project(weight):
        return collect(
            [
                dot(
                    lax.dynamic_slice_in_dim(weight, owner(i) * local, local), captions, 1, 1
                )
                for i in range(tensor_size)
            ]
        )

    text_key_norm, text_key_inv = rms_parts(
        caption_project(key_full).reshape(heads, HEAD, slots), 1
    )
    text_keys = half(text_key_norm * local_gains[6]).reshape(local, slots)
    text_values = half(caption_project(value_full))
    text_key_rows, text_value_rows = rows_of(text_keys), rows_of(text_values)

    source = latents.astype(jnp.float32)
    attn_norm, attn_inv = rms_parts(source)
    attn_full = in_place(spread(half(attn_norm * gains[0] * (1.0 + scale_attn))))
    projected = dot(in_full, attn_full, 0, 1)
    query_norm, query_inv = rms_parts(projected[:local].reshape(heads, HEAD, row_tokens), 1)
    key_norm, key_inv = rms_parts(
        projected[local : 2 * local].reshape(heads, HEAD, row_tokens), 1
    )
    cosine, sine = rope_tables(rope_rows[0], rope_cols[0])
    queries = half(rotate(query_norm * local_gains[4], cosine, sine)).reshape(local, row_tokens)
    keys = half(rotate(key_norm * local_gains[5], cosine, sine)).reshape(local, row_tokens)
    values = half(projected[2 * local :])
    key_rows, value_rows = rows_of(keys), rows_of(values)

    tiles = row_tokens // TILE
    first_id = segment.reshape(tiles, TILE)[:, 0]
    last_id = segment.reshape(tiles, TILE)[:, TILE - 1]
    low = jnp.sum((segment[None] < first_id[:, None]).astype(jnp.int32), axis=1) // TILE
    high = (
        jnp.sum((segment[None] <= last_id[:, None]).astype(jnp.int32), axis=1) + TILE - 1
    ) // TILE
    self_meta = jnp.stack([low, high], axis=1).reshape(-1)
    cross_meta = jnp.stack([first_id, last_id + 1], axis=1).reshape(-1)
    ids_row = image_ids
    ids_column = segment[:, None]
    own_out, own_inv = attention(
        False, self_meta, lengths, ids_row, ids_column, queries, key_rows, values
    )
    other_out, other_inv = attention(
        True, cross_meta, lengths, ids_row, ids_column, queries, text_key_rows, text_values
    )
    cross_gate = jnp.tanh(local_gains[7]).reshape(local, 1)
    mixed = half(own_out + cross_gate * other_out)
    attn_sum = collect(
        [
            dot(
                lax.dynamic_slice_in_dim(mixed, owner(i) * shard_rows, shard_rows, 1),
                out_full,
                0,
                1,
            )
            for i in range(tensor_size)
        ]
    )
    first_norm, first_inv = rms_parts(attn_sum)
    branch_attn = first_norm * gains[1]
    tanh_attn = jnp.tanh(gate_attn)
    middle = source + tanh_attn * branch_attn
    feed_norm, feed_inv = rms_parts(middle)
    feed_all = jnp.concatenate(spread(half(feed_norm * gains[2] * (1.0 + scale_feed))), axis=0)
    gate_up = dot(feed_all, feed_full, 1, 0)
    gate_part, up_part = gate_up[:, :units], gate_up[:, units:]
    sigmoid_gate = jax.nn.sigmoid(gate_part)
    silu_gate = gate_part * sigmoid_gate
    hidden = half(silu_gate * up_part)

    def split(value):
        return [value[i * shard_rows : (i + 1) * shard_rows] for i in range(tensor_size)]

    feed_sum = collect(split(dot(hidden, down_full, 1, 1)))
    second_norm, second_inv = rms_parts(feed_sum)
    branch_feed = second_norm * gains[3]
    tanh_feed = jnp.tanh(gate_feed)
    block_out = middle + tanh_feed * branch_feed
    branch_feed_grad = tanh_feed * cotangent
    gate_feed_grad = cotangent * branch_feed * (1.0 - tanh_feed * tanh_feed)
    feed_sum_grad = jnp.concatenate(
        spread(half(rms_back(second_norm, second_inv, branch_feed_grad * gains[3]))), axis=0
    )
    hidden_grad = dot(feed_sum_grad, down_full, 1, 0)
    feed_out_sum = scatter_dp(half(dot(feed_sum_grad, hidden, 0, 0)))
    gate_grad = (
        hidden_grad * up_part * (sigmoid_gate + gate_part * sigmoid_gate * (1.0 - sigmoid_gate))
    )
    up_grad = hidden_grad * silu_gate
    pair_grad = jnp.concatenate([half(gate_grad), half(up_grad)], axis=1)
    feed_input_grad = collect(split(dot(pair_grad, feed_full, 1, 1)))
    feed_in_sum = scatter_dp(half(dot(feed_all, pair_grad, 0, 0)))
    scale_feed_grad = feed_input_grad * feed_norm * gains[2]
    middle_grad = cotangent + rms_back(
        feed_norm, feed_inv, feed_input_grad * gains[2] * (1.0 + scale_feed)
    )
    branch_attn_grad = tanh_attn * middle_grad
    gate_attn_grad = middle_grad * branch_attn * (1.0 - tanh_attn * tanh_attn)
    attn_sum_grad = in_place(
        spread(half(rms_back(first_norm, first_inv, branch_attn_grad * gains[1])))
    )
    mixed_grad = dot(out_full, attn_sum_grad, 0, 1)
    out_sum = scatter_dp(half(dot(attn_sum_grad, mixed, 0, 1)))
    gate_channel_grad = jnp.sum(mixed_grad * other_out, axis=1, keepdims=True) * (
        1.0 - cross_gate * cross_gate
    )
    own_grad = half(mixed_grad)
    other_grad = half(cross_gate * mixed_grad)
    query_two, text_key_grad, text_value_grad = attention_back(
        True,
        cross_meta,
        lengths,
        ids_row,
        ids_column,
        queries,
        text_key_rows,
        text_keys,
        text_value_rows,
        other_inv,
        other_out,
        other_grad,
    )
    text_value_full = in_place(spread(half(text_value_grad)))
    text_key_grad = text_key_grad.reshape(heads, HEAD, slots)
    text_gain_grad = jnp.sum(text_key_grad * text_key_norm, axis=2)
    text_raw_grad = rms_back(text_key_norm, text_key_inv, text_key_grad * local_gains[6], 1)
    text_key_full = in_place(spread(half(text_raw_grad).reshape(local, slots)))
    value_sum = scatter_dp(half(dot(text_value_full, captions, 1, 0)))
    key_sum = scatter_dp(half(dot(text_key_full, captions, 1, 0)))
    query_one, key_rot_grad, value_grad = attention_back(
        False,
        self_meta,
        lengths,
        ids_row,
        ids_column,
        queries,
        key_rows,
        keys,
        value_rows,
        own_inv,
        own_out,
        own_grad,
    )
    query_turn = rotate(
        (query_one + query_two).reshape(heads, HEAD, row_tokens), cosine, -sine
    )
    key_turn = rotate(key_rot_grad.reshape(heads, HEAD, row_tokens), cosine, -sine)
    query_gain_grad = jnp.sum(query_turn * query_norm, axis=2)
    key_gain_grad = jnp.sum(key_turn * key_norm, axis=2)
    query_raw_grad = rms_back(query_norm, query_inv, query_turn * local_gains[4], 1)
    key_raw_grad = rms_back(key_norm, key_inv, key_turn * local_gains[5], 1)
    triple_grad = jnp.concatenate(
        [
            half(query_raw_grad).reshape(local, row_tokens),
            half(key_raw_grad).reshape(local, row_tokens),
            half(value_grad),
        ],
        axis=0,
    )
    attn_input_grad = collect(
        [
            dot(
                lax.dynamic_slice_in_dim(triple_grad, owner(i) * shard_rows, shard_rows, 1),
                in_full,
                0,
                1,
            )
            for i in range(tensor_size)
        ]
    )
    in_sum = scatter_dp(half(dot(attn_full, triple_grad, 0, 1)))
    scale_attn_grad = attn_input_grad * attn_norm * gains[0]
    latent_grad = middle_grad + rms_back(
        attn_norm, attn_inv, attn_input_grad * gains[0] * (1.0 + scale_attn)
    )
    shared_rows = jnp.stack(
        [
            jnp.sum(attn_input_grad * attn_norm * (1.0 + scale_attn), axis=0),
            jnp.sum(branch_attn_grad * first_norm, axis=0),
            jnp.sum(feed_input_grad * feed_norm * (1.0 + scale_feed), axis=0),
            jnp.sum(branch_feed_grad * second_norm, axis=0),
        ]
    )
    head_rows = jnp.stack(
        [
            query_gain_grad.reshape(local),
            key_gain_grad.reshape(local),
            text_gain_grad.reshape(local),
            gate_channel_grad.reshape(local),
        ]
    )
    head_full = lax.dynamic_update_slice(
        jnp.zeros((4, width), jnp.float32), head_rows, (jnp.zeros((), jnp.int32), offset)
    )
    channel_total = lax.psum(
        jnp.concatenate([shared_rows, head_full], axis=0), ("dp", "tensor")
    )
    channel_columns = channels.shape[1]
    channel_sum = lax.dynamic_slice_in_dim(
        channel_total, dp_index * channel_columns, channel_columns, 1
    )
    factor_tokens = jnp.concatenate(
        [scale_attn_grad, gate_attn_grad, scale_feed_grad, gate_feed_grad], axis=1
    )
    factor_image = jnp.dot(chooser.T, factor_tokens, precision=HIGH)
    factor_image = jnp.transpose(
        factor_image.reshape(per_row, dp_size, tensor_size, own_columns), (2, 1, 0, 3)
    )
    factor_mine = lax.psum_scatter(factor_image, "tensor", scatter_dimension=0, tiled=False)
    factor_grad = lax.all_to_all(factor_mine, "dp", 0, 0, tiled=True).reshape(images, own_columns)
    modulator_sum = jnp.dot(augmented.astype(jnp.float32).T, factor_grad, precision=HIGH)

    in_sum, out_sum, feed_in_sum, feed_out_sum, key_sum, value_sum = (
        value.astype(jnp.float32)
        for value in (in_sum, out_sum, feed_in_sum, feed_out_sum, key_sum, value_sum)
    )
    squares = (
        jnp.sum(in_sum * in_sum)
        + jnp.sum(out_sum * out_sum)
        + jnp.sum(feed_in_sum * feed_in_sum)
        + jnp.sum(feed_out_sum * feed_out_sum)
        + jnp.sum(key_sum * key_sum)
        + jnp.sum(value_sum * value_sum)
        + jnp.sum(modulator_sum * modulator_sum)
        + jnp.sum(channel_sum * channel_sum) / tensor_size
    )
    in_sum = jnp.stack([in_sum[:, i * local : (i + 1) * local] for i in range(3)])
    feed_in_sum = jnp.stack([feed_in_sum[:, i * units : (i + 1) * units] for i in range(2)])
    caption_sum = jnp.stack([key_sum.T, value_sum.T])
    grad_norm = jnp.sqrt(lax.psum(squares, ("dp", "tensor")))
    factor = CLIP / jnp.maximum(grad_norm, CLIP)
    results = [
        adamw(grad * factor, weight, moment, square, DECAY, RATE)
        for grad, weight, moment, square in (
            (in_sum, attention_in, moment_attention_in, square_attention_in),
            (out_sum.T, attention_out, moment_attention_out, square_attention_out),
            (feed_in_sum, feed_in, moment_feed_in, square_feed_in),
            (feed_out_sum.T, feed_out, moment_feed_out, square_feed_out),
            (caption_sum, caption_in, moment_caption_in, square_caption_in),
            (modulator_sum, modulator, moment_modulator, square_modulator),
        )
    ]
    results.append(
        adamw(channel_sum * factor, channels, moment_channels, square_channels, 0.0, GAIN_RATE)
    )
    return (block_out, latent_grad, grad_norm, *(part for result in results for part in result))


def solution(mesh):
    return jax.shard_map(
        body,
        mesh=mesh,
        in_specs=(
            P(("dp", "tensor"), None),
            P(("dp", "tensor"), None),
            P("dp", "tensor"),
            P(),
            P("dp", None),
            P("dp", None),
            P("dp", None),
            P("dp", None),
            P(None, "dp", "tensor"),
            P("tensor", "dp"),
            P(None, "dp", "tensor"),
            P("tensor", "dp"),
            P(None, "tensor", "dp"),
            P(None, ("dp", "tensor")),
            P(None, "dp"),
            P(None, "dp", "tensor"),
            P(None, "dp", "tensor"),
            P("tensor", "dp"),
            P("tensor", "dp"),
            P(None, "dp", "tensor"),
            P(None, "dp", "tensor"),
            P("tensor", "dp"),
            P("tensor", "dp"),
            P(None, "tensor", "dp"),
            P(None, "tensor", "dp"),
            P(None, ("dp", "tensor")),
            P(None, ("dp", "tensor")),
            P(None, "dp"),
            P(None, "dp"),
        ),
        out_specs=(
            P(("dp", "tensor"), None),
            P(("dp", "tensor"), None),
            P(),
            P(None, "dp", "tensor"),
            P(None, "dp", "tensor"),
            P(None, "dp", "tensor"),
            P("tensor", "dp"),
            P("tensor", "dp"),
            P("tensor", "dp"),
            P(None, "dp", "tensor"),
            P(None, "dp", "tensor"),
            P(None, "dp", "tensor"),
            P("tensor", "dp"),
            P("tensor", "dp"),
            P("tensor", "dp"),
            P(None, "tensor", "dp"),
            P(None, "tensor", "dp"),
            P(None, "tensor", "dp"),
            P(None, ("dp", "tensor")),
            P(None, ("dp", "tensor")),
            P(None, ("dp", "tensor")),
            P(None, "dp"),
            P(None, "dp"),
            P(None, "dp"),
        ),
        check_vma=False,
    )
```

time: 2760 us -> 1120 us (0.41)
  waiting for transfers between devices: 1850 us -> 400 us
  matrix products: 375 us -> 131 us
  local copies, waits for them, and re-layouts: 217 us -> 107 us
  Pallas kernels: 0 us -> 86.6 us
  blocking collectives: 77.8 us -> 148 us
  starting transfers between devices: 1.85 us -> 41.5 us
    reduce_scatter x8 -> x7, waiting for transfers between devices: 714 us -> 0.07 us  [the longest x6 0.07 us: scatter_dp(): lax.psum_scatter(summed, 'dp', scatter_dimension=0, tiled=True, axis_inde...]
    unnamed x27 -> x12, waiting for transfers between devices: 687 us -> 0.88 us
    all_gather x11 -> x5, waiting for transfers between devices: 446 us -> 13 us  [the longest x4 13 us: gather_dp(): lax.all_gather(value, 'dp', axis=0, tiled=True, axis_index_groups=groups)]
    ppermute x0 -> x42, waiting for transfers between devices: none -> 386 us  [the longest x30 205 us: swap_tensor(): lax.ppermute(value, 'tensor', [(i, i ^ bits) for i in range(lax.axis_size...]
    dot_general x42 -> x28, matrix products: 362 us -> 124 us  [dot(): lax.dot_general(left, right, (((left_dim,), (right_dim,)), ((), ())), pre...]
    dynamic_update_slice x12 -> x0, local copies, waits for them, and re-layouts: 96.6 us -> none  [body(): lax.scan(forward_block, jnp.zeros((), jnp.float32), (query_blocks, id_blo...]
    pallas_call x0 -> x4, Pallas kernels: none -> 86.6 us  [the longest x2 50.6 us: attention_back(): pl.pallas_call(functools.partial(attention_back_kernel, heads, cross), gr...]
    convert_element_type x16 -> x20, other arithmetic: 75.4 us -> 34.4 us  [half(): return value.astype(jnp.bfloat16)]
  transfers between devices with their start and end apart: 23 -> 56, of which waited for: 21 -> 24; matrix products, arithmetic and copies ran while one was open for 14% -> 29% of each run, Pallas kernels for 0% -> 8%
where the time goes in v1:
time: 1120 us; the launch traced here: 1110 us
  waiting for transfers between devices  400 us (36%)
  other arithmetic  170 us (15%)
  blocking collectives  148 us (13%)
  matrix products  131 us (12%)
  local copies, waits for them, and re-layouts  107 us (10%)
  Pallas kernels  86.6 us (8%)
  starting transfers between devices  41.5 us (4%)
  between operations  24.2 us (2%)
    ppermute x30, waiting for transfers between devices, swap_tensor(): lax.ppermute(value, 'tensor', [(i, i ^ bits) for i in range(lax.axis_size...  205 us
    ppermute x12, waiting for transfers between devices, near_swap(): lax.ppermute(value, 'dp', [(i, i ^ 1) for i in range(lax.axis_size('dp'))])  182 us
    dot_general x28, matrix products, dot(): lax.dot_general(left, right, (((left_dim,), (right_dim,)), ((), ())), pre...  124 us
    pallas_call x2, Pallas kernels, attention_back(): pl.pallas_call(functools.partial(attention_back_kernel, heads, cross), gr...  50.6 us
    unnamed x369, local copies, waits for them, and re-layouts  45 us
    psum x1, blocking collectives, body(): lax.psum(jnp.concatenate([shared_rows, head_full], axis=0), ('dp', 'tenso...  41.4 us
    psum x1, blocking collectives, body(): grad_norm = jnp.sqrt(lax.psum(squares, ('dp', 'tensor')))  40.4 us
    pallas_call x2, Pallas kernels, attention(): pl.pallas_call(functools.partial(attention_kernel, heads, cross), grid_sp...  36 us
  transfers between devices with their start and end apart: 56, of which 24 were waited for; matrix products, arithmetic and copies ran while one was open for 29% of the time, Pallas kernels for 8%

profile of v1, /device:TPU:0, one launch (start us, length us, event | category | flops | bytes accessed | tf_op | source)
XLA Modules:
  0.0 1108.5 jit_solution(17211967702960787558)
XLA Ops:
  20.6 25.0 %all_gather.33 = bf16[768,384]{1,0:T(8,128)(2,1)S(1)} all-gather(bf16[192,384]{1,0:T(8,128)(2,1)S(1)} %convert_bitcast_fusion.3), channel_id=1, replica_groups={{0,8,16,24},{4,12,20,28},{1,9,17,25},{5,13,21,29},{2,10,18,26},{6,14,22..., dimensions={0}, use_global_device_ids=true | all-gather | bytes 737280 | tf_op jit(solution)/shard_map/all_gather | solution.py:92
  48.2 35.2 %all-gather.1 = bf16[8,192,8]{1,2,0:T(8,128)(2,1)S(1)} all-gather(bf16[1,192,8]{1,2,0:T(8,128)(2,1)S(1)} %convert_bitcast_fusion.4), channel_id=1, replica_groups=mesh['dp'=8,'tensor'=4] {'dp'}, dimensions={0}, use_global_device_ids=true | all-gather | bytes 27648 | tf_op jit(solution)/shard_map/all_gather | solution.py:419
  100.3 17.1 %collective-permute-done.2 = bf16[256,1536]{1,0:T(8,128)(2,1)} collective-permute-done((bf16[256,1536]{1,0:T(8,128)(2,1)S(1)}, bf16[256,1536]{1,0:T(8,128)(2,1)}, u32[]{:S(2)}, u32[]{:S(2)}) %collective-permute-start.2) | collective-permute-done | bytes 786464 | tf_op jit(solution)/shard_map/ppermute | solution.py:118
  141.8 13.1 %collective-permute-done.7 = bf16[768,1024]{1,0:T(8,128)(2,1)} collective-permute-done((bf16[768,1024]{1,0:T(8,128)(2,1)}, bf16[768,1024]{1,0:T(8,128)(2,1)}, u32[]{:S(2)}, u32[]{:S(2)}) %collective-permute-start.7) | collective-permute-done | bytes 1572896 | tf_op jit(solution)/shard_map/ppermute | solution.py:75
  166.2 22.4 %collective-permute-done.4 = bf16[768,1024]{1,0:T(8,128)(2,1)} collective-permute-done((bf16[768,1024]{1,0:T(8,128)(2,1)}, bf16[768,1024]{1,0:T(8,128)(2,1)}, u32[]{:S(2)}, u32[]{:S(2)}) %collective-permute-start.4) | collective-permute-done | bytes 1572896 | tf_op jit(solution)/shard_map/ppermute | solution.py:75
  196.6 29.4 %collective-permute-done = bf16[768,1152]{1,0:T(8,128)(2,1)S(1)} collective-permute-done((bf16[768,1152]{1,0:T(8,128)(2,1)}, bf16[768,1152]{1,0:T(8,128)(2,1)S(1)}, u32[]{:S(2)}, u32[]{:S(2)}) %collective-permute-start) | collective-permute-done | bytes 1769504 | tf_op jit(solution)/shard_map/ppermute | solution.py:75
  270.9 17.9 %self_forward.1 = (f32[384,1024]{1,0:T(8,128)S(1)}, f32[6,8,1024]{2,1,0:T(8,128)S(1)}) custom-call(s32[8]{0:T(128)S(1)} %reshape.746.meta, s32[8]{0:T(128)S(1)} %bitcast.307, s32[1,1024]{1,0:T(1,128)S(1)} %copy-done.12, s32[1024,1]{1,0:T(8,128)S(1)} %copy.219.ids_column, bf16[384,1024]{1,0:T(8,128)(2,1)S(1)} %bitcast.297, ...), custom_call_target="tpu_custom_call" | custom-call | flops 805306368 | bytes 6291456 | tf_op jit(solution)/shard_map/self_forward/pallas_call | solution.py:266
  306.9 19.9 %collective-permute-done.9 = bf16[384,2048]{1,0:T(8,128)(2,1)} collective-permute-done((bf16[384,2048]{1,0:T(8,128)(2,1)}, bf16[384,2048]{1,0:T(8,128)(2,1)}, u32[]{:S(2)}, u32[]{:S(2)}) %collective-permute-start.9) | collective-permute-done | bytes 1572896 | tf_op jit(solution)/shard_map/ppermute | solution.py:118
  335.9 18.1 %cross_forward.1 = (f32[384,1024]{1,0:T(8,128)S(1)}, f32[6,8,1024]{2,1,0:T(8,128)S(1)}) custom-call(s32[8]{0:T(128)S(1)} %reshape.750.meta, s32[8]{0:T(128)S(1)} %bitcast.308, s32[1,1024]{1,0:T(1,128)S(1)} %copy-done.12, s32[1024,1]{1,0:T(8,128)S(1)} %copy.219.ids_column, bf16[384,1024]{1,0:T(8,128)(2,1)S(1)} %bitcast.298, ...), custom_call_target="tpu_custom_call" | custom-call | flops 805306368 | bytes 6291456 | tf_op jit(solution)/shard_map/cross_forward/pallas_call | solution.py:266
  372.7 15.6 %collective-permute-done.12 = bf16[256,1536]{1,0:T(8,128)(2,1)} collective-permute-done((bf16[256,1536]{1,0:T(8,128)(2,1)}, bf16[256,1536]{1,0:T(8,128)(2,1)}, u32[]{:S(2)}, u32[]{:S(2)}) %collective-permute-start.12) | collective-permute-done | bytes 786464 | tf_op jit(solution)/shard_map/ppermute | solution.py:118
  396.2 17.3 %collective-permute-done.14 = bf16[256,1536]{1,0:T(8,128)(2,1)S(1)} collective-permute-done((bf16[256,1536]{1,0:T(8,128)(2,1)S(1)}, bf16[256,1536]{1,0:T(8,128)(2,1)S(1)}, u32[]{:S(2)}, u32[]{:S(2)}) %collective-permute-start.14) | collective-permute-done | bytes 786464 | tf_op jit(solution)/shard_map/ppermute | solution.py:118
  413.5 26.5 %collective-permute-done.16 = bf16[768,2048]{1,0:T(8,128)(2,1)} collective-permute-done((bf16[768,2048]{1,0:T(8,128)(2,1)}, bf16[768,2048]{1,0:T(8,128)(2,1)}, u32[]{:S(2)}, u32[]{:S(2)}) %collective-permute-start.16) | collective-permute-done | bytes 3145760 | tf_op jit(solution)/shard_map/ppermute | solution.py:75
  466.9 19.0 %collective-permute-done.19 = bf16[256,1536]{1,0:T(8,128)(2,1)S(1)} collective-permute-done((bf16[256,1536]{1,0:T(8,128)(2,1)S(1)}, bf16[256,1536]{1,0:T(8,128)(2,1)S(1)}, u32[]{:S(2)}, u32[]{:S(2)}) %collective-permute-start.19) | collective-permute-done | bytes 786464 | tf_op jit(solution)/shard_map/ppermute | solution.py:118
  491.0 18.1 %collective-permute-done.21 = bf16[256,1536]{1,0:T(8,128)(2,1)S(1)} collective-permute-done((bf16[256,1536]{1,0:T(8,128)(2,1)S(1)}, bf16[256,1536]{1,0:T(8,128)(2,1)S(1)}, u32[]{:S(2)}, u32[]{:S(2)}) %collective-permute-start.21) | collective-permute-done | bytes 786464 | tf_op jit(solution)/shard_map/ppermute | solution.py:118
  569.4 18.6 %collective-permute-done.26 = bf16[256,1536]{1,0:T(8,128)(2,1)} collective-permute-done((bf16[256,1536]{1,0:T(8,128)(2,1)}, bf16[256,1536]{1,0:T(8,128)(2,1)}, u32[]{:S(2)}, u32[]{:S(2)}) %collective-permute-start.26) | collective-permute-done | bytes 786464 | tf_op jit(solution)/shard_map/ppermute | solution.py:118
  614.2 25.7 %cross_backward.1 = (f32[384,1024]{1,0:T(8,128)}, f32[384,2048]{1,0:T(8,128)}, f32[384,2048]{1,0:T(8,128)}) custom-call(s32[8]{0:T(128)} %copy-done.13, s32[8]{0:T(128)} %bitcast.305, s32[1,1024]{1,0:T(1,128)} %ids_row.7, s32[1024,1]{1,0:T(8,128)} %copy-done.1, bf16[384,1024]{1,0:T(8,128)(2,1)} %bitcast.299, bf16[6,2048,64]{2,1,0:T(8,128)(2,1)} %fusion.33.k_ref, ...), custom_call_target="tpu_custom_call" | custom-call | flops 2013265920 | bytes 11796480 | tf_op jit(solution)/shard_map/cross_backward/pallas_call | solution.py:304
  639.8 24.9 %self_backward.1 = (f32[384,1024]{1,0:T(8,128)}, f32[384,1024]{1,0:T(8,128)}, f32[384,1024]{1,0:T(8,128)}) custom-call(s32[8]{0:T(128)} %copy-done.15, s32[8]{0:T(128)} %bitcast.306, s32[1,1024]{1,0:T(1,128)} %ids_row.7, s32[1024,1]{1,0:T(8,128)} %copy-done.1, bf16[384,1024]{1,0:T(8,128)(2,1)} %bitcast.300, bf16[6,1024,64]{2,1,0:T(8,128)(2,1)} %copy-done.7, ...), custom_call_target="tpu_custom_call" | custom-call | flops 2013265920 | bytes 11796480 | tf_op jit(solution)/shard_map/self_backward/pallas_call | solution.py:304
  756.5 14.7 %collective-permute-done.30 = bf16[768,1152]{1,0:T(8,128)(2,1)} collective-permute-done((bf16[768,1152]{1,0:T(8,128)(2,1)}, bf16[768,1152]{1,0:T(8,128)(2,1)}, u32[]{:S(2)}, u32[]{:S(2)}) %collective-permute-start.30) | collective-permute-done | bytes 1769504 | tf_op jit(solution)/shard_map/ppermute | solution.py:75
  793.6 34.0 %collective-permute-done.35 = bf16[384,2048]{1,0:T(8,128)(2,1)} collective-permute-done((bf16[384,2048]{1,0:T(8,128)(2,1)S(1)}, bf16[384,2048]{1,0:T(8,128)(2,1)}, u32[]{:S(2)}, u32[]{:S(2)}) %collective-permute-start.35) | collective-permute-done | bytes 1572896 | tf_op jit(solution)/shard_map/ppermute | solution.py:118
  843.5 16.2 %collective-permute-done.39 = bf16[384,2048]{1,0:T(8,128)(2,1)} collective-permute-done((bf16[384,2048]{1,0:T(8,128)(2,1)}, bf16[384,2048]{1,0:T(8,128)(2,1)}, u32[]{:S(2)}, u32[]{:S(2)}) %collective-permute-start.39) | collective-permute-done | bytes 1572896 | tf_op jit(solution)/shard_map/ppermute | solution.py:118
  883.6 30.2 %collective-permute-done.37 = bf16[768,1024]{1,0:T(8,128)(2,1)S(1)} collective-permute-done((bf16[768,1024]{1,0:T(8,128)(2,1)S(1)}, bf16[768,1024]{1,0:T(8,128)(2,1)S(1)}, u32[]{:S(2)}, u32[]{:S(2)}) %collective-permute-start.37) | collective-permute-done | bytes 1572896 | tf_op jit(solution)/shard_map/ppermute | solution.py:75
  929.1 34.7 %collective-permute-done.41 = bf16[768,1024]{1,0:T(8,128)(2,1)S(1)} collective-permute-done((bf16[768,1024]{1,0:T(8,128)(2,1)S(1)}, bf16[768,1024]{1,0:T(8,128)(2,1)S(1)}, u32[]{:S(2)}, u32[]{:S(2)}) %collective-permute-start.41) | collective-permute-done | bytes 1572896 | tf_op jit(solution)/shard_map/ppermute | solution.py:75
  979.2 41.4 %psum.14 = f32[8,1536]{1,0:T(8,128)S(1)} all-reduce(f32[8,1536]{1,0:T(8,128)S(1)} %concatenate.123), channel_id=1, replica_groups=mesh['dp'=8,'tensor'=4] {'dp','tensor'}, use_global_device_ids=true, to_apply=%region_38.39 | all-reduce | flops 12288 | bytes 98304 | tf_op jit(solution)/shard_map/psum | solution.py:638
  1040.1 40.4 %psum.15 = f32[]{:T(128)} all-reduce(f32[]{:T(128)S(6)} %add.536), channel_id=1, replica_groups=mesh['dp'=8,'tensor'=4] {'dp','tensor'}, use_global_device_ids=true, to_apply=%region_40.41 | all-reduce | flops 1 | bytes 8 | tf_op jit(solution)/shard_map/psum | solution.py:673
  (704 shorter events, 508.9 us)
Async XLA Ops:
  7.2 110.2 %all-gather.12.cloned.1.call-start = ((), (), s32[]{:S(2)}) async-start(), calls=%async_computation.11 | async-start | bytes 1966080 | tf_op jit(solution)/shard_map/all_gather | solution.py:92
  9.8 116.8 %all-gather.10.cloned.1.call-start = ((), (), s32[]{:S(2)}) async-start(), calls=%async_computation.10 | async-start | bytes 1966080 | tf_op jit(solution)/shard_map/all_gather | solution.py:92
  10.6 129.7 %all-gather.8.cloned.1.call-start = ((), (), s32[]{:S(2)}) async-start(), calls=%async_computation.9 | async-start | bytes 2211840 | tf_op jit(solution)/shard_map/all_gather | solution.py:92
  13.3 72.3 %all-to-all-start = ((f32[8,8,192]{2,1,0:T(8,128)}), f32[8,8,192]{2,1,0:T(8,128)S(1)}, u32[]{:S(2)}, u32[]{:S(2)}) async-start(f32[8,8,192]{2,1,0:T(8,128)} %convolution_bitcast_fusion), calls=%async_computation | async-start | bytes 131072 | tf_op jit(solution)/shard_map/all_to_all | solution.py:427
  20.5 349.3 %all-gather.14.cloned.1.call-start = ((), (), s32[]{:S(2)}) async-start(), calls=%async_computation.12 | async-start | bytes 3932160 | tf_op jit(solution)/shard_map/all_gather | solution.py:92
  45.6 74.6 %collective-permute-start.10 = (bf16[768,384]{1,0:T(8,128)(2,1)S(1)}, bf16[768,384]{1,0:T(8,128)(2,1)}, u32[]{:S(2)}, u32[]{:S(2)}) collective-permute-start(bf16[768,384]{1,0:T(8,128)(2,1)S(1)} %all_gather.33), channel_id=1, source_target_pairs={{0,4},{4,0},{8,12},{12,8},{16,20},{20,16},{24,28},{28,24},{1,5},{5... | collective-permute-start | bytes 1769480 | tf_op jit(solution)/shard_map/ppermute | solution.py:75
  48.1 407.7 %all-gather.16.cloned.1.call-start = ((), (), s32[]{:S(2)}) async-start(), calls=%async_computation.13 | async-start | bytes 3932160 | tf_op jit(solution)/shard_map/all_gather | solution.py:91
  126.7 61.9 %collective-permute-start.4 = (bf16[768,1024]{1,0:T(8,128)(2,1)}, bf16[768,1024]{1,0:T(8,128)(2,1)}, u32[]{:S(2)}, u32[]{:S(2)}) collective-permute-start(bf16[768,1024]{1,0:T(8,128)(2,1)} %all-gather.10.cloned.1.call-done), channel_id=1, source_target_pairs={{0,4},{4,0},{8,12},{12,8},{16,20},{20,16},{24,28},{28,24},{1,5},{5... | collective-permute-start | bytes 4718600 | tf_op jit(solution)/shard_map/ppermute | solution.py:75
  140.3 85.7 %collective-permute-start = (bf16[768,1152]{1,0:T(8,128)(2,1)}, bf16[768,1152]{1,0:T(8,128)(2,1)S(1)}, u32[]{:S(2)}, u32[]{:S(2)}) collective-permute-start(bf16[768,1152]{1,0:T(8,128)(2,1)} %all-gather.8.cloned.1.call-done), channel_id=1, source_target_pairs={{0,4},{4,0},{8,12},{12,8},{16,20},{20,16},{24,28},{28,24},{1,5},{5... | collective-permute-start | bytes 5308424 | tf_op jit(solution)/shard_map/ppermute | solution.py:75
  166.2 94.3 %collective-permute-start.8 = (bf16[768,2048]{1,0:T(8,128)(2,1)}, bf16[768,2048]{1,0:T(8,128)(2,1)}, u32[]{:S(2)}, u32[]{:S(2)}) collective-permute-start(bf16[768,2048]{1,0:T(8,128)(2,1)} %pad_maximum_fusion.10), channel_id=1, source_target_pairs={{0,1},{1,0},{2,3},{3,2},{4,5},{5,4},{6,7},{7,6},{8,9},{9,8},{10,11... | collective-permute-start | bytes 9437192 | tf_op jit(solution)/shard_map/ppermute | solution.py:118
  196.6 53.7 %collective-permute-start.5 = (bf16[768,2048]{1,0:T(8,128)(2,1)}, bf16[768,2048]{1,0:T(8,128)(2,1)}, u32[]{:S(2)}, u32[]{:S(2)}) collective-permute-start(bf16[768,2048]{1,0:T(8,128)(2,1)} %pad_maximum_fusion.8), channel_id=1, source_target_pairs={{0,1},{1,0},{2,3},{3,2},{4,5},{5,4},{6,7},{7,6},{8,9},{9,8},{10,11... | collective-permute-start | bytes 9437192 | tf_op jit(solution)/shard_map/ppermute | solution.py:118
  269.2 57.6 %collective-permute-start.9 = (bf16[384,2048]{1,0:T(8,128)(2,1)}, bf16[384,2048]{1,0:T(8,128)(2,1)}, u32[]{:S(2)}, u32[]{:S(2)}) collective-permute-start(bf16[384,2048]{1,0:T(8,128)(2,1)} %fusion.34), channel_id=1, source_target_pairs={{0,2},{1,3},{2,0},{3,1},{4,6},{5,7},{6,4},{7,5},{8,10},{9,11},{10,... | collective-permute-start | bytes 4718600 | tf_op jit(solution)/shard_map/ppermute | solution.py:118
  369.9 70.2 %collective-permute-start.16 = (bf16[768,2048]{1,0:T(8,128)(2,1)}, bf16[768,2048]{1,0:T(8,128)(2,1)}, u32[]{:S(2)}, u32[]{:S(2)}) collective-permute-start(bf16[768,2048]{1,0:T(8,128)(2,1)} %all-gather.14.cloned.1.call-done), channel_id=1, source_target_pairs={{0,4},{4,0},{8,12},{12,8},{16,20},{20,16},{24,28},{28,24},{1,5},{5... | collective-permute-start | bytes 9437192 | tf_op jit(solution)/shard_map/ppermute | solution.py:75
  372.2 594.6 %reduce-scatter.14.cloned.1.call-start = ((), (), s32[]{:S(2)}) async-start(), calls=%async_computation.17 | async-start | bytes 1966080 | tf_op jit(solution)/shard_map/reduce_scatter | solution.py:112
  546.5 54.0 %collective-permute-start.33 = (bf16[768,1024]{1,0:T(8,128)(2,1)}, bf16[768,1024]{1,0:T(8,128)(2,1)}, u32[]{:S(2)}, u32[]{:S(2)}) collective-permute-start(bf16[768,1024]{1,0:T(8,128)(2,1)} %bitcast.88), channel_id=1, source_target_pairs={{0,4},{4,0},{8,12},{12,8},{16,20},{20,16},{24,28},{28,24},{1,5},{5... | collective-permute-start | bytes 4718600 | tf_op jit(solution)/shard_map/ppermute | solution.py:75
  603.7 364.9 %reduce-scatter.10.cloned.1.call-start = ((), (), s32[]{:S(2)}) async-start(), calls=%async_computation.15 | async-start | bytes 737280 | tf_op jit(solution)/shard_map/reduce_scatter | solution.py:112
  740.4 229.7 %reduce-scatter.20.cloned.1.call-start = ((), (), s32[]{:S(2)}) async-start(), calls=%async_computation.20 | async-start | bytes 327680 | tf_op jit(solution)/shard_map/reduce_scatter | solution.py:652
  747.4 90.9 %collective-permute-start.32 = (bf16[768,2048]{1,0:T(8,128)(2,1)}, bf16[768,2048]{1,0:T(8,128)(2,1)}, u32[]{:S(2)}, u32[]{:S(2)}) collective-permute-start(bf16[768,2048]{1,0:T(8,128)(2,1)} %bitcast.85), channel_id=1, source_target_pairs={{0,4},{4,0},{8,12},{12,8},{16,20},{20,16},{24,28},{28,24},{1,5},{5... | collective-permute-start | bytes 9437192 | tf_op jit(solution)/shard_map/ppermute | solution.py:75
  756.5 266.7 %reduce-scatter.8.cloned.1.call-start = ((), (), s32[]{:S(2)}) async-start(), calls=%async_computation.14 | async-start | bytes 2211840 | tf_op jit(solution)/shard_map/reduce_scatter | solution.py:112
  774.9 253.5 %reduce-scatter.12.cloned.1.call-start = ((), (), s32[]{:S(2)}) async-start(), calls=%async_computation.16 | async-start | bytes 3932160 | tf_op jit(solution)/shard_map/reduce_scatter | solution.py:112
  790.8 68.8 %collective-permute-start.34 = (bf16[384,2048]{1,0:T(8,128)(2,1)S(1)}, bf16[384,2048]{1,0:T(8,128)(2,1)}, u32[]{:S(2)}, u32[]{:S(2)}) collective-permute-start(bf16[384,2048]{1,0:T(8,128)(2,1)S(1)} %get-tuple-element.109), channel_id=1, source_target_pairs={{0,1},{1,0},{2,3},{3,2},{4,5},{5,4},{6,7},{7,6},{8,9},{9,8},{10,11... | collective-permute-start | bytes 4718600 | tf_op jit(solution)/shard_map/ppermute | solution.py:118
  792.2 67.4 %collective-permute-start.39 = (bf16[384,2048]{1,0:T(8,128)(2,1)}, bf16[384,2048]{1,0:T(8,128)(2,1)}, u32[]{:S(2)}, u32[]{:S(2)}) collective-permute-start(bf16[384,2048]{1,0:T(8,128)(2,1)} %convert_element_type.392), channel_id=1, source_target_pairs={{0,2},{1,3},{2,0},{3,1},{4,6},{5,7},{6,4},{7,5},{8,10},{9,11},{10,... | collective-permute-start | bytes 4718600 | tf_op jit(solution)/shard_map/ppermute | solution.py:118
  843.4 189.8 %reduce-scatter.16.cloned.1.call-start = ((), (), s32[]{:S(2)}) async-start(), calls=%async_computation.18 | async-start | bytes 1966080 | tf_op jit(solution)/shard_map/reduce_scatter | solution.py:112
  915.8 120.0 %reduce-scatter.18.cloned.1.call-start = ((), (), s32[]{:S(2)}) async-start(), calls=%async_computation.19 | async-start | bytes 1966080 | tf_op jit(solution)/shard_map/reduce_scatter | solution.py:112
  (214 other events, 3899.8 us)
Sparse Core Ops, SparseCore 0:
  10.2 50.3 all-gather.11
  62.7 36.1 all-gather.9
  101.0 39.2 all-gather.7
  142.3 62.3 all-gather.13
  372.3 63.4 all-gather.15
  603.8 35.4 reduce-scatter.13
  740.5 21.3 reduce-scatter.9
  764.9 18.4 reduce-scatter.19
  785.8 38.3 reduce-scatter.7
  843.5 60.1 reduce-scatter.11
  915.9 35.2 reduce-scatter.15
  965.9 36.3 reduce-scatter.17

commit v2 on v1

v2 whole, which is shorter than its diff:
```python
import functools
import math

import jax
import jax.numpy as jnp
from jax import lax
from jax.experimental import pallas as pl
from jax.experimental.pallas import tpu as pltpu
from jax.sharding import PartitionSpec as P

HEAD = 64
CAP = 256
STEP = 10


EPS = 1e-06
NEG = -1e30
THETA = 10000.0
BETA1 = 0.9
BETA2 = 0.95
RATE = 0.05
GAIN_RATE = 0.8
DECAY = 0.1
ADAM_EPS = 1e-08
CLIP = 1.0
HIGH = lax.Precision.HIGHEST


def half(value):
    return value.astype(jnp.bfloat16)


TILE = 256
LOG2E = 1.0 / math.log(2.0)
MESH = pl.DeviceIdType.MESH


def dot(left, right, left_dim, right_dim):
    return lax.dot_general(
        left, right, (((left_dim,), (right_dim,)), ((), ())), preferred_element_type=jnp.float32
    )


def rms_parts(value, axis=-1):
    inverse = lax.rsqrt(jnp.mean(value * value, axis=axis, keepdims=True) + EPS)
    return (value * inverse, inverse)


def rms_back(normed, inverse, grad, axis=-1):
    return inverse * (grad - normed * jnp.mean(grad * normed, axis=axis, keepdims=True))


def rope_tables(rows, columns):
    quarter = HEAD // 4
    frequency = THETA ** (-jnp.arange(quarter, dtype=jnp.float32) / quarter)
    angles = jnp.concatenate(
        [
            frequency[:, None] * rows.astype(jnp.float32)[None, :],
            frequency[:, None] * columns.astype(jnp.float32)[None, :],
        ],
        axis=0,
    )
    return (jnp.cos(angles), jnp.sin(angles))


def gate_kernel(value, after, out):
    del value, after, out


def gate(value, after):
    anywhere = pl.BlockSpec(memory_space=pl.ANY)
    return pl.pallas_call(
        gate_kernel,
        out_shape=jax.ShapeDtypeStruct(value.shape, value.dtype),
        in_specs=[anywhere, anywhere],
        out_specs=anywhere,
        input_output_aliases={0: 0},
        name="gate",
    )(value, after)


def near_swap(value):
    return lax.ppermute(value, "dp", [(i, i ^ 1) for i in range(lax.axis_size("dp"))])


def far_groups():
    count = lax.axis_size("dp")
    return [list(range(near, count, 2)) for near in range(2)]


def near_pair(value, other):
    odd = lax.axis_index("dp") % 2
    return jnp.concatenate(
        [jnp.where(odd == 0, value, other), jnp.where(odd == 0, other, value)], axis=0
    )


def gather_far(value):
    return lax.all_gather(value, "dp", axis=0, tiled=True, axis_index_groups=far_groups())


def join_near(line, other, rows, start=0, stop=None):
    odd = lax.axis_index("dp") % 2
    line = line[:, start:stop]
    other = other[:, start:stop]
    columns = line.shape[1]
    line = line.reshape(-1, rows, columns)
    other = other.reshape(-1, rows, columns)
    both = jnp.stack(
        [jnp.where(odd == 0, line, other), jnp.where(odd == 0, other, line)], axis=1
    )
    return both.reshape(-1, columns)


def swap_half(parts):
    odd = lax.axis_index("dp") % 2
    send = lax.dynamic_index_in_dim(parts, 1 - odd, 1, keepdims=False)
    return near_swap(send.reshape(-1, send.shape[2])).reshape(send.shape)


def scatter_far(parts, others):
    odd = lax.axis_index("dp") % 2
    summed = [
        half(
            lax.dynamic_index_in_dim(part, odd, 1, keepdims=False).astype(jnp.float32)
            + other.astype(jnp.float32)
        )
        for part, other in zip(parts, others)
    ]
    summed = jnp.concatenate(summed, axis=2)
    return lax.psum_scatter(
        summed.reshape(-1, summed.shape[2]),
        "dp",
        scatter_dimension=0,
        tiled=True,
        axis_index_groups=far_groups(),
    )


def swap_tensor(value, bits):
    return lax.ppermute(value, "tensor", [(i, i ^ bits) for i in range(lax.axis_size("tensor"))])


def owner(place):
    if lax.axis_size("tensor") == 4:
        return lax.axis_index("tensor") ^ place
    return jnp.int32(place)


def spread(value):
    count = lax.axis_size("tensor")
    if count == 4:
        near = swap_tensor(value, 1)
        far = swap_tensor(value, 2)
        return [value, near, far, swap_tensor(far, 1)]
    whole = lax.all_gather(value, "tensor", axis=0, tiled=False)
    return [whole[i] for i in range(count)]


def collect_near(parts):
    if len(parts) == 4:
        rows = parts[0].shape[0]
        sent = swap_tensor(half(jnp.concatenate([parts[3], parts[1]], axis=0)), 1)
        sent = sent.astype(jnp.float32)
        return (parts[0] + sent[rows:], half(parts[2] + sent[:rows]))
    return (half(jnp.concatenate(parts, axis=0)),)


def collect_far(sums):
    if len(sums) == 2:
        return sums[0] + swap_tensor(sums[1], 2).astype(jnp.float32)
    return lax.psum_scatter(
        sums[0], "tensor", scatter_dimension=0, tiled=True
    ).astype(jnp.float32)


def collect(parts):
    return collect_far(collect_near(parts))


def in_place(blocks):
    if len(blocks) == 4:
        stacked = jnp.stack(blocks)
        mine = lax.axis_index("tensor")
        blocks = [
            lax.dynamic_index_in_dim(stacked, mine ^ i, 0, keepdims=False)
            for i in range(len(blocks))
        ]
    return jnp.concatenate(blocks, axis=0)


def dp_neighbour():
    mine = lax.axis_index("dp")
    return mine + 1 - 2 * (mine % 2)


def meet(everyone, carries):
    barrier = pltpu.get_barrier_semaphore()
    if everyone:
        others = [
            {axis: (lax.axis_index(axis) + step) % lax.axis_size(axis)}
            for axis in ("dp", "tensor")
            for step in range(1, lax.axis_size(axis))
        ]
    else:
        _, near, far, _ = row_peers()
        others = [{"tensor": near}, {"tensor": far}]
        if carries:
            others.append({"dp": dp_neighbour()})
    for other in others:
        pl.semaphore_signal(barrier, inc=1, device_id=other, device_id_type=MESH)
    pl.semaphore_wait(barrier, len(others))


def remote_call(
    kernel, name, number, operands, outs, scratch, carry=(), everyone=False, after=()
):
    copies = sum(1 if len(array.shape) == 2 else array.shape[0] for array in carry)
    swapped = [
        jax.ShapeDtypeStruct(
            array.shape if len(array.shape) == 2 else (array.shape[0], *array.shape[2:]),
            array.dtype,
        )
        for array in carry
    ]

    def run(*refs):
        refs = list(refs)
        ins = [refs.pop(0) for _ in operands]
        sources = [refs.pop(0) for _ in carry]
        del refs[: len(after)]
        results = [refs.pop(0) for _ in outs]
        targets = [refs.pop(0) for _ in carry]
        meet(everyone, bool(carry))
        started = []
        if carry:
            sems = refs.pop()
            other = dp_neighbour()
            pairs = []
            for source, target in zip(sources, targets):
                if len(source.shape) == 2:
                    pairs.append((source, target))
                else:
                    pairs += [
                        (source.at[i, other % 2], target.at[i]) for i in range(source.shape[0])
                    ]
            for i, (source, target) in enumerate(pairs):
                copy = pltpu.make_async_remote_copy(
                    src_ref=source,
                    dst_ref=target,
                    send_sem=sems.at[0, i],
                    recv_sem=sems.at[1, i],
                    device_id={"dp": other},
                    device_id_type=MESH,
                )
                copy.start()
                started.append(copy)
        kernel(*ins, *results, *refs)
        for copy in started:
            copy.wait()

    whole = pl.BlockSpec(memory_space=pltpu.VMEM)
    anywhere = pl.BlockSpec(memory_space=pl.ANY)
    return pl.pallas_call(
        run,
        out_shape=[*outs, *swapped],
        in_specs=[whole] * len(operands) + [anywhere] * (len(carry) + len(after)),
        out_specs=[whole] * len(outs) + [anywhere] * len(carry),
        scratch_shapes=[
            *scratch,
            *([pltpu.SemaphoreType.DMA((2, copies))] if carry else []),
        ],
        compiler_params=pltpu.CompilerParams(
            collective_id=number, has_side_effects=True, vmem_limit_bytes=60 * 1024 * 1024
        ),
        name=name,
    )(*operands, *carry, *after)


def send_blocks(axis, pick, target, send_sem, recv_sem):
    count = lax.axis_size(axis)
    mine = lax.axis_index(axis)

    def copy(other, place):
        return pltpu.make_async_remote_copy(
            src_ref=pick(other),
            dst_ref=target.at[place],
            send_sem=send_sem.at[other],
            recv_sem=recv_sem.at[place],
            device_id={axis: other},
            device_id_type=MESH,
        )

    others = [(mine + step) % count for step in range(1, count)]
    for other in others:
        copy(other, mine).start()
    for other in others:
        copy(other, mine).wait_send()
        copy(other, other).wait_recv()


def spread_kernel(source, target, middle, send_dp, recv_dp, send_tensor, recv_tensor):
    mine = lax.axis_index("dp")
    middle[mine] = source[mine]
    send_blocks("dp", lambda other: source.at[other], middle, send_dp, recv_dp)
    target[lax.axis_index("tensor")] = middle[...]
    send_blocks("tensor", lambda other: middle, target, send_tensor, recv_tensor)


def return_kernel(
    source, target, middle, summed, last, send_dp, recv_dp, send_tensor, recv_tensor
):
    place = lax.axis_index("tensor")
    middle[place] = source[place]
    send_blocks("tensor", lambda other: source.at[other], middle, send_tensor, recv_tensor)
    total = middle[0]
    for other in range(1, lax.axis_size("tensor")):
        total += middle[other]
    summed[...] = total
    mine = lax.axis_index("dp")
    last[mine] = summed[mine]
    send_blocks("dp", lambda other: summed.at[other], last, send_dp, recv_dp)
    target[...] = last[...]


def total_kernel(source, target, near, far, part, send_dp, recv_dp, send_tensor, recv_tensor):
    near[lax.axis_index("tensor")] = source[...]
    send_blocks("tensor", lambda other: source, near, send_tensor, recv_tensor)
    part[...] = jnp.sum(near[...], axis=0)
    far[lax.axis_index("dp")] = part[...]
    send_blocks("dp", lambda other: part, far, send_dp, recv_dp)
    target[...] = jnp.sum(far[...], axis=0)


def exchange_scratch(shapes):
    sizes = (lax.axis_size("dp"),) * 2 + (lax.axis_size("tensor"),) * 2
    return [pltpu.VMEM(shape, jnp.float32) for shape in shapes] + [
        pltpu.SemaphoreType.DMA((size,)) for size in sizes
    ]


CHUNKS = 4


def row_peers():
    mine = lax.axis_index("tensor")
    near = mine + 1 - 2 * (mine % 2)
    return (mine, near, (mine + 2) % 4, (near + 2) % 4)


def remote(source, target, sems, index, other):
    return pltpu.make_async_remote_copy(
        src_ref=source,
        dst_ref=target,
        send_sem=sems.at[0, index],
        recv_sem=sems.at[1, index],
        device_id={"tensor": other},
        device_id_type=MESH,
    )


def chunk_rows(total):
    size = total // CHUNKS
    return [slice(i * size, (i + 1) * size) for i in range(CHUNKS)]


def sum_blocks(partial, finish, work, sems):
    mine, near, far, both = row_peers()
    send_both, send_near, near_both, near_own, send_far, far_own, base = work
    chunks = chunk_rows(base.shape[0])

    def keep(columns, value):
        base[:, columns] = value

    def to_both(columns, value):
        send_both[:, columns] = half(value)

    def to_near(columns, value):
        send_near[:, columns] = half(value)

    partial(both, to_both)
    first = remote(send_both, near_both, sems, 0, near)
    first.start()
    partial(far, keep)
    first.wait()
    across = []
    for i, rows in enumerate(chunks):
        send_far[rows, :] = half(base[rows, :] + near_both[rows, :].astype(jnp.float32))
        across.append(remote(send_far.at[rows], far_own.at[rows], sems, 2 + i, far))
        across[i].start()
    partial(near, to_near)
    second = remote(send_near, near_own, sems, 1, near)
    second.start()
    partial(mine, keep)
    second.wait()
    for i, rows in enumerate(chunks):
        across[i].wait()
        finish(
            rows,
            base[rows, :]
            + near_own[rows, :].astype(jnp.float32)
            + far_own[rows, :].astype(jnp.float32),
        )


def sum_scratch(rows, columns):
    narrow = pltpu.VMEM((rows, columns), jnp.bfloat16)
    return [narrow] * 6 + [pltpu.VMEM((rows, columns), jnp.float32)]


class Spread:
    def __init__(self, gathered, sems, base):
        self.gathered, self.sems, self.base = gathered, sems, base
        self.mine, self.near, self.far, self.both = row_peers()
        self.chunks = chunk_rows(gathered.shape[1])
        self.started = []

    def copy(self, block, i, kind, other):
        part = self.gathered.at[block, self.chunks[i]]
        return remote(part, part, self.sems, self.base + CHUNKS * kind + i, other)

    def offer(self, i, value):
        self.gathered[self.mine, self.chunks[i], :] = value
        for kind, other in ((0, self.far), (1, self.near)):
            copy = self.copy(self.mine, i, kind, other)
            copy.start()
            self.started.append(copy)

    def settle(self):
        for i in range(CHUNKS):
            self.copy(self.far, i, 0, self.far).wait_recv()
            forward = self.copy(self.far, i, 2, self.near)
            forward.start()
            self.started.append(forward)
        for i in range(CHUNKS):
            self.copy(self.near, i, 1, self.near).wait_recv()
            self.copy(self.both, i, 2, self.near).wait_recv()
        for copy in self.started:
            copy.wait_send()


def tiles_of(total, size):
    def run(step):
        def body(index, carry):
            step(pl.ds(pl.multiple_of(index * size, size), size))
            return carry

        lax.fori_loop(0, total // size, body, 0)

    return run


def enter_kernel(latents, scale, gain, gathered, sems):
    share = Spread(gathered, sems, 0)
    for i, rows in enumerate(share.chunks):
        share.offer(i, enter_point(latents[rows, :].astype(jnp.float32), scale[rows, :], gain[0:1]))
    share.settle()


def project_kernel(weight, captions, total, *rest):
    work, sems = rest[:-1], rest[-1]
    local = total.shape[0]

    def partial(block, store):
        rows = pl.ds(pl.multiple_of(block * local, local), local)

        @tiles_of(captions.shape[0], 512)
        def _(columns):
            store(columns, dot(weight[rows, :], captions[columns, :], 1, 1))

    def finish(rows, value):
        total[rows, :] = value

    sum_blocks(partial, finish, work, sems)


def attention_out_kernel(
    mixed, weight, latents, gate, scale, gain, summed, middle, gathered, *rest
):
    lhs, work, sems = rest[0], rest[1:-1], rest[-1]
    size = latents.shape[0]

    def partial(block, store):
        own = pl.ds(pl.multiple_of(block * size, size), size)
        lhs[...] = mixed[:, own].astype(jnp.float32).T.astype(jnp.bfloat16)

        @tiles_of(weight.shape[0], 512)
        def _(columns):
            store(columns, dot(lhs[...], weight[columns, :], 1, 1))

    share = Spread(gathered, sems, 2 + CHUNKS)

    def finish(rows, value):
        summed[rows, :] = value
        middle[rows, :], out = middle_point(
            value,
            latents[rows, :].astype(jnp.float32),
            gate[rows, :],
            scale[rows, :],
            gain[1:2],
            gain[2:3],
        )
        share.offer(share.chunks.index(rows), out)

    sum_blocks(partial, finish, work, sems)
    share.settle()


def feed_kernel(
    inputs, feed, down, middle, gate, cotangent, gain, gate_up, hidden, summed, out, gathered, *rest
):
    work, sems = rest[:-1], rest[-1]
    size = middle.shape[0]
    units = hidden.shape[1]

    def partial(block, store):
        own = pl.ds(pl.multiple_of(block * size, size), size)

        @tiles_of(units, 256)
        def _(columns):
            start = pl.multiple_of(columns.start + units, 256)
            first = dot(inputs[own, :], feed[:, columns], 1, 0)
            second = dot(inputs[own, :], feed[:, pl.ds(start, 256)], 1, 0)
            gate_up[own, columns] = first
            gate_up[own, pl.ds(start, 256)] = second
            hidden[own, columns] = half(first * jax.nn.sigmoid(first) * second)

        @tiles_of(down.shape[0], 512)
        def _(columns):
            store(columns, dot(hidden[own, :], down[columns, :], 1, 1))

    share = Spread(gathered, sems, 2 + CHUNKS)

    def finish(rows, value):
        summed[rows, :] = value
        out[rows, :], back = end_point(
            value, middle[rows, :], gate[rows, :], cotangent[rows, :], gain[3:4]
        )
        share.offer(share.chunks.index(rows), back)

    sum_blocks(partial, finish, work, sems)
    share.settle()


def feed_back_kernel(
    back, gate_up, feed, down, summed, middle, gate, scale, cotangent, gain,
    pair, input_grad, middle_grad, gathered, *rest
):
    work, sems = rest[:-1], rest[-1]
    size = middle.shape[0]
    units = down.shape[1]

    def partial(block, store):
        own = pl.ds(pl.multiple_of(block * size, size), size)

        @tiles_of(units, 256)
        def _(columns):
            other = pl.ds(pl.multiple_of(columns.start + units, 256), 256)
            grad = dot(back[own, :], down[:, columns], 1, 0)
            first, second = gate_up[own, columns], gate_up[own, other]
            pair[own, columns], pair[own, other] = pair_point(grad, first, second)

        @tiles_of(feed.shape[0], 256)
        def _(columns):
            store(columns, dot(pair[own, :], feed[columns, :], 1, 1))

    share = Spread(gathered, sems, 2 + CHUNKS)

    def finish(rows, value):
        input_grad[rows, :] = value
        middle_grad[rows, :], out = middle_back_point(
            value,
            summed[rows, :],
            middle[rows, :],
            gate[rows, :],
            scale[rows, :],
            cotangent[rows, :],
            gain[1:2],
            gain[2:3],
        )
        share.offer(share.chunks.index(rows), out)

    sum_blocks(partial, finish, work, sems)
    share.settle()


def text_kernel(own, captions, grad, gathered, *rest):
    (sems,) = rest
    mine, near, far, both = row_peers()
    share = Spread(gathered, sems, 0)
    local = own.shape[0]
    size = local // CHUNKS

    def work(block, i):
        rows = pl.ds(pl.multiple_of(block * local + i * size, 16), size)
        grad[rows, :] = half(dot(gathered[block, share.chunks[i], :], captions[...], 1, 0))

    for i, rows in enumerate(share.chunks):
        share.offer(i, own[rows, :])
    for i in range(CHUNKS):
        work(mine, i)
    for i in range(CHUNKS):
        share.copy(near, i, 1, near).wait_recv()
        work(near, i)
    for i in range(CHUNKS):
        share.copy(far, i, 0, far).wait_recv()
        forward = share.copy(far, i, 2, near)
        forward.start()
        share.started.append(forward)
        work(far, i)
        if i:
            share.copy(both, i - 1, 2, near).wait_recv()
            work(both, i - 1)
    share.copy(both, CHUNKS - 1, 2, near).wait_recv()
    work(both, CHUNKS - 1)
    for copy in share.started:
        copy.wait_send()


def enter_back_kernel(triple, weight, total, *rest):
    lhs, work, sems = rest[0], rest[1:-1], rest[-1]
    size = total.shape[0]

    def partial(block, store):
        own = pl.ds(pl.multiple_of(block * size, size), size)
        lhs[...] = triple[:, own].astype(jnp.float32).T.astype(jnp.bfloat16)

        @tiles_of(weight.shape[0], 512)
        def _(columns):
            store(columns, dot(lhs[...], weight[columns, :], 1, 1))

    def finish(rows, value):
        total[rows, :] = value

    sum_blocks(partial, finish, work, sems)


def enter_point(source, scale, gain):
    normed, _ = rms_parts(source)
    return half(normed * gain * (1.0 + scale))


def middle_point(summed, source, gate, scale, first_gain, second_gain):
    normed, _ = rms_parts(summed)
    middle = source + jnp.tanh(gate) * (normed * first_gain)
    return (middle, enter_point(middle, scale, second_gain))


def end_point(summed, middle, gate, cotangent, gain):
    normed, inverse = rms_parts(summed)
    turned = jnp.tanh(gate)
    out = middle + turned * (normed * gain)
    return (out, half(rms_back(normed, inverse, turned * cotangent * gain)))


def pair_point(grad, first, second):
    sigmoid = jax.nn.sigmoid(first)
    return (
        half(grad * second * (sigmoid + first * sigmoid * (1.0 - sigmoid))),
        half(grad * (first * sigmoid)),
    )


def middle_back_point(
    input_grad, summed, middle, gate, scale, cotangent, first_gain, second_gain
):
    normed, inverse = rms_parts(middle)
    middle_grad = cotangent + rms_back(
        normed, inverse, input_grad * second_gain * (1.0 + scale)
    )
    normed, inverse = rms_parts(summed)
    back = jnp.tanh(gate) * middle_grad * first_gain
    return (middle_grad, half(rms_back(normed, inverse, back)))


def spans(heads):
    return [slice(head * HEAD, (head + 1) * HEAD) for head in range(heads)]


def head_norm(value):
    inverse = lax.rsqrt(jnp.mean(value * value, axis=0, keepdims=True) + EPS)
    return (value * inverse, inverse)


def head_back(normed, inverse, grad):
    return inverse * (grad - normed * jnp.mean(grad * normed, axis=0, keepdims=True))


def turn(value, cosine, sine):
    middle = HEAD // 2
    first, second = value[:middle], value[middle:]
    return jnp.concatenate(
        [first * cosine - second * sine, second * cosine + first * sine], axis=0
    )


def score_block(keys, query, bias):
    return jnp.exp2(dot(keys, query, 1, 0) * (HEAD ** (-0.5) * LOG2E) + bias)


def self_bias(step, ids_row, ids_column):
    start = pl.multiple_of(step * TILE, TILE)
    return jnp.where(ids_column[pl.ds(start, TILE), :] == ids_row[...], 0.0, NEG)


def cross_bias(step, ids_row, lengths):
    slots = lax.broadcasted_iota(jnp.int32, (TILE, 1), 0) < lengths[step]
    return jnp.where(slots & (ids_row[...] == step), 0.0, NEG)


def attend_tile(heads, meta, bias_of, query, key_rows, value, out, total, inv_ref):
    base = 2 * pl.program_id(0)
    out[...] = jnp.zeros_like(out)
    total[...] = jnp.zeros_like(total)

    def step(index, carry):
        bias = bias_of(index)
        rows = pl.ds(pl.multiple_of(index * TILE, TILE), TILE)
        for head, span in enumerate(spans(heads)):
            expo = score_block(key_rows[head, rows, :], query[span, :], bias)
            total[head] += jnp.sum(expo.reshape(TILE // 8, 8, TILE), axis=0)
            out[span, :] += dot(value[span, rows], half(expo), 1, 0)
        return carry

    lax.fori_loop(meta[base], meta[base + 1], step, 0)
    for head, span in enumerate(spans(heads)):
        inverse = 1.0 / jnp.sum(total[head], axis=0, keepdims=True)
        inv_ref[head] = jnp.broadcast_to(inverse, (8, TILE))
        out[span, :] = out[span, :] * inverse


def attend_back_tile(
    heads, meta, bias_of, query, key_rows, key, value_rows, inv_ref, out, back, dq, dk, dv, centre
):
    base = 2 * pl.program_id(0)
    scale = HEAD ** (-0.5)
    dq[...] = jnp.zeros_like(dq)
    for head, span in enumerate(spans(heads)):
        both = out[span, :] * back[span, :].astype(jnp.float32)
        centre[head] = jnp.broadcast_to(jnp.sum(both, axis=0, keepdims=True), (8, TILE))

    def step(index, carry):
        bias = bias_of(index)
        rows = pl.ds(pl.multiple_of(index * TILE, TILE), TILE)
        for head, span in enumerate(spans(heads)):
            probs = score_block(key_rows[head, rows, :], query[span, :], bias)
            probs = probs * inv_ref[head, 0:1, :]
            prob_grad = dot(value_rows[head, rows, :], back[span, :], 1, 0)
            score_grad = half(probs * (prob_grad - centre[head, 0:1, :]))
            dv[span, rows] += dot(back[span, :], half(probs), 1, 1)
            dk[span, rows] += dot(query[span, :], score_grad, 1, 1) * scale
            dq[span, :] += dot(key[span, rows], score_grad, 1, 0) * scale
        return carry

    lax.fori_loop(meta[base], meta[base + 1], step, 0)


def self_forward_kernel(
    heads,
    meta,
    ids_row,
    ids_column,
    gain,
    cosine,
    sine,
    cosine_all,
    sine_all,
    raw_query,
    raw_rest,
    query,
    key,
    key_rows,
    value_rows,
    out,
    inv_ref,
    value,
    total,
):
    local = heads * HEAD

    @pl.when(pl.program_id(0) == 0)
    def _():
        for head, span in enumerate(spans(heads)):
            normed, _ = head_norm(raw_rest[span, :])
            turned = turn(normed * gain[span, 1:2], cosine_all[...], sine_all[...])
            key[span, :] = half(turned)
            key_rows[head] = half(turned.T)
            plain = raw_rest[local + head * HEAD : local + (head + 1) * HEAD, :]
            value[span, :] = half(plain)
            value_rows[head] = half(plain.T)

    for span in spans(heads):
        normed, _ = head_norm(raw_query[span, :])
        query[span, :] = half(turn(normed * gain[span, 0:1], cosine[...], sine[...]))
    attend_tile(
        heads,
        meta,
        lambda index: self_bias(index, ids_row, ids_column),
        query,
        key_rows,
        value,
        out,
        total,
        inv_ref,
    )


def cross_forward_kernel(
    heads,
    meta,
    lengths,
    ids_row,
    gain,
    query,
    own_out,
    raw_key,
    raw_value,
    key,
    key_rows,
    value_rows,
    out,
    inv_ref,
    mixed,
    value,
    total,
):
    @pl.when(pl.program_id(0) == 0)
    def _():
        for head, span in enumerate(spans(heads)):
            normed, _ = head_norm(raw_key[span, :])
            normed = normed * gain[span, 2:3]
            key[span, :] = half(normed)
            key_rows[head] = half(normed.T)
            plain = raw_value[span, :]
            value[span, :] = half(plain)
            value_rows[head] = half(plain.T)

    attend_tile(
        heads,
        meta,
        lambda index: cross_bias(index, ids_row, lengths),
        query,
        key_rows,
        value,
        out,
        total,
        inv_ref,
    )
    mixed[...] = half(own_out[...] + jnp.tanh(gain[:, 3:4]) * out[...])


def cross_backward_kernel(
    heads,
    meta,
    lengths,
    ids_row,
    gain,
    query,
    key_rows,
    key,
    value_rows,
    inv_ref,
    out,
    mixed_grad,
    raw_key,
    dq,
    dk,
    dv,
    gain_grad,
    back,
    centre,
    dk_sum,
    dv_sum,
    gate_sum,
):
    place = pl.program_id(0)

    @pl.when(place == 0)
    def _():
        dk_sum[...] = jnp.zeros_like(dk_sum)
        dv_sum[...] = jnp.zeros_like(dv_sum)
        gate_sum[...] = jnp.zeros_like(gate_sum)

    gate = jnp.tanh(gain[:, 3:4])
    back[...] = half(gate * mixed_grad[...])
    gate_sum[...] += mixed_grad[...] * out[...]
    attend_back_tile(
        heads,
        meta,
        lambda index: cross_bias(index, ids_row, lengths),
        query,
        key_rows,
        key,
        value_rows,
        inv_ref,
        out,
        back,
        dq,
        dk_sum,
        dv_sum,
        centre,
    )

    @pl.when(place == pl.num_programs(0) - 1)
    def _():
        dv[...] = half(dv_sum[...])
        gate_grad = jnp.sum(gate_sum[...], axis=1, keepdims=True) * (1.0 - gate * gate)
        gain_grad[:, 0:128] = jnp.broadcast_to(gate_grad, (heads * HEAD, 128))
        for span in spans(heads):
            normed, inverse = head_norm(raw_key[span, :])
            grad = dk_sum[span, :]
            summed = jnp.sum(grad * normed, axis=1, keepdims=True)
            gain_grad[span, 128:256] = jnp.broadcast_to(summed, (HEAD, 128))
            dk[span, :] = half(head_back(normed, inverse, grad * gain[span, 2:3]))


def self_backward_kernel(
    heads,
    meta,
    ids_row,
    ids_column,
    gain,
    cosine,
    sine,
    cosine_all,
    sine_all,
    query,
    key_rows,
    key,
    value_rows,
    inv_ref,
    out,
    mixed_grad,
    other_dq,
    raw_query,
    raw_key,
    triple,
    gain_grad,
    back,
    centre,
    dq,
    dk_sum,
    dv_sum,
    query_sum,
):
    place = pl.program_id(0)
    local = heads * HEAD

    @pl.when(place == 0)
    def _():
        dk_sum[...] = jnp.zeros_like(dk_sum)
        dv_sum[...] = jnp.zeros_like(dv_sum)
        query_sum[...] = jnp.zeros_like(query_sum)

    back[...] = half(mixed_grad[...])
    attend_back_tile(
        heads,
        meta,
        lambda index: self_bias(index, ids_row, ids_column),
        query,
        key_rows,
        key,
        value_rows,
        inv_ref,
        out,
        back,
        dq,
        dk_sum,
        dv_sum,
        centre,
    )
    columns = pl.ds(pl.multiple_of(place * TILE, TILE), TILE)
    for span in spans(heads):
        normed, inverse = head_norm(raw_query[span, :])
        grad = turn(dq[span, :] + other_dq[span, :], cosine[...], -sine[...])
        query_sum[span, :] += grad * normed
        triple[span, columns] = half(head_back(normed, inverse, grad * gain[span, 0:1]))

    @pl.when(place == pl.num_programs(0) - 1)
    def _():
        summed = jnp.sum(query_sum[...], axis=1, keepdims=True)
        gain_grad[:, 0:128] = jnp.broadcast_to(summed, (local, 128))
        triple[2 * local :, :] = half(dv_sum[...])
        for head, span in enumerate(spans(heads)):
            normed, inverse = head_norm(raw_key[span, :])
            grad = turn(dk_sum[span, :], cosine_all[...], -sine_all[...])
            summed = jnp.sum(grad * normed, axis=1, keepdims=True)
            gain_grad[span, 128:256] = jnp.broadcast_to(summed, (HEAD, 128))
            triple[local + head * HEAD : local + (head + 1) * HEAD, :] = half(
                head_back(normed, inverse, grad * gain[span, 1:2])
            )


def attention_call(kernel, name, scalars, operands, outs, scratch, tokens, weight, after=()):
    def block(array, tiled):
        lead = array.shape[:-1]
        if tiled:
            return pl.BlockSpec((*lead, TILE), lambda i, *_: (*([0] * len(lead)), i))
        return pl.BlockSpec(array.shape, lambda i, *_: (0,) * len(array.shape))

    count = len(scalars) + len(operands)

    def run(*refs):
        kernel(*refs[:count], *refs[count + len(after) :])

    return pl.pallas_call(
        run,
        grid_spec=pltpu.PrefetchScalarGridSpec(
            num_scalar_prefetch=len(scalars),
            grid=(tokens // TILE,),
            in_specs=[block(*operand) for operand in operands]
            + [pl.BlockSpec(memory_space=pl.ANY)] * len(after),
            out_specs=[block(*out) for out in outs],
            scratch_shapes=scratch,
        ),
        out_shape=[out for out, _ in outs],
        compiler_params=pltpu.CompilerParams(
            vmem_limit_bytes=58 * 1024 * 1024, dimension_semantics=("arbitrary",)
        ),
        cost_estimate=pl.CostEstimate(
            flops=weight, bytes_accessed=weight, transcendentals=0
        ),
        name=name,
    )(*scalars, *(operand for operand, _ in operands), *after)


def adamw(grad, weight, moment, square, decay, rate):
    moment_new = BETA1 * moment + (1.0 - BETA1) * grad
    square_new = BETA2 * square + (1.0 - BETA2) * grad * grad
    step_size = (
        moment_new / (1.0 - BETA1**STEP) / (jnp.sqrt(square_new / (1.0 - BETA2**STEP)) + ADAM_EPS)
    )
    return (moment_new, square_new, weight - rate * (step_size + decay * weight))


def body(
    latents,
    cotangent,
    captions,
    conditions,
    image_ids,
    rope_rows,
    rope_cols,
    caption_lengths,
    attention_in,
    attention_out,
    feed_in,
    feed_out,
    caption_in,
    modulator,
    channels,
    moment_attention_in,
    square_attention_in,
    moment_attention_out,
    square_attention_out,
    moment_feed_in,
    square_feed_in,
    moment_feed_out,
    square_feed_out,
    moment_caption_in,
    square_caption_in,
    moment_modulator,
    square_modulator,
    moment_channels,
    square_channels,
):
    tensor_size = lax.axis_size("tensor")
    tensor_index = lax.axis_index("tensor")
    dp_size = lax.axis_size("dp")
    dp_index = lax.axis_index("dp")
    shard_rows, width = latents.shape
    local = attention_in.shape[2]
    heads = local // HEAD
    units = feed_in.shape[2]
    segment = image_ids[0]
    row_tokens = segment.shape[0]
    images = conditions.shape[0]
    per_row = caption_lengths.shape[1]
    lengths = caption_lengths[0]
    slots = captions.shape[0]
    offset = tensor_index * local
    own_ids = lax.dynamic_slice_in_dim(segment, tensor_index * shard_rows, shard_rows)

    rows = attention_in.shape[1]
    fused = tensor_size == 4
    caption_half = half(caption_in)
    key_line = gather_far(caption_half[0].T)
    value_line = gather_far(caption_half[1].T)
    in_half = half(attention_in)
    attention_line = gather_far(
        jnp.concatenate([in_half[0], in_half[1], in_half[2], half(attention_out).T], axis=1)
    )
    down_line = gather_far(half(feed_out).T)
    feed_half = half(feed_in)
    feed_own = jnp.concatenate([feed_half[0], feed_half[1]], axis=1)

    augmented = half(
        jnp.concatenate([jax.nn.silu(conditions), jnp.ones((images, 1), jnp.float32)], axis=1)
    )
    factor_part = jnp.dot(augmented, half(modulator), preferred_element_type=jnp.float32)
    own_columns = factor_part.shape[1]
    payload = jnp.concatenate(
        [
            factor_part.reshape(dp_size, per_row, own_columns),
            jnp.broadcast_to(
                lax.reduce_precision(channels, 8, 7).reshape(-1, own_columns),
                (dp_size, channels.size // own_columns, own_columns),
            ),
        ],
        axis=1,
    )
    received, feed_other = remote_call(
        spread_kernel,
        "modulation_exchange",
        0,
        [payload],
        [jax.ShapeDtypeStruct((tensor_size, *payload.shape), jnp.float32)],
        exchange_scratch([payload.shape]),
        [feed_own],
        everyone=True,
    )
    feed_full = gather_far(near_pair(feed_own, feed_other))
    factor_row = jnp.transpose(received[:, :, :per_row], (2, 1, 0, 3)).reshape(per_row, -1)
    gains = received[0, :, per_row:].reshape(dp_size, 8, -1)
    gains = jnp.transpose(gains, (1, 0, 2)).reshape(8, width)
    local_gains = lax.dynamic_slice_in_dim(gains[4:], offset, local, 1).T
    chooser = (own_ids[:, None] == jnp.arange(per_row, dtype=jnp.int32)[None, :]).astype(
        jnp.float32
    )
    token_factor = jnp.dot(chooser, factor_row, precision=HIGH)
    scale_attn = token_factor[:, :width]
    gate_attn = token_factor[:, width : 2 * width]
    scale_feed = token_factor[:, 2 * width : 3 * width]
    gate_feed = token_factor[:, 3 * width :]

    def split(value):
        return [value[i * shard_rows : (i + 1) * shard_rows] for i in range(tensor_size)]

    f32, bf16 = jnp.float32, jnp.bfloat16

    def shape(dims, dtype=f32):
        return jax.ShapeDtypeStruct(dims, dtype)

    gathered = shape((tensor_size, shard_rows, width), bf16)
    in_kernel = sum_scratch(shard_rows, width)

    def semaphores(count):
        return pltpu.SemaphoreType.DMA((2, count))

    sum_sems, all_sems = semaphores(2 + CHUNKS), semaphores(2 + 4 * CHUNKS)
    source = latents.astype(f32)
    attn_norm, attn_inv = rms_parts(source)

    def caption_project(weight, carry, number):
        if fused:
            return remote_call(
                project_kernel,
                "project",
                number,
                [weight, captions],
                [shape((local, slots))],
                [*sum_scratch(local, slots), sum_sems],
                [carry],
            )
        total = collect(
            [
                dot(
                    lax.dynamic_slice_in_dim(weight, owner(i) * local, local), captions, 1, 1
                )
                for i in range(tensor_size)
            ]
        )
        return (total, near_swap(carry))

    if fused:
        attn_full, key_other = remote_call(
            enter_kernel,
            "enter",
            3,
            [latents, scale_attn, gains],
            [gathered],
            [semaphores(3 * CHUNKS)],
            [key_line],
        )
        attn_full = attn_full.reshape(row_tokens, width)
    else:
        attn_full = in_place(spread(enter_point(source, scale_attn, gains[0])))
        key_other = near_swap(key_line)
    text_key_raw, value_other = caption_project(
        join_near(key_line, key_other, rows), value_line, 4
    )
    text_value_raw, attention_other = caption_project(
        join_near(value_line, value_other, rows), attention_line, 11
    )
    in_full = join_near(attention_line, attention_other, rows, 0, 3 * local)
    out_full = join_near(attention_line, attention_other, rows, 3 * local)
    projected = dot(in_full, attn_full, 0, 1)
    raw_query, raw_rest = projected[:local], projected[local:]
    cosine, sine = rope_tables(rope_rows[0], rope_cols[0])

    tiles = row_tokens // TILE
    first_id = segment.reshape(tiles, TILE)[:, 0]
    last_id = segment.reshape(tiles, TILE)[:, TILE - 1]
    low = jnp.sum((segment[None] < first_id[:, None]).astype(jnp.int32), axis=1) // TILE
    high = (
        jnp.sum((segment[None] <= last_id[:, None]).astype(jnp.int32), axis=1) + TILE - 1
    ) // TILE
    self_meta = jnp.stack([low, high], axis=1).reshape(-1)
    cross_meta = jnp.stack([first_id, last_id + 1], axis=1).reshape(-1)
    ids_row = image_ids
    ids_column = segment[:, None]
    wide = jax.ShapeDtypeStruct((local, row_tokens), jnp.float32)
    narrow = jax.ShapeDtypeStruct((local, row_tokens), jnp.bfloat16)
    sums = jax.ShapeDtypeStruct((heads, 8, row_tokens), jnp.float32)
    by_rows = jax.ShapeDtypeStruct((heads, row_tokens, HEAD), jnp.bfloat16)
    text_narrow = jax.ShapeDtypeStruct((local, slots), jnp.bfloat16)
    text_rows = jax.ShapeDtypeStruct((heads, slots, HEAD), jnp.bfloat16)
    gain_shape = jax.ShapeDtypeStruct((local, 256), jnp.float32)
    tile_sums = pltpu.VMEM((heads, 8, TILE), jnp.float32)
    tables = [(cosine, True), (sine, True), (cosine, False), (sine, False)]
    queries, keys, key_rows, value_rows, own_out, own_inv = attention_call(
        functools.partial(self_forward_kernel, heads),
        "self_forward",
        [self_meta],
        [
            (ids_row, True),
            (ids_column, False),
            (local_gains, False),
            *tables,
            (raw_query, True),
            (raw_rest, False),
        ],
        [
            (narrow, True),
            (narrow, False),
            (by_rows, False),
            (by_rows, False),
            (wide, True),
            (sums, True),
        ],
        [pltpu.VMEM((local, row_tokens), jnp.bfloat16), tile_sums],
        row_tokens,
        15000,
    )
    text_keys, text_key_rows, text_value_rows, other_out, other_inv, mixed = attention_call(
        functools.partial(cross_forward_kernel, heads),
        "cross_forward",
        [cross_meta, lengths],
        [
            (ids_row, True),
            (local_gains, False),
            (queries, True),
            (own_out, True),
            (text_key_raw, False),
            (text_value_raw, False),
        ],
        [
            (text_narrow, False),
            (text_rows, False),
            (text_rows, False),
            (wide, True),
            (sums, True),
            (narrow, True),
        ],
        [pltpu.VMEM((local, slots), jnp.bfloat16), tile_sums],
        row_tokens,
        18000,
    )
    norm_gains = gains
    if fused:
        attn_sum, middle, feed_all, down_other = remote_call(
            attention_out_kernel,
            "attention_out",
            5,
            [mixed, out_full, latents, gate_attn, scale_feed, norm_gains],
            [shape((shard_rows, width)), shape((shard_rows, width)), gathered],
            [pltpu.VMEM((shard_rows, local), bf16), *in_kernel, all_sems],
            [down_line],
        )
        feed_all = feed_all.reshape(row_tokens, width)
        down_full = join_near(down_line, down_other, rows)
        gate_up, hidden, feed_sum, block_out, feed_sum_grad = remote_call(
            feed_kernel,
            "feed_forward",
            6,
            [feed_all, feed_full, down_full, middle, gate_feed, cotangent, norm_gains],
            [
                shape((row_tokens, 2 * units)),
                shape((row_tokens, units), bf16),
                shape((shard_rows, width)),
                shape((shard_rows, width)),
                gathered,
            ],
            [*in_kernel, all_sems],
        )
        feed_sum_grad = feed_sum_grad.reshape(row_tokens, width)
    else:
        attn_sum = collect(
            [
                dot(
                    lax.dynamic_slice_in_dim(mixed, owner(i) * shard_rows, shard_rows, 1),
                    out_full,
                    0,
                    1,
                )
                for i in range(tensor_size)
            ]
        )
        middle, feed_block = middle_point(
            attn_sum, source, gate_attn, scale_feed, gains[1], gains[2]
        )
        feed_all = in_place(spread(feed_block))
        down_full = join_near(down_line, near_swap(down_line), rows)
        gate_up = dot(feed_all, feed_full, 1, 0)
        hidden = half(jax.nn.silu(gate_up[:, :units]) * gate_up[:, units:])
        feed_sum = collect(split(dot(hidden, down_full, 1, 1)))
        block_out, feed_block_grad = end_point(
            feed_sum, middle, gate_feed, cotangent, gains[3]
        )
        feed_sum_grad = in_place(spread(feed_block_grad))
    feed_out_grad = half(dot(feed_sum_grad, hidden, 0, 0))
    feed_out_parts = feed_out_grad.reshape(dp_size // 2, 2, -1, units)
    if fused:
        pair_grad, feed_input_grad, middle_grad, attn_sum_grad, feed_out_other = remote_call(
            feed_back_kernel,
            "feed_backward",
            7,
            [
                feed_sum_grad,
                gate_up,
                feed_full,
                down_full,
                attn_sum,
                middle,
                gate_attn,
                scale_feed,
                cotangent,
                norm_gains,
            ],
            [
                shape((row_tokens, 2 * units), bf16),
                shape((shard_rows, width)),
                shape((shard_rows, width)),
                gathered,
            ],
            [*in_kernel, all_sems],
            [feed_out_parts],
        )
        attn_sum_grad = attn_sum_grad.reshape(row_tokens, width)
    else:
        hidden_grad = dot(feed_sum_grad, down_full, 1, 0)
        pair_grad = jnp.concatenate(
            pair_point(hidden_grad, gate_up[:, :units], gate_up[:, units:]), axis=1
        )
        feed_input_grad = collect(split(dot(pair_grad, feed_full, 1, 1)))
        middle_grad, attn_block_grad = middle_back_point(
            feed_input_grad,
            attn_sum,
            middle,
            gate_attn,
            scale_feed,
            cotangent,
            gains[1],
            gains[2],
        )
        attn_sum_grad = in_place(spread(attn_block_grad))
        feed_out_other = swap_half(feed_out_parts)
    feed_out_sum = scatter_far((feed_out_parts,), (feed_out_other,))
    feed_in_grad = half(dot(feed_all, pair_grad, 0, 0))
    feed_in_both = lax.psum_scatter(
        feed_in_grad, "dp", scatter_dimension=0, tiled=True, axis_index_groups=far_groups()
    )
    mixed_grad = dot(out_full, gate(attn_sum_grad, feed_in_grad), 0, 1)
    out_parts = half(dot(attn_sum_grad, mixed, 0, 1)).reshape(dp_size // 2, 2, -1, local)
    query_two, text_key_grad, text_value_grad, text_gains = attention_call(
        functools.partial(cross_backward_kernel, heads),
        "cross_backward",
        [cross_meta, lengths],
        [
            (ids_row, True),
            (local_gains, False),
            (queries, True),
            (text_key_rows, False),
            (text_keys, False),
            (text_value_rows, False),
            (other_inv, True),
            (other_out, True),
            (mixed_grad, True),
            (text_key_raw, False),
        ],
        [(wide, True), (text_narrow, False), (text_narrow, False), (gain_shape, False)],
        [
            pltpu.VMEM((local, TILE), jnp.bfloat16),
            tile_sums,
            pltpu.VMEM((local, slots), jnp.float32),
            pltpu.VMEM((local, slots), jnp.float32),
            pltpu.VMEM((local, TILE), jnp.float32),
        ],
        row_tokens,
        25000,
    )
    triple_grad, own_gains = attention_call(
        functools.partial(self_backward_kernel, heads),
        "self_backward",
        [self_meta],
        [
            (ids_row, True),
            (ids_column, False),
            (local_gains, False),
            *tables,
            (queries, True),
            (key_rows, False),
            (keys, False),
            (value_rows, False),
            (own_inv, True),
            (own_out, True),
            (mixed_grad, True),
            (query_two, True),
            (raw_query, True),
            (raw_rest[:local], False),
        ],
        [
            (jax.ShapeDtypeStruct((3 * local, row_tokens), jnp.bfloat16), False),
            (gain_shape, False),
        ],
        [
            pltpu.VMEM((local, TILE), jnp.bfloat16),
            tile_sums,
            pltpu.VMEM((local, TILE), jnp.float32),
            pltpu.VMEM((local, row_tokens), jnp.float32),
            pltpu.VMEM((local, row_tokens), jnp.float32),
            pltpu.VMEM((local, TILE), jnp.float32),
        ],
        row_tokens,
        25000,
        [feed_out_sum],
    )
    in_parts = half(dot(attn_full, triple_grad, 0, 1)).reshape(dp_size // 2, 2, -1, 3 * local)

    def caption_back(grad, carry, after=()):
        if fused:
            grad, _, *others = remote_call(
                text_kernel,
                f"text_gradient_{len(carry)}",
                7 + len(carry),
                [grad, captions],
                [
                    shape((tensor_size * local, captions.shape[1]), bf16),
                    shape((tensor_size, local, slots), bf16),
                ],
                [semaphores(3 * CHUNKS)],
                carry,
                after=after,
            )
        else:
            grad = half(dot(in_place(spread(grad)), captions, 1, 0))
            others = [swap_half(parts) for parts in carry]
        return (grad.reshape(dp_size // 2, 2, -1, captions.shape[1]), *others)

    value_parts, in_other, out_other = caption_back(text_value_grad, [in_parts, out_parts])
    attention_sum = scatter_far((in_parts, out_parts), (in_other, out_other))
    key_parts, value_other = caption_back(text_key_grad, [value_parts], [feed_in_both])
    value_sum = scatter_far((value_parts,), (value_other,))
    if fused:
        attn_input_grad, key_other = remote_call(
            enter_back_kernel,
            "enter_backward",
            10,
            [triple_grad, in_full],
            [shape((shard_rows, width))],
            [pltpu.VMEM((shard_rows, 3 * local), bf16), *in_kernel, sum_sems],
            [key_parts],
            after=[attention_sum],
        )
    else:
        attn_input_grad = collect(
            [
                dot(
                    lax.dynamic_slice_in_dim(triple_grad, owner(i) * shard_rows, shard_rows, 1),
                    in_full,
                    0,
                    1,
                )
                for i in range(tensor_size)
            ]
        )
        key_other = swap_half(key_parts)
    key_sum = scatter_far((key_parts,), (key_other,))
    in_sum, out_sum = attention_sum[:, : 3 * local], attention_sum[:, 3 * local :]
    first_norm, _ = rms_parts(attn_sum)
    feed_norm, _ = rms_parts(middle)
    second_norm, _ = rms_parts(feed_sum)
    tanh_attn, tanh_feed = jnp.tanh(gate_attn), jnp.tanh(gate_feed)
    branch_attn_grad, branch_feed_grad = tanh_attn * middle_grad, tanh_feed * cotangent
    gate_attn_grad = middle_grad * (first_norm * gains[1]) * (1.0 - tanh_attn * tanh_attn)
    gate_feed_grad = cotangent * (second_norm * gains[3]) * (1.0 - tanh_feed * tanh_feed)
    scale_feed_grad = feed_input_grad * feed_norm * gains[2]
    scale_attn_grad = attn_input_grad * attn_norm * gains[0]
    latent_grad = middle_grad + rms_back(
        attn_norm, attn_inv, attn_input_grad * gains[0] * (1.0 + scale_attn)
    )
    shared_rows = jnp.stack(
        [
            jnp.sum(attn_input_grad * attn_norm * (1.0 + scale_attn), axis=0),
            jnp.sum(branch_attn_grad * first_norm, axis=0),
            jnp.sum(feed_input_grad * feed_norm * (1.0 + scale_feed), axis=0),
            jnp.sum(branch_feed_grad * second_norm, axis=0),
        ]
    )
    head_rows = jnp.stack(
        [own_gains[:, 0], own_gains[:, 128], text_gains[:, 128], text_gains[:, 0]]
    )
    head_full = lax.dynamic_update_slice(
        jnp.zeros((4, width), jnp.float32), head_rows, (jnp.zeros((), jnp.int32), offset)
    )
    channel_part = jnp.concatenate([shared_rows, head_full], axis=0)
    factor_tokens = jnp.concatenate(
        [scale_attn_grad, gate_attn_grad, scale_feed_grad, gate_feed_grad], axis=1
    )
    factor_image = jnp.dot(chooser.T, factor_tokens, precision=HIGH)
    factor_image = jnp.transpose(
        factor_image.reshape(per_row, dp_size, tensor_size, own_columns), (2, 1, 0, 3)
    )
    channel_blocks = jnp.transpose(channel_part.reshape(8, dp_size, -1), (1, 0, 2))
    channel_blocks = channel_blocks.reshape(dp_size, -1, own_columns)
    payload = jnp.concatenate(
        [factor_image, jnp.broadcast_to(channel_blocks, (tensor_size, *channel_blocks.shape))],
        axis=2,
    )
    blocks = payload.shape[1:]
    feed_in_parts = feed_in_both.reshape(1, 2, -1, 2 * units)
    received, feed_in_other = remote_call(
        return_kernel,
        "modulation_return",
        1,
        [payload],
        [shape(blocks)],
        exchange_scratch([payload.shape, blocks, blocks]),
        [feed_in_parts],
        everyone=True,
        after=[value_sum],
    )
    feed_in_sum = lax.dynamic_index_in_dim(
        feed_in_parts, dp_index % 2, 1, keepdims=False
    ).astype(f32) + feed_in_other.astype(f32)
    feed_in_sum = feed_in_sum[0]
    factor_grad = received[:, :per_row].reshape(images, own_columns)
    channel_sum = jnp.sum(received[:, per_row:], axis=0).reshape(channels.shape)
    modulator_sum = jnp.dot(augmented.astype(jnp.float32).T, factor_grad, precision=HIGH)

    in_sum, out_sum, feed_in_sum, feed_out_sum, key_sum, value_sum = (
        value.astype(jnp.float32)
        for value in (in_sum, out_sum, feed_in_sum, feed_out_sum, key_sum, value_sum)
    )
    squares = (
        jnp.sum(in_sum * in_sum)
        + jnp.sum(out_sum * out_sum)
        + jnp.sum(feed_in_sum * feed_in_sum)
        + jnp.sum(feed_out_sum * feed_out_sum)
        + jnp.sum(key_sum * key_sum)
        + jnp.sum(value_sum * value_sum)
        + jnp.sum(modulator_sum * modulator_sum)
        + jnp.sum(channel_sum * channel_sum) / tensor_size
    )
    in_sum = jnp.stack([in_sum[:, i * local : (i + 1) * local] for i in range(3)])
    feed_in_sum = jnp.stack([feed_in_sum[:, i * units : (i + 1) * units] for i in range(2)])
    caption_sum = jnp.stack([key_sum.T, value_sum.T])
    (squares,) = remote_call(
        total_kernel,
        "norm_exchange",
        2,
        [jnp.broadcast_to(squares, (8, 128))],
        [shape((8, 128))],
        exchange_scratch([(tensor_size, 8, 128), (dp_size, 8, 128), (8, 128)]),
        everyone=True,
    )
    grad_norm = jnp.sqrt(squares[0, 0])
    factor = CLIP / jnp.maximum(grad_norm, CLIP)
    results = [
        adamw(grad * factor, weight, moment, square, DECAY, RATE)
        for grad, weight, moment, square in (
            (in_sum, attention_in, moment_attention_in, square_attention_in),
            (out_sum.T, attention_out, moment_attention_out, square_attention_out),
            (feed_in_sum, feed_in, moment_feed_in, square_feed_in),
            (feed_out_sum.T, feed_out, moment_feed_out, square_feed_out),
            (caption_sum, caption_in, moment_caption_in, square_caption_in),
            (modulator_sum, modulator, moment_modulator, square_modulator),
        )
    ]
    results.append(
        adamw(channel_sum * factor, channels, moment_channels, square_channels, 0.0, GAIN_RATE)
    )
    return (block_out, latent_grad, grad_norm, *(part for result in results for part in result))


def solution(mesh):
    return jax.shard_map(
        body,
        mesh=mesh,
        in_specs=(
            P(("dp", "tensor"), None),
            P(("dp", "tensor"), None),
            P("dp", "tensor"),
            P(),
            P("dp", None),
            P("dp", None),
            P("dp", None),
            P("dp", None),
            P(None, "dp", "tensor"),
            P("tensor", "dp"),
            P(None, "dp", "tensor"),
            P("tensor", "dp"),
            P(None, "tensor", "dp"),
            P(None, ("dp", "tensor")),
            P(None, "dp"),
            P(None, "dp", "tensor"),
            P(None, "dp", "tensor"),
            P("tensor", "dp"),
            P("tensor", "dp"),
            P(None, "dp", "tensor"),
            P(None, "dp", "tensor"),
            P("tensor", "dp"),
            P("tensor", "dp"),
            P(None, "tensor", "dp"),
            P(None, "tensor", "dp"),
            P(None, ("dp", "tensor")),
            P(None, ("dp", "tensor")),
            P(None, "dp"),
            P(None, "dp"),
        ),
        out_specs=(
            P(("dp", "tensor"), None),
            P(("dp", "tensor"), None),
            P(),
            P(None, "dp", "tensor"),
            P(None, "dp", "tensor"),
            P(None, "dp", "tensor"),
            P("tensor", "dp"),
            P("tensor", "dp"),
            P("tensor", "dp"),
            P(None, "dp", "tensor"),
            P(None, "dp", "tensor"),
            P(None, "dp", "tensor"),
            P("tensor", "dp"),
            P("tensor", "dp"),
            P("tensor", "dp"),
            P(None, "tensor", "dp"),
            P(None, "tensor", "dp"),
            P(None, "tensor", "dp"),
            P(None, ("dp", "tensor")),
            P(None, ("dp", "tensor")),
            P(None, ("dp", "tensor")),
            P(None, "dp"),
            P(None, "dp"),
            P(None, "dp"),
        ),
        check_vma=False,
    )
```

time: 1120 us -> 837 us (0.75)
  Pallas kernels: 86.6 us -> 634 us
  waiting for transfers between devices: 400 us -> 0.88 us
  blocking collectives: 148 us -> 0 us
  other arithmetic: 170 us -> 81.4 us
  matrix products: 131 us -> 46.8 us
  local copies, waits for them, and re-layouts: 107 us -> 42.3 us
  starting transfers between devices: 41.5 us -> 0.88 us
    pallas_call x4 -> x17, Pallas kernels: 86.6 us -> 634 us  [the longest x12 543 us: remote_call(): pl.pallas_call(run, out_shape=[*outs, *swapped], in_specs=[whole] * len(o...]
    ppermute x42 -> x0, waiting for transfers between devices: 386 us -> none  [the longest x30 205 us: swap_tensor(): lax.ppermute(value, 'tensor', [(i, i ^ bits) for i in range(lax.axis_size...]
    dot_general x28 -> x6, matrix products: 124 us -> 39.4 us  [dot(): lax.dot_general(left, right, (((left_dim,), (right_dim,)), ((), ())), pre...]
    psum x2 -> x0, blocking collectives: 81.8 us -> none  [the longest x1 41.4 us: body(): lax.psum(jnp.concatenate([shared_rows, head_full], axis=0), ('dp', 'tenso...]
    all_gather x3 -> x0, blocking collectives: 66 us -> none  [the longest x1 35.2 us: body(): channel_half = lax.all_gather(half(channels), 'dp', axis=1, tiled=True)]
    ppermute x42 -> x0, starting transfers between devices: 27.9 us -> none  [the longest x12 15.2 us: near_swap(): lax.ppermute(value, 'dp', [(i, i ^ 1) for i in range(lax.axis_size('dp'))])]
    unnamed x369 -> x152, local copies, waits for them, and re-layouts: 45 us -> 20.2 us
    reshape x7 -> x2, local copies, waits for them, and re-layouts: 22.2 us -> 0.96 us  [the longest x1 0.7 us: body(): gains = jnp.transpose(gains, (1, 0, 2)).reshape(8, width)]
  transfers between devices with their start and end apart: 56 -> 10, of which waited for: 24 -> 0; matrix products, arithmetic and copies ran while one was open for 29% -> 14% of each run, Pallas kernels for 8% -> 61%
where the time goes in v2:
time: 837 us; the launch traced here: 829 us
  Pallas kernels  634 us (76%)
  other arithmetic  81.4 us (10%)
  matrix products  46.8 us (6%)
  local copies, waits for them, and re-layouts  42.3 us (5%)
  between operations  22.5 us (3%)
    pallas_call x12, Pallas kernels, remote_call(): pl.pallas_call(run, out_shape=[*outs, *swapped], in_specs=[whole] * len(o...  543 us
    pallas_call x4, Pallas kernels, attention_call(): pl.pallas_call(run, grid_spec=pltpu.PrefetchScalarGridSpec(num_scalar_pre...  91.5 us
    dot_general x6, matrix products, dot(): lax.dot_general(left, right, (((left_dim,), (right_dim,)), ((), ())), pre...  39.4 us
    unnamed x152, local copies, waits for them, and re-layouts  20.2 us
  transfers between devices with their start and end apart: 10, of which 0 were waited for; matrix products, arithmetic and copies ran while one was open for 14% of the time, Pallas kernels for 61%

profile of v2, /device:TPU:0, one launch (start us, length us, event | category | flops | bytes accessed | tf_op | source)
XLA Modules:
  0.0 829.2 jit_solution(14852498153372748251)
XLA Ops:
  16.3 33.1 %modulation_exchange.1 = (f32[4,8,16,192]{3,2,1,0:T(8,128)}, bf16[192,2048]{1,0:T(8,128)(2,1)}) custom-call(f32[8,16,192]{2,1,0:T(8,128)} %pad_maximum_fusion.10.refs_0_, bf16[192,2048]{1,0:T(8,128)(2,1)} %pad_maximum_fusion.7.refs_1_), custom_call_target="tpu_custom_call" | custom-call | tf_op jit(solution)/shard_map/modulation_exchange/pallas_call | solution.py:264
  69.1 42.2 %enter.1 = (bf16[4,256,1536]{2,1,0:T(8,128)(2,1)}, bf16[768,1024]{1,0:T(8,128)(2,1)}) custom-call(bf16[256,1536]{1,0:T(8,128)(2,1)} %refs_2_.4, f32[256,1536]{1,0:T(8,128)} %get-tuple-element.168.refs_1_, f32[8,1536]{1,0:T(8,128)} %reshape.534.refs_2_.refs_5_.refs_6_.refs_9_, bf16[768,1024]{1,0:T(8,128)(2,1)} %all-gather.10.cloned.1.call-done.refs_3_), custom_call_target="tpu_custom_call" | custom-call | tf_op jit(solution)/shard_map/enter/pallas_call | solution.py:264
  115.2 48.1 %project.2 = (f32[384,2048]{1,0:T(8,128)}, bf16[768,1024]{1,0:T(8,128)(2,1)}) custom-call(bf16[1536,1024]{1,0:T(8,128)(2,1)} %bitcast.174, bf16[2048,1024]{1,0:T(8,128)(2,1)} %refs_1_.11, bf16[768,1024]{1,0:T(8,128)(2,1)} %all-gather.8.cloned.1.call-done.refs_2_), custom_call_target="tpu_custom_call" | custom-call | tf_op jit(solution)/shard_map/project/pallas_call | solution.py:264
  167.2 58.5 %project.3 = (f32[384,2048]{1,0:T(8,128)}, bf16[768,1536]{1,0:T(8,128)(2,1)}) custom-call(bf16[1536,1024]{1,0:T(8,128)(2,1)} %bitcast.175, bf16[2048,1024]{1,0:T(8,128)(2,1)} %refs_1_.11, bf16[768,1536]{1,0:T(8,128)(2,1)} %all-gather.6.cloned.1.call-done.refs_2_), custom_call_target="tpu_custom_call" | custom-call | tf_op jit(solution)/shard_map/project/pallas_call | solution.py:264
  230.7 3.9 fusion.70
  238.7 18.5 %self_forward.1 = (bf16[384,1024]{1,0:T(8,128)(2,1)}, bf16[384,1024]{1,0:T(8,128)(2,1)}, bf16[6,1024,64]{2,1,0:T(8,128)(2,1)}, bf16[6,1024,64]{2,1,0:T(8,128)(2,...) custom-call(s32[8]{0:T(128)} %reshape.532.refs_0_, s32[1,1024]{1,0:T(1,128)} %refs_1_.9, s32[1024,1]{1,0:T(8,128)} %copy.127.refs_2_, ...), custom_call_target="tpu_custom_call" | custom-call | flops 15000 | bytes 15000 | tf_op jit(solution)/shard_map/self_forward/pallas_call | solution.py:1006
  257.2 23.7 %cross_forward.1 = (bf16[384,2048]{1,0:T(8,128)(2,1)}, bf16[6,2048,64]{2,1,0:T(8,128)(2,1)}, bf16[6,2048,64]{2,1,0:T(8,128)(2,1)}, f32[384,1024]{1,0:T(8,128)}, ...) custom-call(s32[8]{0:T(128)} %reshape.530.refs_0_, s32[8]{0:T(128)} %bitcast.219, s32[1,1024]{1,0:T(1,128)} %refs_1_.9, ...), custom_call_target="tpu_custom_call" | custom-call | flops 18000 | bytes 18000 | tf_op jit(solution)/shard_map/cross_forward/pallas_call | solution.py:1006
  283.3 54.0 %attention_out.1 = (f32[256,1536]{1,0:T(8,128)}, f32[256,1536]{1,0:T(8,128)}, bf16[4,256,1536]{2,1,0:T(8,128)(2,1)}, bf16[768,1024]{1,0:T(8,128)(2,1)}) custom-call(bf16[384,1024]{1,0:T(8,128)(2,1)} %get-tuple-element.82.refs_0_, bf16[1536,384]{1,0:T(8,128)(2,1)} %bitcast.198, bf16[256,1536]{1,0:T(8,128)(2,1)} %refs_2_.4, ...), custom_call_target="tpu_custom_call" | custom-call | tf_op jit(solution)/shard_map/attention_out/pallas_call | solution.py:264
  340.8 57.8 %feed_forward.1 = (f32[1024,2048]{1,0:T(8,128)}, bf16[1024,1024]{1,0:T(8,128)(2,1)}, f32[256,1536]{1,0:T(8,128)}, f32[256,1536]{1,0:T(8,128)}, bf16[4,256,1536]{2,1,0:T(8,128)(2,1)}) custom-call(bf16[1024,1536]{1,0:T(8,128)(2,1)} %bitcast.200, bf16[1536,2048]{1,0:T(8,128)(2,1)} %all-gather.14.cloned.1.call-done.refs_1_.refs_2_, ...), custom_call_target="tpu_custom_call" | custom-call | tf_op jit(solution)/shard_map/feed_forward/pallas_call | solution.py:264
  398.6 7.6 convolution_convert_fusion.2
  406.3 60.7 %feed_backward.1 = (bf16[1024,2048]{1,0:T(8,128)(2,1)}, f32[256,1536]{1,0:T(8,128)}, f32[256,1536]{1,0:T(8,128)}, bf16[4,256,1536]{2,1,0:T(8,128)(2,1)}, bf16[4,192,1024]{2,1,0:T(8,128)(2,1)}) custom-call(bf16[1024,1536]{1,0:T(8,128)(2,1)} %bitcast.203, f32[1024,2048]{1,0:T(8,128)} %get-tuple-element.89.refs_1_, ...), custom_call_target="tpu_custom_call" | custom-call | tf_op jit(solution)/shard_map/feed_backward/pallas_call | solution.py:264
  470.3 11.7 %convolution_convert_fusion.1.after = bf16[1536,2048]{1,0:T(8,128)(2,1)} fusion(bf16[1024,1536]{1,0:T(8,128)(2,1)} %bitcast.201, bf16[1024,2048]{1,0:T(8,128)(2,1)} %get-tuple-element.98), kind=kOutput, calls=%fused_computation.1 | convolution fusion | flops 6445596672 | bytes 13631488 | tf_op jit(solution)/shard_map/dot_general | solution.py:39
  484.0 4.0 convolution_convert_fusion.3
  489.3 4.5 fusion.71.refs_10_.refs_14_
  493.8 27.2 %cross_backward.1 = (f32[384,1024]{1,0:T(8,128)}, bf16[384,2048]{1,0:T(8,128)(2,1)}, bf16[384,2048]{1,0:T(8,128)(2,1)}, f32[384,256]{1,0:T(8,128)}) custom-call(s32[8]{0:T(128)} %reshape.530.refs_0_, s32[8]{0:T(128)} %bitcast.220, s32[1,1024]{1,0:T(1,128)} %refs_1_.9, f32[384,4]{1,0:T(8,128)} %dynamic-slice_bitcast_fusion.refs_3_, ...), custom_call_target="tpu_custom_call" | custom-call | flops 25000 | bytes 25000 | tf_op jit(solution)/shard_map/cross_backward/pallas_call | solution.py:1006
  521.0 22.1 %self_backward.1 = (bf16[1152,1024]{1,0:T(8,128)(2,1)}, f32[384,256]{1,0:T(8,128)}) custom-call(s32[8]{0:T(128)} %reshape.532.refs_0_, s32[1,1024]{1,0:T(1,128)} %refs_1_.9, s32[1024,1]{1,0:T(8,128)} %copy.127.refs_2_, f32[384,4]{1,0:T(8,128)} %dynamic-slice_bitcast_fusion.refs_3_, f32[32,1024]{1,0:T(8,128)} %get-tuple-element.197.refs_4_.refs_6_, ...), custom_call_target="tpu_custom_call" | custom-call | flops 25000 | bytes 25000 | tf_op jit(solution)/shard_map/self_backward/pallas_call | solution.py:1006
  543.1 7.7 convolution_convert_fusion
  550.8 68.3 %text_gradient_2.1 = (bf16[1536,1024]{1,0:T(8,128)(2,1)}, bf16[4,384,2048]{2,1,0:T(8,128)(2,1)}, bf16[4,192,1152]{2,1,0:T(8,128)(2,1)}, bf16[4,192,384]{2,1,0:T(8,128)(2,1)}) custom-call(bf16[384,2048]{1,0:T(8,128)(2,1)} %get-tuple-element.108.refs_0_, bf16[2048,1024]{1,0:T(8,128)(2,1)} %refs_1_.11, bf16[4,2,192,1152]{3,2,1,0:T(8,128)(2,1)} %bitcast.179, ...), custom_call_target="tpu_custom_call" | custom-call | tf_op jit(solution)/shard_map/text_gradient_2/pallas_call | solution.py:264
  626.7 45.4 %text_gradient_1.1 = (bf16[1536,1024]{1,0:T(8,128)(2,1)}, bf16[4,384,2048]{2,1,0:T(8,128)(2,1)}, bf16[4,192,1024]{2,1,0:T(8,128)(2,1)}) custom-call(bf16[384,2048]{1,0:T(8,128)(2,1)} %get-tuple-element.107.refs_0_, bf16[2048,1024]{1,0:T(8,128)(2,1)} %refs_1_.11, bf16[4,2,192,1024]{3,2,1,0:T(8,128)(2,1)} %bitcast.187, ...), custom_call_target="tpu_custom_call" | custom-call | tf_op jit(solution)/shard_map/text_gradient_1/pallas_call | solution.py:264
  688.4 40.9 %enter_backward.1 = (f32[256,1536]{1,0:T(8,128)}, bf16[4,192,1024]{2,1,0:T(8,128)(2,1)}) custom-call(bf16[1152,1024]{1,0:T(8,128)(2,1)} %get-tuple-element.106.refs_0_, bf16[1536,1152]{1,0:T(8,128)(2,1)} %bitcast.173, bf16[4,2,192,1024]{3,2,1,0:T(8,128)(2,1)} %bitcast.185, bf16[192,1536]{1,0:T(8,128)(2,1)} %reduce-scatter.10.cloned.1.call-done.refs_3_), custom_call_target="tpu_custom_call" | custom-call | tf_op jit(solution)/shard_map/enter_backward/pallas_call | solution.py:264
  734.5 8.0 multiply_reduce_fusion.4
  742.9 5.7 subtract_multiply_fusion
  752.1 23.5 %modulation_return.1 = (f32[8,16,192]{2,1,0:T(8,128)}, bf16[1,192,2048]{2,1,0:T(8,128)(2,1)}) custom-call(f32[4,8,16,192]{3,2,1,0:T(8,128)} %pad_maximum_fusion.9.refs_0_, bf16[1,2,192,2048]{3,2,1,0:T(8,128)(2,1)} %bitcast.176, bf16[192,1024]{1,0:T(8,128)(2,1)} %reduce-scatter.12.cloned.1.call-done.refs_2_), custom_call_target="tpu_custom_call" | custom-call | tf_op jit(solution)/shard_map/modulation_return/pallas_call | solution.py:264
  788.6 10.6 %norm_exchange.1 = f32[8,128]{1,0:T(8,128)} custom-call(f32[8,128]{1,0:T(8,128)} %broadcast_in_dim.11.refs_0_), custom_call_target="tpu_custom_call" | custom-call | tf_op jit(solution)/shard_map/norm_exchange/pallas_call | solution.py:264
  (308 shorter events, 119.2 us)
Async XLA Ops:
  7.2 61.9 %all-gather.10.cloned.1.call-start = ((), (), s32[]{:S(2)}) async-start(), calls=%async_computation.7 | async-start | bytes 1966080 | tf_op jit(solution)/shard_map/all_gather | solution.py:99
  9.7 105.4 %all-gather.8.cloned.1.call-start = ((), (), s32[]{:S(2)}) async-start(), calls=%async_computation.6 | async-start | bytes 1966080 | tf_op jit(solution)/shard_map/all_gather | solution.py:99
  10.5 156.8 %all-gather.6.cloned.1.call-start = ((), (), s32[]{:S(2)}) async-start(), calls=%async_computation.5 | async-start | bytes 2949120 | tf_op jit(solution)/shard_map/all_gather | solution.py:99
  11.6 271.6 %all-gather.12.cloned.1.call-start = ((), (), s32[]{:S(2)}) async-start(), calls=%async_computation.8 | async-start | bytes 1966080 | tf_op jit(solution)/shard_map/all_gather | solution.py:99
  12.7 328.1 %all-gather.14.cloned.1.call-start = ((), (), s32[]{:S(2)}) async-start(), calls=%async_computation.9 | async-start | bytes 7864320 | tf_op jit(solution)/shard_map/all_gather | solution.py:99
  52.2 5.6 copy-start.68
  52.2 468.7 %reduce-scatter.6.cloned.1.call-start = ((), (), s32[]{:S(2)}) async-start(), calls=%async_computation.10 | async-start | bytes 1966080 | tf_op jit(solution)/shard_map/reduce_scatter | solution.py:131
  69.1 42.2 %copy-start.13 = (bf16[768,1024]{1,0:T(8,128)(2,1)S(1)}, bf16[768,1024]{1,0:T(8,128)(2,1)}, u32[]{:S(2)}) copy-start(bf16[768,1024]{1,0:T(8,128)(2,1)} %all-gather.10.cloned.1.call-done.refs_3_) | copy-start | bytes 4718596
  115.2 48.1 %copy-start.17 = (bf16[768,1024]{1,0:T(8,128)(2,1)S(1)}, bf16[768,1024]{1,0:T(8,128)(2,1)}, u32[]{:S(2)}) copy-start(bf16[768,1024]{1,0:T(8,128)(2,1)} %all-gather.8.cloned.1.call-done.refs_2_) | copy-start | bytes 4718596
  167.2 58.5 %copy-start.8 = (bf16[768,1536]{1,0:T(8,128)(2,1)S(1)}, bf16[768,1536]{1,0:T(8,128)(2,1)}, u32[]{:S(2)}) copy-start(bf16[768,1536]{1,0:T(8,128)(2,1)} %all-gather.6.cloned.1.call-done.refs_2_) | copy-start | bytes 7077892
  227.9 6.7 copy-start.5
  283.3 54.0 %copy-start.11 = (bf16[768,1024]{1,0:T(8,128)(2,1)S(1)}, bf16[768,1024]{1,0:T(8,128)(2,1)}, u32[]{:S(2)}) copy-start(bf16[768,1024]{1,0:T(8,128)(2,1)} %all-gather.12.cloned.1.call-done.refs_6_) | copy-start | bytes 4718596
  406.3 60.7 %copy-start.10 = (bf16[1536,1024]{1,0:T(8,128)(2,1)S(1)}, bf16[1536,1024]{1,0:T(8,128)(2,1)}, u32[]{:S(2)}) copy-start(bf16[1536,1024]{1,0:T(8,128)(2,1)} %convolution_convert_fusion.2) | copy-start | bytes 9437188
  470.3 156.4 %reduce-scatter.8.cloned.1.call-start = ((), (), s32[]{:S(2)}) async-start(), calls=%async_computation.11 | async-start | bytes 7864320 | tf_op jit(solution)/shard_map/reduce_scatter | solution.py:1370
  482.1 199.6 %reduce-scatter.10.cloned.1.call-start = ((), (), s32[]{:S(2)}) async-start(), calls=%async_computation.12 | async-start | bytes 2949120 | tf_op jit(solution)/shard_map/reduce_scatter | solution.py:131
  521.0 22.1 %copy-start.72 = (bf16[4,256,1536]{2,1,0:T(8,128)(2,1)S(1)}, bf16[4,256,1536]{2,1,0:T(8,128)(2,1)}, u32[]{:S(2)}) copy-start(bf16[4,256,1536]{2,1,0:T(8,128)(2,1)} %get-tuple-element.77) | copy-start | bytes 9437188
  550.8 69.9 %copy-start.9 = (bf16[1536,1152]{1,0:T(8,128)(2,1)S(1)}, bf16[1536,1152]{1,0:T(8,128)(2,1)}, u32[]{:S(2)}) copy-start(bf16[1536,1152]{1,0:T(8,128)(2,1)} %convolution_convert_fusion) | copy-start | bytes 10616836
  623.0 129.1 %reduce-scatter.12.cloned.1.call-start = ((), (), s32[]{:S(2)}) async-start(), calls=%async_computation.13 | async-start | bytes 1966080 | tf_op jit(solution)/shard_map/reduce_scatter | solution.py:131
  675.8 106.9 %reduce-scatter.14.cloned.1.call-start = ((), (), s32[]{:S(2)}) async-start(), calls=%async_computation.14 | async-start | bytes 1966080 | tf_op jit(solution)/shard_map/reduce_scatter | solution.py:131
  742.8 5.7 copy-start.30
  742.8 5.7 copy-start.33
  742.8 5.7 copy-start.70
  751.3 24.3 %copy-start.7 = (bf16[384,2048]{1,0:T(8,128)(2,1)S(1)}, bf16[384,2048]{1,0:T(8,128)(2,1)}, u32[]{:S(2)}) copy-start(bf16[384,2048]{1,0:T(8,128)(2,1)} %reduce-scatter.8.cloned.1.call-done.refs_3_) | copy-start | bytes 4718596
  775.6 9.6 %copy-start.23 = (bf16[192,1024]{1,0:T(8,128)(2,1)S(1)}, bf16[192,1024]{1,0:T(8,128)(2,1)}, u32[]{:S(2)}) copy-start(bf16[192,1024]{1,0:T(8,128)(2,1)} %reduce-scatter.12.cloned.1.call-done.refs_2_) | copy-start | bytes 1179652
  (59 other events, 131.5 us)
Sparse Core Ops, SparseCore 0:
  10.2 42.6 all-gather.9
  55.0 35.7 all-gather.7
  93.0 49.3 all-gather.5
  144.4 35.8 all-gather.11
  181.7 114.2 all-gather.13
  470.4 32.5 reduce-scatter.5
  505.3 109.6 reduce-scatter.7
  623.1 45.3 reduce-scatter.9
  675.9 32.7 reduce-scatter.11
  733.2 33.1 reduce-scatter.13

commit v3 on v2

--- a/solution.py
+++ b/solution.py
@@ -88,28 +88,21 @@
     return [list(range(near, count, 2)) for near in range(2)]
 
 
-def near_pair(value, other):
-    odd = lax.axis_index("dp") % 2
-    return jnp.concatenate(
-        [jnp.where(odd == 0, value, other), jnp.where(odd == 0, other, value)], axis=0
-    )
-
-
 def gather_far(value):
     return lax.all_gather(value, "dp", axis=0, tiled=True, axis_index_groups=far_groups())
 
 
-def join_near(line, other, rows, start=0, stop=None):
+def flat(blocks):
+    return blocks.reshape(-1, blocks.shape[-1])
+
+
+def join_near(own, other, count):
     odd = lax.axis_index("dp") % 2
-    line = line[:, start:stop]
-    other = other[:, start:stop]
-    columns = line.shape[1]
-    line = line.reshape(-1, rows, columns)
-    other = other.reshape(-1, rows, columns)
-    both = jnp.stack(
-        [jnp.where(odd == 0, line, other), jnp.where(odd == 0, other, line)], axis=1
-    )
-    return both.reshape(-1, columns)
+    own = own.reshape(-1, count, own.shape[1])
+    other = other.reshape(own.shape)
+    return flat(
+        jnp.stack([jnp.where(odd == 0, own, other), jnp.where(odd == 0, other, own)], axis=1)
+    )
 
 
 def swap_half(parts):
@@ -118,22 +111,15 @@
     return near_swap(send.reshape(-1, send.shape[2])).reshape(send.shape)
 
 
-def scatter_far(parts, others):
+def sum_half(parts, other):
     odd = lax.axis_index("dp") % 2
-    summed = [
-        half(
-            lax.dynamic_index_in_dim(part, odd, 1, keepdims=False).astype(jnp.float32)
-            + other.astype(jnp.float32)
-        )
-        for part, other in zip(parts, others)
-    ]
-    summed = jnp.concatenate(summed, axis=2)
+    keep = lax.dynamic_index_in_dim(parts, odd, 1, keepdims=False)
+    return flat(half(keep.astype(jnp.float32) + other.astype(jnp.float32)))
+
+
+def scatter_far(value):
     return lax.psum_scatter(
-        summed.reshape(-1, summed.shape[2]),
-        "dp",
-        scatter_dimension=0,
-        tiled=True,
-        axis_index_groups=far_groups(),
+        value, "dp", scatter_dimension=0, tiled=True, axis_index_groups=far_groups()
     )
 
 
@@ -194,7 +180,7 @@
     return mine + 1 - 2 * (mine % 2)
 
 
-def meet(everyone, carries):
+def meet(everyone, neighbour):
     barrier = pltpu.get_barrier_semaphore()
     if everyone:
         others = [
@@ -205,7 +191,7 @@
     else:
         _, near, far, _ = row_peers()
         others = [{"tensor": near}, {"tensor": far}]
-        if carries:
+        if neighbour:
             others.append({"dp": dp_neighbour()})
     for other in others:
         pl.semaphore_signal(barrier, inc=1, device_id=other, device_id_type=MESH)
@@ -213,12 +199,12 @@
 
 
 def remote_call(
-    kernel, name, number, operands, outs, scratch, carry=(), everyone=False, after=()
+    kernel, name, number, operands, outs, scratch, carry=(), everyone=False, neighbour=False, after=()
 ):
-    copies = sum(1 if len(array.shape) == 2 else array.shape[0] for array in carry)
-    swapped = [
+    copies = sum(array.shape[0] if len(array.shape) == 4 else 1 for array in carry)
+    traded = [
         jax.ShapeDtypeStruct(
-            array.shape if len(array.shape) == 2 else (array.shape[0], *array.shape[2:]),
+            (array.shape[0], *array.shape[2:]) if len(array.shape) == 4 else array.shape,
             array.dtype,
         )
         for array in carry
@@ -231,7 +217,7 @@
         del refs[: len(after)]
         results = [refs.pop(0) for _ in outs]
         targets = [refs.pop(0) for _ in carry]
-        meet(everyone, bool(carry))
+        meet(everyone, neighbour or bool(carry))
         started = []
         if carry:
             sems = refs.pop()
@@ -263,7 +249,7 @@
     anywhere = pl.BlockSpec(memory_space=pl.ANY)
     return pl.pallas_call(
         run,
-        out_shape=[*outs, *swapped],
+        out_shape=[*outs, *traded],
         in_specs=[whole] * len(operands) + [anywhere] * (len(carry) + len(after)),
         out_specs=[whole] * len(outs) + [anywhere] * len(carry),
         scratch_shapes=[
@@ -273,6 +259,7 @@
         compiler_params=pltpu.CompilerParams(
             collective_id=number, has_side_effects=True, vmem_limit_bytes=60 * 1024 * 1024
         ),
+        cost_estimate=pl.CostEstimate(flops=1 << 20, bytes_accessed=1 << 20, transcendentals=0),
         name=name,
     )(*operands, *carry, *after)
 
@@ -367,45 +354,55 @@
 def sum_blocks(partial, finish, work, sems):
     mine, near, far, both = row_peers()
     send_both, send_near, near_both, near_own, send_far, far_own, base = work
-    chunks = chunk_rows(base.shape[0])
-
-    def keep(columns, value):
-        base[:, columns] = value
-
-    def to_both(columns, value):
-        send_both[:, columns] = half(value)
-
-    def to_near(columns, value):
-        send_near[:, columns] = half(value)
-
-    partial(both, to_both)
-    first = remote(send_both, near_both, sems, 0, near)
-    first.start()
-    partial(far, keep)
-    first.wait()
+    size = base.shape[0] // 2
+    chunks = chunk_rows(size)
+
+    def terms(block, rows):
+        start = pl.multiple_of((block % 2) * size + rows.start, size // CHUNKS)
+        return base[pl.ds(start, size // CHUNKS), :]
+
+    def hand_over(block, source, target, kind):
+        copies = []
+        for i, rows in enumerate(chunks):
+            source[rows, :] = half(terms(block, rows))
+            copies.append(
+                remote(source.at[rows], target.at[rows], sems, CHUNKS * kind + i, near)
+            )
+            copies[i].start()
+        return copies
+
+    partial(far // 2, base)
     across = []
-    for i, rows in enumerate(chunks):
-        send_far[rows, :] = half(base[rows, :] + near_both[rows, :].astype(jnp.float32))
-        across.append(remote(send_far.at[rows], far_own.at[rows], sems, 2 + i, far))
+    for i, copy in enumerate(hand_over(both, send_both, near_both, 0)):
+        rows = chunks[i]
+        copy.wait()
+        send_far[rows, :] = half(terms(far, rows) + near_both[rows, :].astype(jnp.float32))
+        across.append(remote(send_far.at[rows], far_own.at[rows], sems, 2 * CHUNKS + i, far))
         across[i].start()
-    partial(near, to_near)
-    second = remote(send_near, near_own, sems, 1, near)
-    second.start()
-    partial(mine, keep)
-    second.wait()
-    for i, rows in enumerate(chunks):
+    partial(mine // 2, base)
+    for i, copy in enumerate(hand_over(near, send_near, near_own, 1)):
+        rows = chunks[i]
+        copy.wait()
         across[i].wait()
         finish(
+            i,
             rows,
-            base[rows, :]
+            terms(mine, rows)
             + near_own[rows, :].astype(jnp.float32)
             + far_own[rows, :].astype(jnp.float32),
         )
 
 
+SUM_SEMAPHORES = 3 * CHUNKS
+
+
+def chip_rows(chip, size):
+    return pl.ds(pl.multiple_of(chip * 2 * size, 2 * size), 2 * size)
+
+
 def sum_scratch(rows, columns):
     narrow = pltpu.VMEM((rows, columns), jnp.bfloat16)
-    return [narrow] * 6 + [pltpu.VMEM((rows, columns), jnp.float32)]
+    return [narrow] * 6 + [pltpu.VMEM((2 * rows, columns), jnp.float32)]
 
 
 class Spread:
@@ -450,10 +447,31 @@
     return run
 
 
-def enter_kernel(latents, scale, gain, gathered, sems):
+def pick(chooser, factor, which, rows):
+    width = factor.shape[1] // 4
+    return jnp.dot(
+        chooser[rows, :],
+        factor[:, which * width : (which + 1) * width],
+        precision=HIGH,
+        preferred_element_type=jnp.float32,
+    )
+
+
+def add_up(place, target, value):
+    target[place] += jnp.sum(value.reshape(-1, 8, value.shape[1]), axis=0)
+
+
+def add_images(choose, i, place, target, value):
+    target[place] += jnp.dot(
+        choose[i], value, precision=HIGH, preferred_element_type=jnp.float32
+    )
+
+
+def enter_kernel(latents, factor, chooser, gain, gathered, sems):
     share = Spread(gathered, sems, 0)
     for i, rows in enumerate(share.chunks):
-        share.offer(i, enter_point(latents[rows, :].astype(jnp.float32), scale[rows, :], gain[0:1]))
+        scale = pick(chooser, factor, 0, rows)
+        share.offer(i, enter_point(latents[rows, :].astype(jnp.float32), scale, gain[0:1]))
     share.settle()
 
 
@@ -461,178 +479,234 @@
     work, sems = rest[:-1], rest[-1]
     local = total.shape[0]
 
-    def partial(block, store):
-        rows = pl.ds(pl.multiple_of(block * local, local), local)
+    def partial(chip, base):
+        rows = chip_rows(chip, local)
 
         @tiles_of(captions.shape[0], 512)
         def _(columns):
-            store(columns, dot(weight[rows, :], captions[columns, :], 1, 1))
-
-    def finish(rows, value):
+            base[:, columns] = dot(weight[rows, :], captions[columns, :], 1, 1)
+
+    def finish(i, rows, value):
         total[rows, :] = value
 
     sum_blocks(partial, finish, work, sems)
 
 
+def transposed_partial(left, weight, lhs, size):
+    def partial(chip, base):
+        lhs[...] = half(left[:, chip_rows(chip, size)].astype(jnp.float32).T)
+
+        @tiles_of(weight.shape[0], 512)
+        def _(columns):
+            base[:, columns] = dot(lhs[...], weight[columns, :], 1, 1)
+
+    return partial
+
+
 def attention_out_kernel(
-    mixed, weight, latents, gate, scale, gain, summed, middle, gathered, *rest
+    mixed, weight, latents, factor, chooser, gain, summed, middle, gathered, *rest
 ):
     lhs, work, sems = rest[0], rest[1:-1], rest[-1]
-    size = latents.shape[0]
-
-    def partial(block, store):
-        own = pl.ds(pl.multiple_of(block * size, size), size)
-        lhs[...] = mixed[:, own].astype(jnp.float32).T.astype(jnp.bfloat16)
-
-        @tiles_of(weight.shape[0], 512)
-        def _(columns):
-            store(columns, dot(lhs[...], weight[columns, :], 1, 1))
-
-    share = Spread(gathered, sems, 2 + CHUNKS)
-
-    def finish(rows, value):
+    share = Spread(gathered, sems, SUM_SEMAPHORES)
+
+    def finish(i, rows, value):
         summed[rows, :] = value
         middle[rows, :], out = middle_point(
             value,
             latents[rows, :].astype(jnp.float32),
-            gate[rows, :],
-            scale[rows, :],
+            pick(chooser, factor, 1, rows),
+            pick(chooser, factor, 2, rows),
             gain[1:2],
             gain[2:3],
         )
-        share.offer(share.chunks.index(rows), out)
-
-    sum_blocks(partial, finish, work, sems)
+        share.offer(i, out)
+
+    sum_blocks(transposed_partial(mixed, weight, lhs, latents.shape[0]), finish, work, sems)
     share.settle()
 
 
 def feed_kernel(
-    inputs, feed, down, middle, gate, cotangent, gain, gate_up, hidden, summed, out, gathered, *rest
+    inputs, feed, down, middle, factor, chooser, choose, cotangent, gain,
+    gate_up, hidden, out, factor_grad, row_grad, gathered, *rest
 ):
     work, sems = rest[:-1], rest[-1]
     size = middle.shape[0]
     units = hidden.shape[1]
-
-    def partial(block, store):
-        own = pl.ds(pl.multiple_of(block * size, size), size)
-
-        @tiles_of(units, 256)
+    factor_grad[...] = jnp.zeros_like(factor_grad)
+    row_grad[...] = jnp.zeros_like(row_grad)
+
+    def partial(chip, base):
+        own = chip_rows(chip, size)
+
+        @tiles_of(units, 512)
         def _(columns):
-            start = pl.multiple_of(columns.start + units, 256)
+            other = pl.ds(pl.multiple_of(columns.start + units, 512), 512)
             first = dot(inputs[own, :], feed[:, columns], 1, 0)
-            second = dot(inputs[own, :], feed[:, pl.ds(start, 256)], 1, 0)
+            second = dot(inputs[own, :], feed[:, other], 1, 0)
             gate_up[own, columns] = first
-            gate_up[own, pl.ds(start, 256)] = second
+            gate_up[own, other] = second
             hidden[own, columns] = half(first * jax.nn.sigmoid(first) * second)
 
         @tiles_of(down.shape[0], 512)
         def _(columns):
-            store(columns, dot(hidden[own, :], down[columns, :], 1, 1))
-
-    share = Spread(gathered, sems, 2 + CHUNKS)
-
-    def finish(rows, value):
-        summed[rows, :] = value
-        out[rows, :], back = end_point(
-            value, middle[rows, :], gate[rows, :], cotangent[rows, :], gain[3:4]
-        )
-        share.offer(share.chunks.index(rows), back)
+            base[:, columns] = dot(hidden[own, :], down[columns, :], 1, 1)
+
+    share = Spread(gathered, sems, SUM_SEMAPHORES)
+
+    def finish(i, rows, value):
+        out[rows, :], back, gate_grad, row = end_point(
+            value,
+            middle[rows, :],
+            pick(chooser, factor, 3, rows),
+            cotangent[rows, :],
+            gain[3:4],
+        )
+        share.offer(i, back)
+        add_images(choose, i, 0, factor_grad, gate_grad)
+        add_up(0, row_grad, row)
 
     sum_blocks(partial, finish, work, sems)
     share.settle()
 
 
 def feed_back_kernel(
-    back, gate_up, feed, down, summed, middle, gate, scale, cotangent, gain,
-    pair, input_grad, middle_grad, gathered, *rest
+    back, gate_up, feed, down, summed, middle, factor, chooser, choose, cotangent, gain,
+    pair, middle_grad, factor_grad, row_grad, gathered, *rest
 ):
     work, sems = rest[:-1], rest[-1]
     size = middle.shape[0]
     units = down.shape[1]
-
-    def partial(block, store):
-        own = pl.ds(pl.multiple_of(block * size, size), size)
-
-        @tiles_of(units, 256)
+    factor_grad[...] = jnp.zeros_like(factor_grad)
+    row_grad[...] = jnp.zeros_like(row_grad)
+
+    def partial(chip, base):
+        own = chip_rows(chip, size)
+
+        @tiles_of(units, 512)
         def _(columns):
-            other = pl.ds(pl.multiple_of(columns.start + units, 256), 256)
+            other = pl.ds(pl.multiple_of(columns.start + units, 512), 512)
             grad = dot(back[own, :], down[:, columns], 1, 0)
             first, second = gate_up[own, columns], gate_up[own, other]
             pair[own, columns], pair[own, other] = pair_point(grad, first, second)
 
-        @tiles_of(feed.shape[0], 256)
+        @tiles_of(feed.shape[0], 512)
         def _(columns):
-            store(columns, dot(pair[own, :], feed[columns, :], 1, 1))
-
-    share = Spread(gathered, sems, 2 + CHUNKS)
-
-    def finish(rows, value):
-        input_grad[rows, :] = value
-        middle_grad[rows, :], out = middle_back_point(
-            value,
-            summed[rows, :],
-            middle[rows, :],
-            gate[rows, :],
-            scale[rows, :],
-            cotangent[rows, :],
-            gain[1:2],
-            gain[2:3],
-        )
-        share.offer(share.chunks.index(rows), out)
+            base[:, columns] = dot(pair[own, :], feed[columns, :], 1, 1)
+
+    share = Spread(gathered, sems, SUM_SEMAPHORES)
+
+    def finish(i, rows, value):
+        middle_grad[rows, :], out, gate_grad, scale_grad, first_row, second_row = (
+            middle_back_point(
+                value,
+                summed[rows, :],
+                middle[rows, :],
+                pick(chooser, factor, 1, rows),
+                pick(chooser, factor, 2, rows),
+                cotangent[rows, :],
+                gain[1:2],
+                gain[2:3],
+            )
+        )
+        share.offer(i, out)
+        add_images(choose, i, 0, factor_grad, gate_grad)
+        add_images(choose, i, 1, factor_grad, scale_grad)
+        add_up(0, row_grad, first_row)
+        add_up(1, row_grad, second_row)
 
     sum_blocks(partial, finish, work, sems)
     share.settle()
 
 
-def text_kernel(own, captions, grad, gathered, *rest):
-    (sems,) = rest
+def enter_back_kernel(
+    triple, weight, latents, factor, chooser, choose, middle_grad, gain,
+    latent_grad, factor_grad, row_grad, *rest
+):
+    lhs, work, sems = rest[0], rest[1:-1], rest[-1]
+    factor_grad[...] = jnp.zeros_like(factor_grad)
+    row_grad[...] = jnp.zeros_like(row_grad)
+
+    def finish(i, rows, value):
+        latent_grad[rows, :], scale_grad, row = enter_back_point(
+            value,
+            latents[rows, :].astype(jnp.float32),
+            pick(chooser, factor, 0, rows),
+            middle_grad[rows, :],
+            gain[0:1],
+        )
+        add_images(choose, i, 0, factor_grad, scale_grad)
+        add_up(0, row_grad, row)
+
+    sum_blocks(transposed_partial(triple, weight, lhs, latents.shape[0]), finish, work, sems)
+
+
+def text_kernel(own, captions, summed, gathered, kept, sent, arrived, sems):
     mine, near, far, both = row_peers()
-    share = Spread(gathered, sems, 0)
-    local = own.shape[0]
-    size = local // CHUNKS
-
-    def work(block, i):
-        rows = pl.ds(pl.multiple_of(block * local + i * size, 16), size)
-        grad[rows, :] = half(dot(gathered[block, share.chunks[i], :], captions[...], 1, 0))
-
-    for i, rows in enumerate(share.chunks):
-        share.offer(i, own[rows, :])
-    for i in range(CHUNKS):
-        work(mine, i)
-    for i in range(CHUNKS):
-        share.copy(near, i, 1, near).wait_recv()
-        work(near, i)
-    for i in range(CHUNKS):
-        share.copy(far, i, 0, far).wait_recv()
-        forward = share.copy(far, i, 2, near)
-        forward.start()
-        share.started.append(forward)
-        work(far, i)
-        if i:
-            share.copy(both, i - 1, 2, near).wait_recv()
-            work(both, i - 1)
-    share.copy(both, CHUNKS - 1, 2, near).wait_recv()
-    work(both, CHUNKS - 1)
-    for copy in share.started:
+    other = dp_neighbour()
+    odd = 1 - other % 2
+    size = own.shape[0] // CHUNKS
+    each = CHUNKS // 2
+    started = []
+
+    def part(k):
+        base = (1 - odd) if k < each else odd
+        return pl.ds(pl.multiple_of((base * each + k % each) * size, size), size)
+
+    def move(block, k, kind, device):
+        rows = gathered.at[block, part(k)]
+        return remote(rows, rows, sems, CHUNKS * kind + k, device)
+
+    def across(block, order, k):
+        rows = pl.ds(k * size, size)
+        return pltpu.make_async_remote_copy(
+            src_ref=sent.at[block, rows],
+            dst_ref=arrived.at[block, rows],
+            send_sem=sems.at[0, 3 * CHUNKS + order * each + k],
+            recv_sem=sems.at[1, 3 * CHUNKS + order * each + k],
+            device_id={"dp": other},
+            device_id_type=MESH,
+        )
+
+    def begin(copy):
+        copy.start()
+        started.append(copy)
+
+    def work(block, order, k):
+        value = dot(gathered[block, part(k), :], captions[...], 1, 0)
+        rows = pl.ds((k % each) * size, size)
+        if k < each:
+            sent[block, rows, :] = half(value)
+            begin(across(block, order, k))
+        else:
+            kept[block, rows, :] = value
+
+    for k in range(CHUNKS):
+        gathered[mine, part(k), :] = own[part(k), :]
+        begin(move(mine, k, 0, far))
+        begin(move(mine, k, 1, near))
+    for k in range(CHUNKS):
+        work(mine, 0, k)
+    for k in range(CHUNKS):
+        move(near, k, 1, near).wait_recv()
+        work(near, 1, k)
+    for k in range(CHUNKS):
+        move(far, k, 0, far).wait_recv()
+        begin(move(far, k, 2, near))
+        work(far, 2, k)
+        if k:
+            move(both, k - 1, 2, near).wait_recv()
+            work(both, 3, k - 1)
+    move(both, CHUNKS - 1, 2, near).wait_recv()
+    work(both, 3, CHUNKS - 1)
+    for order, block in enumerate((mine, near, far, both)):
+        for k in range(each):
+            across(block, order, k).wait_recv()
+            rows = pl.ds(k * size, size)
+            summed[block, rows, :] = half(
+                kept[block, rows, :] + arrived[block, rows, :].astype(jnp.float32)
+            )
+    for copy in started:
         copy.wait_send()
-
-
-def enter_back_kernel(triple, weight, total, *rest):
-    lhs, work, sems = rest[0], rest[1:-1], rest[-1]
-    size = total.shape[0]
-
-    def partial(block, store):
-        own = pl.ds(pl.multiple_of(block * size, size), size)
-        lhs[...] = triple[:, own].astype(jnp.float32).T.astype(jnp.bfloat16)
-
-        @tiles_of(weight.shape[0], 512)
-        def _(columns):
-            store(columns, dot(lhs[...], weight[columns, :], 1, 1))
-
-    def finish(rows, value):
-        total[rows, :] = value
-
-    sum_blocks(partial, finish, work, sems)
 
 
 def enter_point(source, scale, gain):
@@ -649,8 +723,14 @@
 def end_point(summed, middle, gate, cotangent, gain):
     normed, inverse = rms_parts(summed)
     turned = jnp.tanh(gate)
-    out = middle + turned * (normed * gain)
-    return (out, half(rms_back(normed, inverse, turned * cotangent * gain)))
+    branch = normed * gain
+    grad = turned * cotangent
+    return (
+        middle + turned * branch,
+        half(rms_back(normed, inverse, grad * gain)),
+        cotangent * branch * (1.0 - turned * turned),
+        grad * normed,
+    )
 
 
 def pair_point(grad, first, second):
@@ -665,12 +745,30 @@
     input_grad, summed, middle, gate, scale, cotangent, first_gain, second_gain
 ):
     normed, inverse = rms_parts(middle)
-    middle_grad = cotangent + rms_back(
-        normed, inverse, input_grad * second_gain * (1.0 + scale)
-    )
+    gained = input_grad * (1.0 + scale)
+    middle_grad = cotangent + rms_back(normed, inverse, gained * second_gain)
+    scale_grad, second_row = input_grad * normed * second_gain, gained * normed
     normed, inverse = rms_parts(summed)
-    back = jnp.tanh(gate) * middle_grad * first_gain
-    return (middle_grad, half(rms_back(normed, inverse, back)))
+    turned = jnp.tanh(gate)
+    branch = turned * middle_grad
+    return (
+        middle_grad,
+        half(rms_back(normed, inverse, branch * first_gain)),
+        middle_grad * (normed * first_gain) * (1.0 - turned * turned),
+        scale_grad,
+        branch * normed,
+        second_row,
+    )
+
+
+def enter_back_point(input_grad, source, scale, middle_grad, gain):
+    normed, inverse = rms_parts(source)
+    gained = input_grad * (1.0 + scale)
+    return (
+        middle_grad + rms_back(normed, inverse, gained * gain),
+        input_grad * normed * gain,
+        gained * normed,
+    )
 
 
 def spans(heads):
@@ -766,7 +864,8 @@
     cosine_all,
     sine_all,
     raw_query,
-    raw_rest,
+    raw_key,
+    raw_value,
     query,
     key,
     key_rows,
@@ -781,11 +880,11 @@
     @pl.when(pl.program_id(0) == 0)
     def _():
         for head, span in enumerate(spans(heads)):
-            normed, _ = head_norm(raw_rest[span, :])
+            normed, _ = head_norm(raw_key[span, :])
             turned = turn(normed * gain[span, 1:2], cosine_all[...], sine_all[...])
             key[span, :] = half(turned)
             key_rows[head] = half(turned.T)
-            plain = raw_rest[local + head * HEAD : local + (head + 1) * HEAD, :]
+            plain = raw_value[span, :]
             value[span, :] = half(plain)
             value_rows[head] = half(plain.T)
 
@@ -994,6 +1093,9 @@
 def attention_call(kernel, name, scalars, operands, outs, scratch, tokens, weight, after=()):
     def block(array, tiled):
         lead = array.shape[:-1]
+        if tiled is not True and tiled is not False:
+            third = (lead[0] // 3, tokens if tiled else TILE)
+            return pl.BlockSpec(third, lambda i, *_: (tiled, 0) if tiled else (0, i))
         if tiled:
             return pl.BlockSpec((*lead, TILE), lambda i, *_: (*([0] * len(lead)), i))
         return pl.BlockSpec(array.shape, lambda i, *_: (0,) * len(array.shape))
@@ -1087,9 +1189,8 @@
     key_line = gather_far(caption_half[0].T)
     value_line = gather_far(caption_half[1].T)
     in_half = half(attention_in)
-    attention_line = gather_far(
-        jnp.concatenate([in_half[0], in_half[1], in_half[2], half(attention_out).T], axis=1)
-    )
+    attention_line = gather_far(jnp.concatenate([in_half[0], in_half[1], in_half[2]], axis=1))
+    out_own = half(attention_out).T
     down_line = gather_far(half(feed_out).T)
     feed_half = half(feed_in)
     feed_own = jnp.concatenate([feed_half[0], feed_half[1]], axis=1)
@@ -1109,17 +1210,17 @@
         ],
         axis=1,
     )
-    received, feed_other = remote_call(
+    received, out_other = remote_call(
         spread_kernel,
         "modulation_exchange",
         0,
         [payload],
         [jax.ShapeDtypeStruct((tensor_size, *payload.shape), jnp.float32)],
         exchange_scratch([payload.shape]),
-        [feed_own],
+        [out_own],
         everyone=True,
     )
-    feed_full = gather_far(near_pair(feed_own, feed_other))
+    out_full = gather_far(join_near(out_own, out_other, rows))
     factor_row = jnp.transpose(received[:, :, :per_row], (2, 1, 0, 3)).reshape(per_row, -1)
     gains = received[0, :, per_row:].reshape(dp_size, 8, -1)
     gains = jnp.transpose(gains, (1, 0, 2)).reshape(8, width)
@@ -1127,15 +1228,17 @@
     chooser = (own_ids[:, None] == jnp.arange(per_row, dtype=jnp.int32)[None, :]).astype(
         jnp.float32
     )
-    token_factor = jnp.dot(chooser, factor_row, precision=HIGH)
-    scale_attn = token_factor[:, :width]
-    gate_attn = token_factor[:, width : 2 * width]
-    scale_feed = token_factor[:, 2 * width : 3 * width]
-    gate_feed = token_factor[:, 3 * width :]
+    choose = jnp.transpose(chooser.reshape(CHUNKS, -1, per_row), (0, 2, 1))
+
+    def token_factor(which):
+        return pick(chooser, factor_row, which, slice(None))
 
     def split(value):
         return [value[i * shard_rows : (i + 1) * shard_rows] for i in range(tensor_size)]
 
+    def by_image(*grads):
+        return jnp.stack([jnp.dot(chooser.T, grad, precision=HIGH) for grad in grads])
+
     f32, bf16 = jnp.float32, jnp.bfloat16
 
     def shape(dims, dtype=f32):
@@ -1147,9 +1250,8 @@
     def semaphores(count):
         return pltpu.SemaphoreType.DMA((2, count))
 
-    sum_sems, all_sems = semaphores(2 + CHUNKS), semaphores(2 + 4 * CHUNKS)
+    sum_sems, all_sems = semaphores(SUM_SEMAPHORES), semaphores(SUM_SEMAPHORES + 3 * CHUNKS)
     source = latents.astype(f32)
-    attn_norm, attn_inv = rms_parts(source)
 
     def caption_project(weight, carry, number):
         if fused:
@@ -1160,7 +1262,7 @@
                 [weight, captions],
                 [shape((local, slots))],
                 [*sum_scratch(local, slots), sum_sems],
-                [carry],
+                carry,
             )
         total = collect(
             [
@@ -1170,32 +1272,31 @@
                 for i in range(tensor_size)
             ]
         )
-        return (total, near_swap(carry))
+        return (total, *(near_swap(array) for array in carry))
 
     if fused:
         attn_full, key_other = remote_call(
             enter_kernel,
             "enter",
             3,
-            [latents, scale_attn, gains],
+            [latents, factor_row, chooser, gains],
             [gathered],
             [semaphores(3 * CHUNKS)],
             [key_line],
         )
         attn_full = attn_full.reshape(row_tokens, width)
     else:
-        attn_full = in_place(spread(enter_point(source, scale_attn, gains[0])))
+        attn_full = in_place(spread(enter_point(source, token_factor(0), gains[0])))
         key_other = near_swap(key_line)
-    text_key_raw, value_other = caption_project(
-        join_near(key_line, key_other, rows), value_line, 4
-    )
+    text_key_raw, value_other, feed_other = caption_project(
+        join_near(key_line, key_other, rows), [value_line, feed_own], 4
+    )
+    feed_full = gather_far(join_near(feed_own, feed_other, rows))
     text_value_raw, attention_other = caption_project(
-        join_near(value_line, value_other, rows), attention_line, 11
-    )
-    in_full = join_near(attention_line, attention_other, rows, 0, 3 * local)
-    out_full = join_near(attention_line, attention_other, rows, 3 * local)
+        join_near(value_line, value_other, rows), [attention_line], 11
+    )
+    in_full = join_near(attention_line, attention_other, rows)
     projected = dot(in_full, attn_full, 0, 1)
-    raw_query, raw_rest = projected[:local], projected[local:]
     cosine, sine = rope_tables(rope_rows[0], rope_cols[0])
 
     tiles = row_tokens // TILE
@@ -1227,8 +1328,9 @@
             (ids_column, False),
             (local_gains, False),
             *tables,
-            (raw_query, True),
-            (raw_rest, False),
+            (projected, 0),
+            (projected, 1),
+            (projected, 2),
         ],
         [
             (narrow, True),
@@ -1272,23 +1374,34 @@
             attention_out_kernel,
             "attention_out",
             5,
-            [mixed, out_full, latents, gate_attn, scale_feed, norm_gains],
+            [mixed, out_full, latents, factor_row, chooser, norm_gains],
             [shape((shard_rows, width)), shape((shard_rows, width)), gathered],
-            [pltpu.VMEM((shard_rows, local), bf16), *in_kernel, all_sems],
+            [pltpu.VMEM((2 * shard_rows, local), bf16), *in_kernel, all_sems],
             [down_line],
         )
         feed_all = feed_all.reshape(row_tokens, width)
         down_full = join_near(down_line, down_other, rows)
-        gate_up, hidden, feed_sum, block_out, feed_sum_grad = remote_call(
+        gate_up, hidden, block_out, end_factor, end_row, feed_sum_grad = remote_call(
             feed_kernel,
             "feed_forward",
             6,
-            [feed_all, feed_full, down_full, middle, gate_feed, cotangent, norm_gains],
+            [
+                feed_all,
+                feed_full,
+                down_full,
+                middle,
+                factor_row,
+                chooser,
+                choose,
+                cotangent,
+                norm_gains,
+            ],
             [
                 shape((row_tokens, 2 * units)),
                 shape((row_tokens, units), bf16),
                 shape((shard_rows, width)),
-                shape((shard_rows, width)),
+                shape((1, per_row, width)),
+                shape((1, 8, width)),
                 gathered,
             ],
             [*in_kernel, all_sems],
@@ -1307,21 +1420,29 @@
             ]
         )
         middle, feed_block = middle_point(
-            attn_sum, source, gate_attn, scale_feed, gains[1], gains[2]
+            attn_sum, source, token_factor(1), token_factor(2), gains[1], gains[2]
         )
         feed_all = in_place(spread(feed_block))
         down_full = join_near(down_line, near_swap(down_line), rows)
         gate_up = dot(feed_all, feed_full, 1, 0)
         hidden = half(jax.nn.silu(gate_up[:, :units]) * gate_up[:, units:])
         feed_sum = collect(split(dot(hidden, down_full, 1, 1)))
-        block_out, feed_block_grad = end_point(
-            feed_sum, middle, gate_feed, cotangent, gains[3]
-        )
+        block_out, feed_block_grad, *grads = end_point(
+            feed_sum, middle, token_factor(3), cotangent, gains[3]
+        )
+        end_factor, end_row = by_image(grads[0]), grads[1][None]
         feed_sum_grad = in_place(spread(feed_block_grad))
     feed_out_grad = half(dot(feed_sum_grad, hidden, 0, 0))
     feed_out_parts = feed_out_grad.reshape(dp_size // 2, 2, -1, units)
     if fused:
-        pair_grad, feed_input_grad, middle_grad, attn_sum_grad, feed_out_other = remote_call(
+        (
+            pair_grad,
+            middle_grad,
+            middle_factor,
+            middle_row,
+            attn_sum_grad,
+            feed_out_other,
+        ) = remote_call(
             feed_back_kernel,
             "feed_backward",
             7,
@@ -1332,15 +1453,17 @@
                 down_full,
                 attn_sum,
                 middle,
-                gate_attn,
-                scale_feed,
+                factor_row,
+                chooser,
+                choose,
                 cotangent,
                 norm_gains,
             ],
             [
                 shape((row_tokens, 2 * units), bf16),
                 shape((shard_rows, width)),
-                shape((shard_rows, width)),
+                shape((2, per_row, width)),
+                shape((2, 8, width)),
                 gathered,
             ],
             [*in_kernel, all_sems],
@@ -1353,24 +1476,25 @@
             pair_point(hidden_grad, gate_up[:, :units], gate_up[:, units:]), axis=1
         )
         feed_input_grad = collect(split(dot(pair_grad, feed_full, 1, 1)))
-        middle_grad, attn_block_grad = middle_back_point(
+        middle_grad, attn_block_grad, *grads = middle_back_point(
             feed_input_grad,
             attn_sum,
             middle,
-            gate_attn,
-            scale_feed,
+            token_factor(1),
+            token_factor(2),
             cotangent,
             gains[1],
             gains[2],
         )
+        middle_factor, middle_row = by_image(*grads[:2]), jnp.stack(grads[2:])
         attn_sum_grad = in_place(spread(attn_block_grad))
         feed_out_other = swap_half(feed_out_parts)
-    feed_out_sum = scatter_far((feed_out_parts,), (feed_out_other,))
-    feed_in_grad = half(dot(feed_all, pair_grad, 0, 0))
-    feed_in_both = lax.psum_scatter(
-        feed_in_grad, "dp", scatter_dimension=0, tiled=True, axis_index_groups=far_groups()
-    )
-    mixed_grad = dot(out_full, gate(attn_sum_grad, feed_in_grad), 0, 1)
+    feed_out_sum = scatter_far(sum_half(feed_out_parts, feed_out_other))
+    outer_grad = half(dot(feed_all, pair_grad, 0, 0))
+    outer_both = lax.psum_scatter(
+        outer_grad, "dp", scatter_dimension=0, tiled=True, axis_index_groups=far_groups()
+    )
+    mixed_grad = dot(out_full, gate(attn_sum_grad, outer_grad), 0, 1)
     out_parts = half(dot(attn_sum_grad, mixed, 0, 1)).reshape(dp_size // 2, 2, -1, local)
     query_two, text_key_grad, text_value_grad, text_gains = attention_call(
         functools.partial(cross_backward_kernel, heads),
@@ -1416,8 +1540,8 @@
             (own_out, True),
             (mixed_grad, True),
             (query_two, True),
-            (raw_query, True),
-            (raw_rest[:local], False),
+            (projected, 0),
+            (projected, 1),
         ],
         [
             (jax.ShapeDtypeStruct((3 * local, row_tokens), jnp.bfloat16), False),
@@ -1437,40 +1561,28 @@
     )
     in_parts = half(dot(attn_full, triple_grad, 0, 1)).reshape(dp_size // 2, 2, -1, 3 * local)
 
-    def caption_back(grad, carry, after=()):
-        if fused:
-            grad, _, *others = remote_call(
-                text_kernel,
-                f"text_gradient_{len(carry)}",
-                7 + len(carry),
-                [grad, captions],
-                [
-                    shape((tensor_size * local, captions.shape[1]), bf16),
-                    shape((tensor_size, local, slots), bf16),
-                ],
-                [semaphores(3 * CHUNKS)],
-                carry,
-                after=after,
-            )
-        else:
-            grad = half(dot(in_place(spread(grad)), captions, 1, 0))
-            others = [swap_half(parts) for parts in carry]
-        return (grad.reshape(dp_size // 2, 2, -1, captions.shape[1]), *others)
-
-    value_parts, in_other, out_other = caption_back(text_value_grad, [in_parts, out_parts])
-    attention_sum = scatter_far((in_parts, out_parts), (in_other, out_other))
-    key_parts, value_other = caption_back(text_key_grad, [value_parts], [feed_in_both])
-    value_sum = scatter_far((value_parts,), (value_other,))
     if fused:
-        attn_input_grad, key_other = remote_call(
+        latent_grad, enter_factor, enter_row, in_other = remote_call(
             enter_back_kernel,
             "enter_backward",
             10,
-            [triple_grad, in_full],
-            [shape((shard_rows, width))],
-            [pltpu.VMEM((shard_rows, 3 * local), bf16), *in_kernel, sum_sems],
-            [key_parts],
-            after=[attention_sum],
+            [
+                triple_grad,
+                in_full,
+                latents,
+                factor_row,
+                chooser,
+                choose,
+                middle_grad,
+                norm_gains,
+            ],
+            [
+                shape((shard_rows, width)),
+                shape((1, per_row, width)),
+                shape((1, 8, width)),
+            ],
+            [pltpu.VMEM((2 * shard_rows, 3 * local), bf16), *in_kernel, sum_sems],
+            [in_parts],
         )
     else:
         attn_input_grad = collect(
@@ -1484,28 +1596,48 @@
                 for i in range(tensor_size)
             ]
         )
-        key_other = swap_half(key_parts)
-    key_sum = scatter_far((key_parts,), (key_other,))
-    in_sum, out_sum = attention_sum[:, : 3 * local], attention_sum[:, 3 * local :]
-    first_norm, _ = rms_parts(attn_sum)
-    feed_norm, _ = rms_parts(middle)
-    second_norm, _ = rms_parts(feed_sum)
-    tanh_attn, tanh_feed = jnp.tanh(gate_attn), jnp.tanh(gate_feed)
-    branch_attn_grad, branch_feed_grad = tanh_attn * middle_grad, tanh_feed * cotangent
-    gate_attn_grad = middle_grad * (first_norm * gains[1]) * (1.0 - tanh_attn * tanh_attn)
-    gate_feed_grad = cotangent * (second_norm * gains[3]) * (1.0 - tanh_feed * tanh_feed)
-    scale_feed_grad = feed_input_grad * feed_norm * gains[2]
-    scale_attn_grad = attn_input_grad * attn_norm * gains[0]
-    latent_grad = middle_grad + rms_back(
-        attn_norm, attn_inv, attn_input_grad * gains[0] * (1.0 + scale_attn)
-    )
-    shared_rows = jnp.stack(
-        [
-            jnp.sum(attn_input_grad * attn_norm * (1.0 + scale_attn), axis=0),
-            jnp.sum(branch_attn_grad * first_norm, axis=0),
-            jnp.sum(feed_input_grad * feed_norm * (1.0 + scale_feed), axis=0),
-            jnp.sum(branch_feed_grad * second_norm, axis=0),
-        ]
+        in_other = swap_half(in_parts)
+        latent_grad, *grads = enter_back_point(
+            attn_input_grad, source, token_factor(0), middle_grad, gains[0]
+        )
+        enter_factor, enter_row = by_image(grads[0]), grads[1][None]
+    in_sum = scatter_far(sum_half(in_parts, in_other))
+
+    columns = captions.shape[1]
+
+    def caption_back(grad, carry, number, after):
+        if not fused:
+            parts = half(dot(in_place(spread(grad)), captions, 1, 0))
+            parts = parts.reshape(dp_size // 2, 2, -1, columns)
+            return (sum_half(parts, swap_half(parts)), *(swap_half(array) for array in carry))
+        kept = (tensor_size, local // 2, columns)
+        summed, _, *others = remote_call(
+            text_kernel,
+            "text_gradient",
+            number,
+            [grad, captions],
+            [shape(kept, bf16), shape((tensor_size, local, slots), bf16)],
+            [
+                pltpu.VMEM(kept, f32),
+                pltpu.VMEM(kept, bf16),
+                pltpu.VMEM(kept, bf16),
+                semaphores(5 * CHUNKS),
+            ],
+            carry,
+            neighbour=True,
+            after=after,
+        )
+        return (flat(summed), *others)
+
+    value_grad, out_other = caption_back(text_value_grad, [out_parts], 8, [latent_grad])
+    value_sum = scatter_far(
+        jnp.concatenate([value_grad, sum_half(out_parts, out_other)], axis=1)
+    )
+    (key_grad,) = caption_back(text_key_grad, [], 9, [outer_both, value_grad])
+    key_sum = scatter_far(key_grad)
+    value_sum, out_sum = value_sum[:, :columns], value_sum[:, columns:]
+    shared_rows = jnp.sum(
+        jnp.concatenate([enter_row, middle_row, end_row]), axis=1
     )
     head_rows = jnp.stack(
         [own_gains[:, 0], own_gains[:, 128], text_gains[:, 128], text_gains[:, 0]]
@@ -1514,10 +1646,8 @@
         jnp.zeros((4, width), jnp.float32), head_rows, (jnp.zeros((), jnp.int32), offset)
     )
     channel_part = jnp.concatenate([shared_rows, head_full], axis=0)
-    factor_tokens = jnp.concatenate(
-        [scale_attn_grad, gate_attn_grad, scale_feed_grad, gate_feed_grad], axis=1
-    )
-    factor_image = jnp.dot(chooser.T, factor_tokens, precision=HIGH)
+    factor_image = jnp.concatenate([enter_factor, middle_factor, end_factor])
+    factor_image = jnp.transpose(factor_image, (1, 0, 2))
     factor_image = jnp.transpose(
         factor_image.reshape(per_row, dp_size, tensor_size, own_columns), (2, 1, 0, 3)
     )
@@ -1528,22 +1658,20 @@
         axis=2,
     )
     blocks = payload.shape[1:]
-    feed_in_parts = feed_in_both.reshape(1, 2, -1, 2 * units)
-    received, feed_in_other = remote_call(
+    outer_parts = outer_both.reshape(1, 2, -1, outer_both.shape[1])
+    received, outer_other = remote_call(
         return_kernel,
         "modulation_return",
         1,
         [payload],
         [shape(blocks)],
         exchange_scratch([payload.shape, blocks, blocks]),
-        [feed_in_parts],
+        [outer_parts],
         everyone=True,
-        after=[value_sum],
-    )
-    feed_in_sum = lax.dynamic_index_in_dim(
-        feed_in_parts, dp_index % 2, 1, keepdims=False
-    ).astype(f32) + feed_in_other.astype(f32)
-    feed_in_sum = feed_in_sum[0]
+        after=[in_sum],
+    )
+    feed_in_sum = lax.dynamic_index_in_dim(outer_parts, dp_index % 2, 1, keepdims=False)[0]
+    feed_in_sum = feed_in_sum.astype(f32) + outer_other[0].astype(f32)
     factor_grad = received[:, :per_row].reshape(images, own_columns)
     channel_sum = jnp.sum(received[:, per_row:], axis=0).reshape(channels.shape)
     modulator_sum = jnp.dot(augmented.astype(jnp.float32).T, factor_grad, precision=HIGH)

time: 837 us -> 792 us (0.946)
  Pallas kernels: 634 us -> 615 us
  other arithmetic: 81.4 us -> 63.4 us
  local copies, waits for them, and re-layouts: 42.3 us -> 30.9 us
  waiting for transfers between devices: 0.88 us -> 9.37 us
    pallas_call x12, Pallas kernels: 543 us -> 523 us  [remote_call(): pl.pallas_call(run, out_shape=[*outs, *traded], in_specs=[whole] * len(op...]
    reduce_sum x5 -> x1, other arithmetic: 8.75 us -> 0.06 us  [body(): jnp.sum(jnp.concatenate([enter_row, middle_row, end_row]), axis=1)]
    all_gather x5 -> x6, waiting for transfers between devices: 0.01 us -> 8.46 us  [gather_far(): lax.all_gather(value, 'dp', axis=0, tiled=True, axis_index_groups=far_gro...]
    unnamed x152 -> x131, local copies, waits for them, and re-layouts: 20.2 us -> 12.2 us
  transfers between devices with their start and end apart: 10 -> 11, of which waited for: 0 -> 1; matrix products, arithmetic and copies ran while one was open for 14% -> 11% of each run, Pallas kernels for 61% -> 63%
where the time goes in v3:
time: 792 us; the launch traced here: 784 us
  Pallas kernels  615 us (78%)
  other arithmetic  63.4 us (8%)
  matrix products  42.3 us (5%)
  local copies, waits for them, and re-layouts  30.9 us (4%)
  between operations  22.5 us (3%)
  waiting for transfers between devices  9.37 us (1%)
    pallas_call x12, Pallas kernels, remote_call(): pl.pallas_call(run, out_shape=[*outs, *traded], in_specs=[whole] * len(op...  523 us
    pallas_call x4, Pallas kernels, attention_call(): pl.pallas_call(run, grid_spec=pltpu.PrefetchScalarGridSpec(num_scalar_pre...  91.6 us
    dot_general x6, matrix products, dot(): lax.dot_general(left, right, (((left_dim,), (right_dim,)), ((), ())), pre...  40.5 us
    sub x7, other arithmetic, adamw(): weight - rate * (step_size + decay * weight)  17.8 us
  transfers between devices with their start and end apart: 11, of which 1 were waited for; matrix products, arithmetic and copies ran while one was open for 11% of the time, Pallas kernels for 63%

profile of v3, /device:TPU:0, one launch (start us, length us, event | category | flops | bytes accessed | tf_op | source)
XLA Modules:
  0.0 784.1 jit_solution(3355170259625075728)
XLA Ops:
  13.6 19.4 %modulation_exchange.1 = (f32[4,8,16,192]{3,2,1,0:T(8,128)}, bf16[192,384]{1,0:T(8,128)(2,1)}) custom-call(f32[8,16,192]{2,1,0:T(8,128)} %pad_maximum_fusion.10.refs_0_, bf16[192,384]{1,0:T(8,128)(2,1)} %convert_bitcast_fusion.3.refs_1_), custom_call_target="tpu_custom_call" | custom-call | flops 1048576 | bytes 1048576 | tf_op jit(solution)/shard_map/modulation_exchange/pallas_call | solution.py:250
  41.6 8.4 %all-gather.11.cloned.1.call-done.refs_4_ = bf16[768,1024]{1,0:T(8,128)(2,1)} async-done(((bf16[192,1024]{1,0:T(8,128)(2,1)}), bf16[768,1024]{1,0:T(8,128)(2,1)}) %all-gather.11.cloned.1.call-update) | async-done | bytes 1572880 | tf_op jit(solution)/shard_map/all_gather | solution.py:92
  50.0 40.6 %enter.1 = (bf16[4,256,1536]{2,1,0:T(8,128)(2,1)}, bf16[768,1024]{1,0:T(8,128)(2,1)}) custom-call(bf16[256,1536]{1,0:T(8,128)(2,1)} %refs_2_.7, f32[8,6144]{1,0:T(8,128)} %reshape.450.refs_1_.refs_3_.refs_4_.refs_6_, f32[256,8]{1,0:T(8,128)} %fusion.23.refs_2_.refs_4_.refs_5_.refs_7_, f32[8,1536]{1,0:T(8,128)} %reshape.451.refs_3_.refs_5_.refs_8_.refs_10_.refs_7_, ...), custom_call_target="tpu_custom_call" | custom-call | flops 1048576 | bytes 1048576 | tf_op jit(solution)/shard_map/enter/pallas_call | solution.py:250
  94.4 57.9 %project.2 = (f32[384,2048]{1,0:T(8,128)}, bf16[768,1024]{1,0:T(8,128)(2,1)}, bf16[192,2048]{1,0:T(8,128)(2,1)}) custom-call(bf16[1536,1024]{1,0:T(8,128)(2,1)} %bitcast.175, bf16[2048,1024]{1,0:T(8,128)(2,1)} %refs_1_.11, bf16[768,1024]{1,0:T(8,128)(2,1)} %all-gather.9.cloned.1.call-done.refs_2_, bf16[192,2048]{1,0:T(8,128)(2,1)} %pad_maximum_fusion.6.refs_3_), custom_call_target="tpu_custom_call" | custom-call | flops 1048576 | bytes 1048576 | tf_op jit(solution)/shard_map/project/pallas_call | solution.py:250
  166.4 48.5 %project.3 = (f32[384,2048]{1,0:T(8,128)}, bf16[768,1152]{1,0:T(8,128)(2,1)}) custom-call(bf16[1536,1024]{1,0:T(8,128)(2,1)} %bitcast.174, bf16[2048,1024]{1,0:T(8,128)(2,1)} %refs_1_.11, bf16[768,1152]{1,0:T(8,128)(2,1)} %all-gather.7.cloned.1.call-done.refs_2_), custom_call_target="tpu_custom_call" | custom-call | flops 1048576 | bytes 1048576 | tf_op jit(solution)/shard_map/project/pallas_call | solution.py:250
  219.8 5.6 fusion.46.refs_8_.refs_9_.refs_10_.refs_16_.refs_17_
  225.4 18.4 %self_forward.1 = (bf16[384,1024]{1,0:T(8,128)(2,1)}, bf16[384,1024]{1,0:T(8,128)(2,1)}, bf16[6,1024,64]{2,1,0:T(8,128)(2,1)}, bf16[6,1024,64]{2,1,0:T(8,128)(2,...) custom-call(s32[8]{0:T(128)} %reshape.449.refs_0_, s32[1,1024]{1,0:T(1,128)} %refs_1_.9, s32[1024,1]{1,0:T(8,128)} %copy.124.refs_2_, ...), custom_call_target="tpu_custom_call" | custom-call | flops 15000 | bytes 15000 | tf_op jit(solution)/shard_map/self_forward/pallas_call | solution.py:1108
  243.8 23.7 %cross_forward.1 = (bf16[384,2048]{1,0:T(8,128)(2,1)}, bf16[6,2048,64]{2,1,0:T(8,128)(2,1)}, bf16[6,2048,64]{2,1,0:T(8,128)(2,1)}, f32[384,1024]{1,0:T(8,128)}, ...) custom-call(s32[8]{0:T(128)} %reshape.447.refs_0_, s32[8]{0:T(128)} %bitcast.214, s32[1,1024]{1,0:T(1,128)} %refs_1_.9, ...), custom_call_target="tpu_custom_call" | custom-call | flops 18000 | bytes 18000 | tf_op jit(solution)/shard_map/cross_forward/pallas_call | solution.py:1108
  267.5 52.7 %attention_out.1 = (f32[256,1536]{1,0:T(8,128)}, f32[256,1536]{1,0:T(8,128)}, bf16[4,256,1536]{2,1,0:T(8,128)(2,1)}, bf16[768,1024]{1,0:T(8,128)(2,1)}) custom-call(bf16[384,1024]{1,0:T(8,128)(2,1)} %get-tuple-element.85.refs_0_, bf16[1536,384]{1,0:T(8,128)(2,1)} %all-gather.13.cloned.1.call-done.refs_1_, bf16[256,1536]{1,0:T(8,128)(2,1)} %refs_2_.7, ...), custom_call_target="tpu_custom_call" | custom-call | flops 1048576 | bytes 1048576 | tf_op jit(solution)/shard_map/attention_out/pallas_call | solution.py:250
  323.8 56.3 %feed_forward.1 = (f32[1024,2048]{1,0:T(8,128)}, bf16[1024,1024]{1,0:T(8,128)(2,1)}, f32[256,1536]{1,0:T(8,128)}, f32[1,8,1536]{2,1,0:T(8,128)}, f32[1,8,1536]{2,1,0:T(8,128)}, /*index=5*/bf16[4,256,1536]{2,1,0:T(8,128)(2,1)}) custom-call(bf16[1024,1536]{1,0:T(8,128)(2,1)} %bitcast.199, bf16[1536,2048]{1,0:T(8,128)(2,1)} %all-gather.17.cloned.1.call-done.refs_1_.refs_2_, ...), custom_call_target="tpu_custom_call" | custom-call | flops 1048576 | bytes 1048576 | tf_op jit(solution)/shard_map/feed_forward/pallas_call | solution.py:250
  380.1 7.6 convolution_convert_fusion.2
  387.7 58.0 %feed_backward.1 = (bf16[1024,2048]{1,0:T(8,128)(2,1)}, f32[256,1536]{1,0:T(8,128)}, f32[2,8,1536]{2,1,0:T(8,128)}, f32[2,8,1536]{2,1,0:T(8,128)}, bf16[4,256,15...) custom-call(bf16[1024,1536]{1,0:T(8,128)(2,1)} %bitcast.196, f32[1024,2048]{1,0:T(8,128)} %get-tuple-element.97.refs_1_, ...), custom_call_target="tpu_custom_call" | custom-call | flops 1048576 | bytes 1048576 | tf_op jit(solution)/shard_map/feed_backward/pallas_call | solution.py:250
  449.2 11.3 %convolution_convert_fusion.1.after = bf16[1536,2048]{1,0:T(8,128)(2,1)} fusion(bf16[1024,1536]{1,0:T(8,128)(2,1)} %bitcast.200, bf16[1024,2048]{1,0:T(8,128)(2,1)} %get-tuple-element.101), kind=kOutput, calls=%fused_computation.1 | convolution fusion | flops 6445596672 | bytes 13631488 | tf_op jit(solution)/shard_map/dot_general | solution.py:39
  462.4 4.1 convolution_convert_fusion.3
  467.7 4.5 fusion.47.refs_10_.refs_14_
  472.2 27.4 %cross_backward.1 = (f32[384,1024]{1,0:T(8,128)}, bf16[384,2048]{1,0:T(8,128)(2,1)}, bf16[384,2048]{1,0:T(8,128)(2,1)}, f32[384,256]{1,0:T(8,128)}) custom-call(s32[8]{0:T(128)} %reshape.447.refs_0_, s32[8]{0:T(128)} %bitcast.215, s32[1,1024]{1,0:T(1,128)} %refs_1_.9, f32[384,4]{1,0:T(8,128)} %dynamic-slice_bitcast_fusion.refs_3_, ...), custom_call_target="tpu_custom_call" | custom-call | flops 25000 | bytes 25000 | tf_op jit(solution)/shard_map/cross_backward/pallas_call | solution.py:1108
  499.6 22.1 %self_backward.1 = (bf16[1152,1024]{1,0:T(8,128)(2,1)}, f32[384,256]{1,0:T(8,128)}) custom-call(s32[8]{0:T(128)} %reshape.449.refs_0_, s32[1,1024]{1,0:T(1,128)} %refs_1_.9, s32[1024,1]{1,0:T(8,128)} %copy.124.refs_2_, f32[384,4]{1,0:T(8,128)} %dynamic-slice_bitcast_fusion.refs_3_, f32[32,1024]{1,0:T(8,128)} %get-tuple-element.186.refs_4_.refs_6_, ...), custom_call_target="tpu_custom_call" | custom-call | flops 25000 | bytes 25000 | tf_op jit(solution)/shard_map/self_backward/pallas_call | solution.py:1108
  521.8 7.5 convolution_convert_fusion
  529.2 54.2 %enter_backward.1 = (f32[256,1536]{1,0:T(8,128)}, f32[1,8,1536]{2,1,0:T(8,128)}, f32[1,8,1536]{2,1,0:T(8,128)}, bf16[4,192,1152]{2,1,0:T(8,128)(2,1)}) custom-call(bf16[1152,1024]{1,0:T(8,128)(2,1)} %get-tuple-element.109.refs_0_, bf16[1536,1152]{1,0:T(8,128)(2,1)} %bitcast.173, bf16[256,1536]{1,0:T(8,128)(2,1)} %refs_2_.7, ...), custom_call_target="tpu_custom_call" | custom-call | flops 1048576 | bytes 1048576 | tf_op jit(solution)/shard_map/enter_backward/pallas_call | solution.py:250
  586.6 55.7 %text_gradient.2 = (bf16[4,192,1024]{2,1,0:T(8,128)(2,1)}, bf16[4,384,2048]{2,1,0:T(8,128)(2,1)}, bf16[4,192,384]{2,1,0:T(8,128)(2,1)}) custom-call(bf16[384,2048]{1,0:T(8,128)(2,1)} %get-tuple-element.113.refs_0_, bf16[2048,1024]{1,0:T(8,128)(2,1)} %refs_1_.11, bf16[4,2,192,384]{3,2,1,0:T(8,128)(2,1)} %bitcast.201, f32[256,1536]{1,0:T(8,128)} %get-tuple-element.220.refs_3_), custom_call_target="tpu_custom_call" | custom-call | flops 1048576 | bytes 1048576 | tf_op jit(solution)/shard_map/text_gradient/pallas_call | solution.py:250
  645.8 44.9 %text_gradient.3 = (bf16[4,192,1024]{2,1,0:T(8,128)(2,1)}, bf16[4,384,2048]{2,1,0:T(8,128)(2,1)}) custom-call(bf16[384,2048]{1,0:T(8,128)(2,1)} %get-tuple-element.125.refs_0_, bf16[2048,1024]{1,0:T(8,128)(2,1)} %refs_1_.11, bf16[384,2048]{1,0:T(8,128)(2,1)} %reduce-scatter.12.cloned.1.call-done.refs_2_, bf16[768,1024]{1,0:T(8,128)(2,1)} %bitcast.193), custom_call_target="tpu_custom_call" | custom-call | flops 1048576 | bytes 1048576 | tf_op jit(solution)/shard_map/text_gradient/pallas_call | solution.py:250
  704.3 25.2 %modulation_return.1 = (f32[8,16,192]{2,1,0:T(8,128)}, bf16[1,192,2048]{2,1,0:T(8,128)(2,1)}) custom-call(f32[4,8,16,192]{3,2,1,0:T(8,128)} %pad_maximum_fusion.7.refs_0_, bf16[1,2,192,2048]{3,2,1,0:T(8,128)(2,1)} %bitcast.176, bf16[192,1152]{1,0:T(8,128)(2,1)} %reduce-scatter.8.cloned.1.call-done.refs_2_), custom_call_target="tpu_custom_call" | custom-call | flops 1048576 | bytes 1048576 | tf_op jit(solution)/shard_map/modulation_return/pallas_call | solution.py:250
  741.5 10.2 %norm_exchange.1 = f32[8,128]{1,0:T(8,128)} custom-call(f32[8,128]{1,0:T(8,128)} %broadcast_in_dim.22.refs_0_), custom_call_target="tpu_custom_call" | custom-call | flops 1048576 | bytes 1048576 | tf_op jit(solution)/shard_map/norm_exchange/pallas_call | solution.py:250
  757.9 4.7 multiply_subtract_fusion.1
  (268 shorter events, 93.0 us)
Async XLA Ops:
  7.2 42.8 %all-gather.11.cloned.1.call-start = ((), (), s32[]{:S(2)}) async-start(), calls=%async_computation.7 | async-start | bytes 1966080 | tf_op jit(solution)/shard_map/all_gather | solution.py:92
  9.7 84.7 %all-gather.9.cloned.1.call-start = ((), (), s32[]{:S(2)}) async-start(), calls=%async_computation.6 | async-start | bytes 1966080 | tf_op jit(solution)/shard_map/all_gather | solution.py:92
  10.5 155.9 %all-gather.7.cloned.1.call-start = ((), (), s32[]{:S(2)}) async-start(), calls=%async_computation.5 | async-start | bytes 2211840 | tf_op jit(solution)/shard_map/all_gather | solution.py:92
  11.5 256.0 %all-gather.13.cloned.1.call-start = ((), (), s32[]{:S(2)}) async-start(), calls=%async_computation.8 | async-start | bytes 1474560 | tf_op jit(solution)/shard_map/all_gather | solution.py:92
  12.3 22.6 %copy-start.21 = (f32[1024,192]{0,1:T(8,128)S(1)}, f32[1024,192]{0,1:T(8,128)}, u32[]{:S(2)}) copy-start(f32[1024,192]{0,1:T(8,128)} %param.40) | copy-start | bytes 2359300
  34.8 232.7 %all-gather.15.cloned.1.call-start = ((), (), s32[]{:S(2)}) async-start(), calls=%async_computation.9 | async-start | bytes 1966080 | tf_op jit(solution)/shard_map/all_gather | solution.py:92
  35.7 288.1 %all-gather.17.cloned.1.call-start = ((), (), s32[]{:S(2)}) async-start(), calls=%async_computation.10 | async-start | bytes 7864320 | tf_op jit(solution)/shard_map/all_gather | solution.py:92
  50.0 40.6 %copy-start.8 = (bf16[768,1024]{1,0:T(8,128)(2,1)S(1)}, bf16[768,1024]{1,0:T(8,128)(2,1)}, u32[]{:S(2)}) copy-start(bf16[768,1024]{1,0:T(8,128)(2,1)} %all-gather.11.cloned.1.call-done.refs_4_) | copy-start | bytes 4718596
  155.1 8.7 %copy-start.31 = (bf16[768,1024]{1,0:T(8,128)(2,1)S(1)}, bf16[768,1024]{1,0:T(8,128)(2,1)}, u32[]{:S(2)}) copy-start(bf16[768,1024]{1,0:T(8,128)(2,1)} %get-tuple-element.78) | copy-start | bytes 4718596
  155.1 344.5 %reduce-scatter.6.cloned.1.call-start = ((), (), s32[]{:S(2)}) async-start(), calls=%async_computation.11 | async-start | bytes 1966080 | tf_op jit(solution)/shard_map/reduce_scatter | solution.py:121
  166.4 48.5 %copy-start.4 = (bf16[768,1152]{1,0:T(8,128)(2,1)S(1)}, bf16[768,1152]{1,0:T(8,128)(2,1)}, u32[]{:S(2)}) copy-start(bf16[768,1152]{1,0:T(8,128)(2,1)} %all-gather.7.cloned.1.call-done.refs_2_) | copy-start | bytes 5308420
  267.5 52.7 %copy-start.7 = (bf16[768,1024]{1,0:T(8,128)(2,1)S(1)}, bf16[768,1024]{1,0:T(8,128)(2,1)}, u32[]{:S(2)}) copy-start(bf16[768,1024]{1,0:T(8,128)(2,1)} %all-gather.15.cloned.1.call-done.refs_6_) | copy-start | bytes 4718596
  387.7 58.0 %copy-start.3 = (bf16[1536,1024]{1,0:T(8,128)(2,1)S(1)}, bf16[1536,1024]{1,0:T(8,128)(2,1)}, u32[]{:S(2)}) copy-start(bf16[1536,1024]{1,0:T(8,128)(2,1)} %convolution_convert_fusion.2) | copy-start | bytes 9437188
  449.1 196.6 %reduce-scatter.12.cloned.1.call-start = ((), (), s32[]{:S(2)}) async-start(), calls=%async_computation.14 | async-start | bytes 7864320 | tf_op jit(solution)/shard_map/reduce_scatter | solution.py:1494
  460.5 234.1 %reduce-scatter.8.cloned.1.call-start = ((), (), s32[]{:S(2)}) async-start(), calls=%async_computation.12 | async-start | bytes 2211840 | tf_op jit(solution)/shard_map/reduce_scatter | solution.py:121
  499.6 22.1 %copy-start.63 = (bf16[4,256,1536]{2,1,0:T(8,128)(2,1)S(1)}, bf16[4,256,1536]{2,1,0:T(8,128)(2,1)}, u32[]{:S(2)}) copy-start(bf16[4,256,1536]{2,1,0:T(8,128)(2,1)} %get-tuple-element.80) | copy-start | bytes 9437188
  529.2 54.2 %copy-start.2 = (bf16[1536,1152]{1,0:T(8,128)(2,1)S(1)}, bf16[1536,1152]{1,0:T(8,128)(2,1)}, u32[]{:S(2)}) copy-start(bf16[1536,1152]{1,0:T(8,128)(2,1)} %convolution_convert_fusion) | copy-start | bytes 10616836
  586.5 111.0 %reduce-scatter.10.cloned.1.call-start = ((), (), s32[]{:S(2)}) async-start(), calls=%async_computation.13 | async-start | bytes 2703360 | tf_op jit(solution)/shard_map/reduce_scatter | solution.py:121
  586.6 55.7 %copy-start.28 = (bf16[1536,384]{1,0:T(8,128)(2,1)S(1)}, bf16[1536,384]{1,0:T(8,128)(2,1)}, u32[]{:S(2)}) copy-start(bf16[1536,384]{1,0:T(8,128)(2,1)} %convolution_convert_fusion.3) | copy-start | bytes 3538948
  645.5 91.7 %reduce-scatter.14.cloned.1.call-start = ((), (), s32[]{:S(2)}) async-start(), calls=%async_computation.15 | async-start | bytes 1966080 | tf_op jit(solution)/shard_map/reduce_scatter | solution.py:121
  702.2 27.3 %copy-start.1 = (bf16[384,2048]{1,0:T(8,128)(2,1)S(1)}, bf16[384,2048]{1,0:T(8,128)(2,1)}, u32[]{:S(2)}) copy-start(bf16[384,2048]{1,0:T(8,128)(2,1)} %reduce-scatter.12.cloned.1.call-done.refs_2_) | copy-start | bytes 4718596
  735.9 17.7 %copy-start.58 = (f32[8,192]{1,0:T(8,128)S(1)}, f32[8,192]{1,0:T(8,128)}, u32[]{:S(2)}) copy-start(f32[8,192]{1,0:T(8,128)} %param.57) | copy-start | bytes 18436
  735.9 17.7 %copy-start.59 = (f32[8,192]{1,0:T(8,128)S(1)}, f32[8,192]{1,0:T(8,128)}, u32[]{:S(2)}) copy-start(f32[8,192]{1,0:T(8,128)} %param.56) | copy-start | bytes 18436
  735.9 18.4 %copy-start.15 = (f32[1025,192]{0,1:T(8,128)S(1)}, f32[1025,192]{0,1:T(8,128)}, u32[]{:S(2)}) copy-start(f32[1025,192]{0,1:T(8,128)} %param.42) | copy-start | bytes 2361604
  (51 other events, 145.6 us)
Sparse Core Ops, SparseCore 0:
  10.2 39.7 all-gather.10
  52.1 36.7 all-gather.8
  91.1 39.1 all-gather.6
  132.3 29.3 all-gather.12
  163.7 36.2 all-gather.14
  201.9 114.2 all-gather.16
  449.2 34.6 reduce-scatter.5
  486.3 109.7 reduce-scatter.11
  598.4 38.9 reduce-scatter.7
  645.6 43.8 reduce-scatter.9
  691.8 36.7 reduce-scatter.13

commit v4 on v3

--- a/solution.py
+++ b/solution.py
@@ -31,6 +31,7 @@
 
 
 TILE = 256
+AHEAD = 2
 LOG2E = 1.0 / math.log(2.0)
 MESH = pl.DeviceIdType.MESH
 
@@ -351,45 +352,58 @@
     return [slice(i * size, (i + 1) * size) for i in range(CHUNKS)]
 
 
-def sum_blocks(partial, finish, work, sems):
+def sum_blocks(partial, finish, work, sems, by_columns=False):
     mine, near, far, both = row_peers()
     send_both, send_near, near_both, near_own, send_far, far_own, base = work
-    size = base.shape[0] // 2
-    chunks = chunk_rows(size)
-
-    def terms(block, rows):
-        start = pl.multiple_of((block % 2) * size + rows.start, size // CHUNKS)
-        return base[pl.ds(start, size // CHUNKS), :]
-
-    def hand_over(block, source, target, kind):
+    size, width = base.shape[0] // 2, base.shape[1]
+    step = width // CHUNKS
+    if by_columns:
+        chunks = [(slice(None), slice(i * step, (i + 1) * step)) for i in range(CHUNKS)]
+    else:
+        chunks = [(rows, slice(None)) for rows in chunk_rows(size)]
+
+    def terms(block, place):
+        rows, columns = place
+        first, count = rows.start or 0, size if by_columns else size // CHUNKS
+        start = pl.multiple_of((block % 2) * size + first, count)
+        return base[pl.ds(start, count), columns]
+
+    def hand_over(chip, block, source, target, kind):
         copies = []
-        for i, rows in enumerate(chunks):
-            source[rows, :] = half(terms(block, rows))
+        if not by_columns:
+            partial(chip, base, None)
+        for i, place in enumerate(chunks):
+            if by_columns:
+                partial(chip, base, place[1])
+            source[place] = half(terms(block, place))
             copies.append(
-                remote(source.at[rows], target.at[rows], sems, CHUNKS * kind + i, near)
+                remote(source.at[place], target.at[place], sems, CHUNKS * kind + i, near)
             )
             copies[i].start()
-        return copies
-
-    partial(far // 2, base)
+            if by_columns and i:
+                yield i - 1, copies[i - 1]
+        for i in range(CHUNKS - 1 if by_columns else 0, CHUNKS):
+            yield i, copies[i]
+
     across = []
-    for i, copy in enumerate(hand_over(both, send_both, near_both, 0)):
-        rows = chunks[i]
+    for i, copy in hand_over(far // 2, both, send_both, near_both, 0):
+        place = chunks[i]
         copy.wait()
-        send_far[rows, :] = half(terms(far, rows) + near_both[rows, :].astype(jnp.float32))
-        across.append(remote(send_far.at[rows], far_own.at[rows], sems, 2 * CHUNKS + i, far))
+        send_far[place] = half(terms(far, place) + near_both[place].astype(jnp.float32))
+        across.append(
+            remote(send_far.at[place], far_own.at[place], sems, 2 * CHUNKS + i, far)
+        )
         across[i].start()
-    partial(mine // 2, base)
-    for i, copy in enumerate(hand_over(near, send_near, near_own, 1)):
-        rows = chunks[i]
+    for i, copy in hand_over(mine // 2, near, send_near, near_own, 1):
+        place = chunks[i]
         copy.wait()
         across[i].wait()
         finish(
             i,
-            rows,
-            terms(mine, rows)
-            + near_own[rows, :].astype(jnp.float32)
-            + far_own[rows, :].astype(jnp.float32),
+            place[1] if by_columns else place[0],
+            terms(mine, place)
+            + near_own[place].astype(jnp.float32)
+            + far_own[place].astype(jnp.float32),
         )
 
 
@@ -479,21 +493,17 @@
     work, sems = rest[:-1], rest[-1]
     local = total.shape[0]
 
-    def partial(chip, base):
-        rows = chip_rows(chip, local)
-
-        @tiles_of(captions.shape[0], 512)
-        def _(columns):
-            base[:, columns] = dot(weight[rows, :], captions[columns, :], 1, 1)
-
-    def finish(i, rows, value):
-        total[rows, :] = value
-
-    sum_blocks(partial, finish, work, sems)
+    def partial(chip, base, columns):
+        base[:, columns] = dot(weight[chip_rows(chip, local), :], captions[columns, :], 1, 1)
+
+    def finish(i, columns, value):
+        total[:, columns] = value
+
+    sum_blocks(partial, finish, work, sems, by_columns=True)
 
 
 def transposed_partial(left, weight, lhs, size):
-    def partial(chip, base):
+    def partial(chip, base, _):
         lhs[...] = half(left[:, chip_rows(chip, size)].astype(jnp.float32).T)
 
         @tiles_of(weight.shape[0], 512)
@@ -535,7 +545,7 @@
     factor_grad[...] = jnp.zeros_like(factor_grad)
     row_grad[...] = jnp.zeros_like(row_grad)
 
-    def partial(chip, base):
+    def partial(chip, base, _):
         own = chip_rows(chip, size)
 
         @tiles_of(units, 512)
@@ -579,7 +589,7 @@
     factor_grad[...] = jnp.zeros_like(factor_grad)
     row_grad[...] = jnp.zeros_like(row_grad)
 
-    def partial(chip, base):
+    def partial(chip, base, _):
         own = chip_rows(chip, size)
 
         @tiles_of(units, 512)
@@ -792,10 +802,6 @@
     )
 
 
-def score_block(keys, query, bias):
-    return jnp.exp2(dot(keys, query, 1, 0) * (HEAD ** (-0.5) * LOG2E) + bias)
-
-
 def self_bias(step, ids_row, ids_column):
     start = pl.multiple_of(step * TILE, TILE)
     return jnp.where(ids_column[pl.ds(start, TILE), :] == ids_row[...], 0.0, NEG)
@@ -808,14 +814,19 @@
 
 def attend_tile(heads, meta, bias_of, query, key_rows, value, out, total, inv_ref):
     base = 2 * pl.program_id(0)
+    factor = HEAD ** (-0.5) * LOG2E
     out[...] = jnp.zeros_like(out)
     total[...] = jnp.zeros_like(total)
 
     def step(index, carry):
         bias = bias_of(index)
         rows = pl.ds(pl.multiple_of(index * TILE, TILE), TILE)
+        scores = [
+            dot(key_rows[head, rows, :], query[span, :], 1, 0)
+            for head, span in enumerate(spans(heads))
+        ]
         for head, span in enumerate(spans(heads)):
-            expo = score_block(key_rows[head, rows, :], query[span, :], bias)
+            expo = jnp.exp2(scores[head] * factor + bias)
             total[head] += jnp.sum(expo.reshape(TILE // 8, 8, TILE), axis=0)
             out[span, :] += dot(value[span, rows], half(expo), 1, 0)
         return carry
@@ -840,10 +851,20 @@
     def step(index, carry):
         bias = bias_of(index)
         rows = pl.ds(pl.multiple_of(index * TILE, TILE), TILE)
+        def products(head):
+            span = spans(heads)[head]
+            return (
+                dot(key_rows[head, rows, :], query[span, :], 1, 0),
+                dot(value_rows[head, rows, :], back[span, :], 1, 0),
+            )
+
+        ahead = [products(head) for head in range(min(AHEAD, heads))]
         for head, span in enumerate(spans(heads)):
-            probs = score_block(key_rows[head, rows, :], query[span, :], bias)
+            scores, prob_grad = ahead.pop(0)
+            if head + AHEAD < heads:
+                ahead.append(products(head + AHEAD))
+            probs = jnp.exp2(scores * (scale * LOG2E) + bias)
             probs = probs * inv_ref[head, 0:1, :]
-            prob_grad = dot(value_rows[head, rows, :], back[span, :], 1, 0)
             score_grad = half(probs * (prob_grad - centre[head, 0:1, :]))
             dv[span, rows] += dot(back[span, :], half(probs), 1, 1)
             dk[span, rows] += dot(query[span, :], score_grad, 1, 1) * scale
@@ -1187,10 +1208,11 @@
     fused = tensor_size == 4
     caption_half = half(caption_in)
     key_line = gather_far(caption_half[0].T)
-    value_line = gather_far(caption_half[1].T)
+    value_line = gather_far(
+        jnp.concatenate([caption_half[1].T, half(attention_out).T], axis=1)
+    )
     in_half = half(attention_in)
     attention_line = gather_far(jnp.concatenate([in_half[0], in_half[1], in_half[2]], axis=1))
-    out_own = half(attention_out).T
     down_line = gather_far(half(feed_out).T)
     feed_half = half(feed_in)
     feed_own = jnp.concatenate([feed_half[0], feed_half[1]], axis=1)
@@ -1210,17 +1232,17 @@
         ],
         axis=1,
     )
-    received, out_other = remote_call(
+    received, feed_other = remote_call(
         spread_kernel,
         "modulation_exchange",
         0,
         [payload],
         [jax.ShapeDtypeStruct((tensor_size, *payload.shape), jnp.float32)],
         exchange_scratch([payload.shape]),
-        [out_own],
+        [feed_own],
         everyone=True,
     )
-    out_full = gather_far(join_near(out_own, out_other, rows))
+    feed_full = gather_far(join_near(feed_own, feed_other, rows))
     factor_row = jnp.transpose(received[:, :, :per_row], (2, 1, 0, 3)).reshape(per_row, -1)
     gains = received[0, :, per_row:].reshape(dp_size, 8, -1)
     gains = jnp.transpose(gains, (1, 0, 2)).reshape(8, width)
@@ -1288,13 +1310,15 @@
     else:
         attn_full = in_place(spread(enter_point(source, token_factor(0), gains[0])))
         key_other = near_swap(key_line)
-    text_key_raw, value_other, feed_other = caption_project(
-        join_near(key_line, key_other, rows), [value_line, feed_own], 4
-    )
-    feed_full = gather_far(join_near(feed_own, feed_other, rows))
-    text_value_raw, attention_other = caption_project(
-        join_near(value_line, value_other, rows), [attention_line], 11
-    )
+    text_key_raw, value_other = caption_project(
+        join_near(key_line, key_other, rows), [value_line], 4
+    )
+    features = captions.shape[1]
+    value_full, out_full = (
+        join_near(value_line[:, part], value_other[:, part], rows)
+        for part in (slice(0, features), slice(features, None))
+    )
+    text_value_raw, attention_other = caption_project(value_full, [attention_line], 11)
     in_full = join_near(attention_line, attention_other, rows)
     projected = dot(in_full, attn_full, 0, 1)
     cosine, sine = rope_tables(rope_rows[0], rope_cols[0])
@@ -1635,7 +1659,6 @@
     )
     (key_grad,) = caption_back(text_key_grad, [], 9, [outer_both, value_grad])
     key_sum = scatter_far(key_grad)
-    value_sum, out_sum = value_sum[:, :columns], value_sum[:, columns:]
     shared_rows = jnp.sum(
         jnp.concatenate([enter_row, middle_row, end_row]), axis=1
     )
@@ -1670,25 +1693,28 @@
         everyone=True,
         after=[in_sum],
     )
+    in_sum, value_sum = gate(in_sum, received), gate(value_sum, received)
+    feed_out_sum = gate(feed_out_sum, received)
+    value_sum, out_sum = value_sum[:, :columns], value_sum[:, columns:]
     feed_in_sum = lax.dynamic_index_in_dim(outer_parts, dp_index % 2, 1, keepdims=False)[0]
     feed_in_sum = feed_in_sum.astype(f32) + outer_other[0].astype(f32)
     factor_grad = received[:, :per_row].reshape(images, own_columns)
     channel_sum = jnp.sum(received[:, per_row:], axis=0).reshape(channels.shape)
     modulator_sum = jnp.dot(augmented.astype(jnp.float32).T, factor_grad, precision=HIGH)
 
-    in_sum, out_sum, feed_in_sum, feed_out_sum, key_sum, value_sum = (
-        value.astype(jnp.float32)
-        for value in (in_sum, out_sum, feed_in_sum, feed_out_sum, key_sum, value_sum)
-    )
+    def square(value):
+        value = value.astype(f32)
+        return jnp.sum(value * value)
+
     squares = (
-        jnp.sum(in_sum * in_sum)
-        + jnp.sum(out_sum * out_sum)
-        + jnp.sum(feed_in_sum * feed_in_sum)
-        + jnp.sum(feed_out_sum * feed_out_sum)
-        + jnp.sum(key_sum * key_sum)
-        + jnp.sum(value_sum * value_sum)
-        + jnp.sum(modulator_sum * modulator_sum)
-        + jnp.sum(channel_sum * channel_sum) / tensor_size
+        square(in_sum)
+        + square(out_sum)
+        + square(feed_in_sum)
+        + square(feed_out_sum)
+        + square(key_sum)
+        + square(value_sum)
+        + square(modulator_sum)
+        + square(channel_sum) / tensor_size
     )
     in_sum = jnp.stack([in_sum[:, i * local : (i + 1) * local] for i in range(3)])
     feed_in_sum = jnp.stack([feed_in_sum[:, i * units : (i + 1) * units] for i in range(2)])
@@ -1705,8 +1731,8 @@
     grad_norm = jnp.sqrt(squares[0, 0])
     factor = CLIP / jnp.maximum(grad_norm, CLIP)
     results = [
-        adamw(grad * factor, weight, moment, square, DECAY, RATE)
-        for grad, weight, moment, square in (
+        adamw(grad.astype(f32) * factor, weight, moment, second, DECAY, RATE)
+        for grad, weight, moment, second in (
             (in_sum, attention_in, moment_attention_in, square_attention_in),
             (out_sum.T, attention_out, moment_attention_out, square_attention_out),
             (feed_in_sum, feed_in, moment_feed_in, square_feed_in),

time: 792 us -> 762 us (0.962)
  Pallas kernels: 615 us -> 590 us
  waiting for transfers between devices: 9.37 us -> 0.28 us
    pallas_call x4, Pallas kernels: 91.6 us -> 64.9 us  [attention_call(): pl.pallas_call(run, grid_spec=pltpu.PrefetchScalarGridSpec(num_scalar_pre...]
    all_gather x6 -> x5, waiting for transfers between devices: 8.46 us -> 0.01 us  [gather_far(): lax.all_gather(value, 'dp', axis=0, tiled=True, axis_index_groups=far_gro...]
  transfers between devices with their start and end apart: 11 -> 10, of which waited for: 1 -> 0; matrix products, arithmetic and copies ran while one was open for 11% -> 12% of each run, Pallas kernels for 63% -> 62%
where the time goes in v4:
time: 762 us; the launch traced here: 750 us
  Pallas kernels  590 us (77%)
  other arithmetic  62.2 us (8%)
  matrix products  42.8 us (6%)
  local copies, waits for them, and re-layouts  32 us (4%)
  between operations  22.5 us (3%)
    pallas_call x12, Pallas kernels, remote_call(): pl.pallas_call(run, out_shape=[*outs, *traded], in_specs=[whole] * len(op...  525 us
    pallas_call x4, Pallas kernels, attention_call(): pl.pallas_call(run, grid_spec=pltpu.PrefetchScalarGridSpec(num_scalar_pre...  64.9 us
    dot_general x6, matrix products, dot(): lax.dot_general(left, right, (((left_dim,), (right_dim,)), ((), ())), pre...  41 us
    sub x7, other arithmetic, adamw(): weight - rate * (step_size + decay * weight)  16.2 us
  transfers between devices with their start and end apart: 10, of which 0 were waited for; matrix products, arithmetic and copies ran while one was open for 12% of the time, Pallas kernels for 62%

profile of v4, /device:TPU:0, one launch (start us, length us, event | category | flops | bytes accessed | tf_op | source)
XLA Modules:
  0.0 750.4 jit_solution(8849257611921341562)
XLA Ops:
  15.9 33.1 %modulation_exchange.1 = (f32[4,8,16,192]{3,2,1,0:T(8,128)}, bf16[192,2048]{1,0:T(8,128)(2,1)}) custom-call(f32[8,16,192]{2,1,0:T(8,128)} %pad_maximum_fusion.13.refs_0_, bf16[192,2048]{1,0:T(8,128)(2,1)} %pad_maximum_fusion.7.refs_1_), custom_call_target="tpu_custom_call" | custom-call | flops 1048576 | bytes 1048576 | tf_op jit(solution)/shard_map/modulation_exchange/pallas_call | solution.py:251
  63.3 41.9 %enter.1 = (bf16[4,256,1536]{2,1,0:T(8,128)(2,1)}, bf16[768,1024]{1,0:T(8,128)(2,1)}) custom-call(bf16[256,1536]{1,0:T(8,128)(2,1)} %refs_2_.7, f32[8,6144]{1,0:T(8,128)} %reshape.480.refs_1_.refs_3_.refs_4_.refs_6_, f32[256,8]{1,0:T(8,128)} %fusion.21.refs_2_.refs_4_.refs_5_.refs_7_, f32[8,1536]{1,0:T(8,128)} %reshape.481.refs_3_.refs_5_.refs_8_.refs_10_.refs_7_, ...), custom_call_target="tpu_custom_call" | custom-call | flops 1048576 | bytes 1048576 | tf_op jit(solution)/shard_map/enter/pallas_call | solution.py:251
  109.2 54.4 %project.2 = (f32[384,2048]{1,0:T(8,128)}, bf16[768,1408]{1,0:T(8,128)(2,1)}) custom-call(bf16[1536,1024]{1,0:T(8,128)(2,1)} %bitcast.170, bf16[2048,1024]{1,0:T(8,128)(2,1)} %refs_1_.11, bf16[768,1408]{1,0:T(8,128)(2,1)} %all-gather.8.cloned.1.call-done.refs_2_), custom_call_target="tpu_custom_call" | custom-call | flops 1048576 | bytes 1048576 | tf_op jit(solution)/shard_map/project/pallas_call | solution.py:251
  167.8 45.9 %project.3 = (f32[384,2048]{1,0:T(8,128)}, bf16[768,1152]{1,0:T(8,128)(2,1)}) custom-call(bf16[1536,1024]{1,0:T(8,128)(2,1)} %bitcast.169, bf16[2048,1024]{1,0:T(8,128)(2,1)} %refs_1_.11, bf16[768,1152]{1,0:T(8,128)(2,1)} %all-gather.6.cloned.1.call-done.refs_2_), custom_call_target="tpu_custom_call" | custom-call | flops 1048576 | bytes 1048576 | tf_op jit(solution)/shard_map/project/pallas_call | solution.py:251
  218.7 6.0 fusion.44.refs_8_.refs_9_.refs_10_.refs_16_.refs_17_
  224.7 11.7 %self_forward.1 = (bf16[384,1024]{1,0:T(8,128)(2,1)}, bf16[384,1024]{1,0:T(8,128)(2,1)}, bf16[6,1024,64]{2,1,0:T(8,128)(2,1)}, bf16[6,1024,64]{2,1,0:T(8,128)(2,...) custom-call(s32[8]{0:T(128)} %reshape.479.refs_0_, s32[1,1024]{1,0:T(1,128)} %refs_1_.9, s32[1024,1]{1,0:T(8,128)} %copy.130.refs_2_, ...), custom_call_target="tpu_custom_call" | custom-call | flops 15000 | bytes 15000 | tf_op jit(solution)/shard_map/self_forward/pallas_call | solution.py:1129
  236.4 15.9 %cross_forward.1 = (bf16[384,2048]{1,0:T(8,128)(2,1)}, bf16[6,2048,64]{2,1,0:T(8,128)(2,1)}, bf16[6,2048,64]{2,1,0:T(8,128)(2,1)}, f32[384,1024]{1,0:T(8,128)}, ...) custom-call(s32[8]{0:T(128)} %reshape.477.refs_0_, s32[8]{0:T(128)} %bitcast.213, s32[1,1024]{1,0:T(1,128)} %refs_1_.9, ...), custom_call_target="tpu_custom_call" | custom-call | flops 18000 | bytes 18000 | tf_op jit(solution)/shard_map/cross_forward/pallas_call | solution.py:1129
  254.9 48.5 %attention_out.1 = (f32[256,1536]{1,0:T(8,128)}, f32[256,1536]{1,0:T(8,128)}, bf16[4,256,1536]{2,1,0:T(8,128)(2,1)}, bf16[768,1024]{1,0:T(8,128)(2,1)}) custom-call(bf16[384,1024]{1,0:T(8,128)(2,1)} %get-tuple-element.84.refs_0_, bf16[1536,384]{1,0:T(8,128)(2,1)} %bitcast.190, bf16[256,1536]{1,0:T(8,128)(2,1)} %refs_2_.7, ...), custom_call_target="tpu_custom_call" | custom-call | flops 1048576 | bytes 1048576 | tf_op jit(solution)/shard_map/attention_out/pallas_call | solution.py:251
  307.0 56.5 %feed_forward.1 = (f32[1024,2048]{1,0:T(8,128)}, bf16[1024,1024]{1,0:T(8,128)(2,1)}, f32[256,1536]{1,0:T(8,128)}, f32[1,8,1536]{2,1,0:T(8,128)}, f32[1,8,1536]{2,1,0:T(8,128)}, /*index=5*/bf16[4,256,1536]{2,1,0:T(8,128)(2,1)}) custom-call(bf16[1024,1536]{1,0:T(8,128)(2,1)} %bitcast.196, bf16[1536,2048]{1,0:T(8,128)(2,1)} %all-gather.14.cloned.1.call-done.refs_1_.refs_2_, ...), custom_call_target="tpu_custom_call" | custom-call | flops 1048576 | bytes 1048576 | tf_op jit(solution)/shard_map/feed_forward/pallas_call | solution.py:251
  363.5 7.6 %convolution_convert_fusion.2 = bf16[1536,1024]{1,0:T(8,128)(2,1)} fusion(bf16[1024,1536]{1,0:T(8,128)(2,1)} %bitcast.192, bf16[1024,1024]{1,0:T(8,128)(2,1)} %get-tuple-element.97), kind=kOutput, calls=%fused_computation.2 | convolution fusion | flops 3222798336 | bytes 8388608 | tf_op jit(solution)/shard_map/dot_general | solution.py:40
  371.1 58.0 %feed_backward.1 = (bf16[1024,2048]{1,0:T(8,128)(2,1)}, f32[256,1536]{1,0:T(8,128)}, f32[2,8,1536]{2,1,0:T(8,128)}, f32[2,8,1536]{2,1,0:T(8,128)}, bf16[4,256,15...) custom-call(bf16[1024,1536]{1,0:T(8,128)(2,1)} %bitcast.193, f32[1024,2048]{1,0:T(8,128)} %get-tuple-element.95.refs_1_, ...), custom_call_target="tpu_custom_call" | custom-call | flops 1048576 | bytes 1048576 | tf_op jit(solution)/shard_map/feed_backward/pallas_call | solution.py:251
  429.1 3.4 fusion.1
  432.5 11.3 %convolution_convert_fusion.1.after = bf16[1536,2048]{1,0:T(8,128)(2,1)} fusion(bf16[1024,1536]{1,0:T(8,128)(2,1)} %bitcast.197, bf16[1024,2048]{1,0:T(8,128)(2,1)} %get-tuple-element.99), kind=kOutput, calls=%fused_computation.1 | convolution fusion | flops 6445596672 | bytes 13631488 | tf_op jit(solution)/shard_map/dot_general | solution.py:40
  445.7 4.0 convolution_convert_fusion.3
  451.0 4.5 fusion.45.refs_10_.refs_14_
  455.5 20.5 %cross_backward.1 = (f32[384,1024]{1,0:T(8,128)}, bf16[384,2048]{1,0:T(8,128)(2,1)}, bf16[384,2048]{1,0:T(8,128)(2,1)}, f32[384,256]{1,0:T(8,128)}) custom-call(s32[8]{0:T(128)} %reshape.477.refs_0_, s32[8]{0:T(128)} %bitcast.214, s32[1,1024]{1,0:T(1,128)} %refs_1_.9, f32[384,4]{1,0:T(8,128)} %dynamic-slice_bitcast_fusion.refs_3_, ...), custom_call_target="tpu_custom_call" | custom-call | flops 25000 | bytes 25000 | tf_op jit(solution)/shard_map/cross_backward/pallas_call | solution.py:1129
  476.1 16.8 %self_backward.1 = (bf16[1152,1024]{1,0:T(8,128)(2,1)}, f32[384,256]{1,0:T(8,128)}) custom-call(s32[8]{0:T(128)} %reshape.479.refs_0_, s32[1,1024]{1,0:T(1,128)} %refs_1_.9, s32[1024,1]{1,0:T(8,128)} %copy.130.refs_2_, f32[384,4]{1,0:T(8,128)} %dynamic-slice_bitcast_fusion.refs_3_, f32[32,1024]{1,0:T(8,128)} %get-tuple-element.184.refs_4_.refs_6_, ...), custom_call_target="tpu_custom_call" | custom-call | flops 25000 | bytes 25000 | tf_op jit(solution)/shard_map/self_backward/pallas_call | solution.py:1129
  492.9 7.6 %convolution_convert_fusion = bf16[1536,1152]{1,0:T(8,128)(2,1)} fusion(bf16[1024,1536]{1,0:T(8,128)(2,1)S(1)} %bitcast.217, bf16[1152,1024]{1,0:T(8,128)(2,1)} %get-tuple-element.107.refs_0_), kind=kOutput, calls=%fused_computation | convolution fusion | flops 3625648128 | bytes 9043968 | tf_op jit(solution)/shard_map/dot_general | solution.py:40
  500.5 50.8 %enter_backward.1 = (f32[256,1536]{1,0:T(8,128)}, f32[1,8,1536]{2,1,0:T(8,128)}, f32[1,8,1536]{2,1,0:T(8,128)}, bf16[4,192,1152]{2,1,0:T(8,128)(2,1)}) custom-call(bf16[1152,1024]{1,0:T(8,128)(2,1)} %get-tuple-element.107.refs_0_, bf16[1536,1152]{1,0:T(8,128)(2,1)} %bitcast.168, bf16[256,1536]{1,0:T(8,128)(2,1)} %refs_2_.7, ...), custom_call_target="tpu_custom_call" | custom-call | flops 1048576 | bytes 1048576 | tf_op jit(solution)/shard_map/enter_backward/pallas_call | solution.py:251
  554.5 55.3 %text_gradient.2 = (bf16[4,192,1024]{2,1,0:T(8,128)(2,1)}, bf16[4,384,2048]{2,1,0:T(8,128)(2,1)}, bf16[4,192,384]{2,1,0:T(8,128)(2,1)}) custom-call(bf16[384,2048]{1,0:T(8,128)(2,1)} %get-tuple-element.120.refs_0_, bf16[2048,1024]{1,0:T(8,128)(2,1)} %refs_1_.11, bf16[4,2,192,384]{3,2,1,0:T(8,128)(2,1)} %bitcast.198, f32[256,1536]{1,0:T(8,128)} %get-tuple-element.218.refs_3_), custom_call_target="tpu_custom_call" | custom-call | flops 1048576 | bytes 1048576 | tf_op jit(solution)/shard_map/text_gradient/pallas_call | solution.py:251
  613.2 45.2 %text_gradient.3 = (bf16[4,192,1024]{2,1,0:T(8,128)(2,1)}, bf16[4,384,2048]{2,1,0:T(8,128)(2,1)}) custom-call(bf16[384,2048]{1,0:T(8,128)(2,1)} %get-tuple-element.124.refs_0_, bf16[2048,1024]{1,0:T(8,128)(2,1)} %refs_1_.11, bf16[384,2048]{1,0:T(8,128)(2,1)} %reduce-scatter.10.cloned.1.call-done.refs_2_, bf16[768,1024]{1,0:T(8,128)(2,1)} %bitcast.188), custom_call_target="tpu_custom_call" | custom-call | flops 1048576 | bytes 1048576 | tf_op jit(solution)/shard_map/text_gradient/pallas_call | solution.py:251
  661.6 24.6 %modulation_return.1 = (f32[8,16,192]{2,1,0:T(8,128)}, bf16[1,192,2048]{2,1,0:T(8,128)(2,1)}) custom-call(f32[4,8,16,192]{3,2,1,0:T(8,128)} %pad_maximum_fusion.10.refs_0_, bf16[1,2,192,2048]{3,2,1,0:T(8,128)(2,1)} %bitcast.171, bf16[192,1152]{1,0:T(8,128)(2,1)} %reduce-scatter.8.cloned.1.call-done.refs_2_.value), custom_call_target="tpu_custom_call" | custom-call | flops 1048576 | bytes 1048576 | tf_op jit(solution)/shard_map/modulation_return/pallas_call | solution.py:251
  690.2 3.3 multiply_reduce_fusion
  707.2 10.8 %norm_exchange.1 = f32[8,128]{1,0:T(8,128)} custom-call(f32[8,128]{1,0:T(8,128)} %broadcast_in_dim.22.refs_0_), custom_call_target="tpu_custom_call" | custom-call | flops 1048576 | bytes 1048576 | tf_op jit(solution)/shard_map/norm_exchange/pallas_call | solution.py:251
  (260 shorter events, 90.3 us)
Async XLA Ops:
  7.2 56.1 %all-gather.10.cloned.1.call-start = ((), (), s32[]{:S(2)}) async-start(), calls=%async_computation.7 | async-start | bytes 1966080 | tf_op jit(solution)/shard_map/all_gather | solution.py:93
  9.6 99.6 %all-gather.8.cloned.1.call-start = ((), (), s32[]{:S(2)}) async-start(), calls=%async_computation.6 | async-start | bytes 2703360 | tf_op jit(solution)/shard_map/all_gather | solution.py:93
  10.7 157.1 %all-gather.6.cloned.1.call-start = ((), (), s32[]{:S(2)}) async-start(), calls=%async_computation.5 | async-start | bytes 2211840 | tf_op jit(solution)/shard_map/all_gather | solution.py:93
  11.7 243.1 %all-gather.12.cloned.1.call-start = ((), (), s32[]{:S(2)}) async-start(), calls=%async_computation.8 | async-start | bytes 1966080 | tf_op jit(solution)/shard_map/all_gather | solution.py:93
  12.6 294.3 %all-gather.14.cloned.1.call-start = ((), (), s32[]{:S(2)}) async-start(), calls=%async_computation.9 | async-start | bytes 7864320 | tf_op jit(solution)/shard_map/all_gather | solution.py:93
  51.8 5.6 copy-start.57
  51.8 424.2 %reduce-scatter.6.cloned.1.call-start = ((), (), s32[]{:S(2)}) async-start(), calls=%async_computation.10 | async-start | bytes 1966080 | tf_op jit(solution)/shard_map/reduce_scatter | solution.py:122
  63.3 42.0 %copy-start.11 = (bf16[768,1024]{1,0:T(8,128)(2,1)S(1)}, bf16[768,1024]{1,0:T(8,128)(2,1)}, u32[]{:S(2)}) copy-start(bf16[768,1024]{1,0:T(8,128)(2,1)} %all-gather.10.cloned.1.call-done.refs_4_) | copy-start | bytes 4718596
  109.2 54.4 %copy-start.2 = (bf16[768,1408]{1,0:T(8,128)(2,1)S(1)}, bf16[768,1408]{1,0:T(8,128)(2,1)}, u32[]{:S(2)}) copy-start(bf16[768,1408]{1,0:T(8,128)(2,1)} %all-gather.8.cloned.1.call-done.refs_2_) | copy-start | bytes 6488068
  167.8 45.9 %copy-start.6 = (bf16[768,1152]{1,0:T(8,128)(2,1)S(1)}, bf16[768,1152]{1,0:T(8,128)(2,1)}, u32[]{:S(2)}) copy-start(bf16[768,1152]{1,0:T(8,128)(2,1)} %all-gather.6.cloned.1.call-done.refs_2_) | copy-start | bytes 5308420
  215.9 8.8 %copy-start = (bf16[4,2,192,1152]{3,2,1,0:T(8,128)(2,1)}, bf16[4,2,192,1152]{3,2,1,0:T(8,128)(2,1)S(1)}, u32[]{:S(2)}) copy-start(bf16[4,2,192,1152]{3,2,1,0:T(8,128)(2,1)S(1)} %pad_maximum_fusion) | copy-start | bytes 10616836
  254.9 48.5 %copy-start.10 = (bf16[768,1024]{1,0:T(8,128)(2,1)S(1)}, bf16[768,1024]{1,0:T(8,128)(2,1)}, u32[]{:S(2)}) copy-start(bf16[768,1024]{1,0:T(8,128)(2,1)} %all-gather.12.cloned.1.call-done.refs_6_) | copy-start | bytes 4718596
  371.1 58.0 %copy-start.4 = (bf16[1536,1024]{1,0:T(8,128)(2,1)S(1)}, bf16[1536,1024]{1,0:T(8,128)(2,1)}, u32[]{:S(2)}) copy-start(bf16[1536,1024]{1,0:T(8,128)(2,1)} %convolution_convert_fusion.2) | copy-start | bytes 9437188
  432.5 180.8 %reduce-scatter.10.cloned.1.call-start = ((), (), s32[]{:S(2)}) async-start(), calls=%async_computation.12 | async-start | bytes 7864320 | tf_op jit(solution)/shard_map/reduce_scatter | solution.py:1518
  443.8 217.7 %reduce-scatter.8.cloned.1.call-start = ((), (), s32[]{:S(2)}) async-start(), calls=%async_computation.11 | async-start | bytes 2211840 | tf_op jit(solution)/shard_map/reduce_scatter | solution.py:122
  476.1 16.8 %copy-start.59 = (bf16[4,256,1536]{2,1,0:T(8,128)(2,1)S(1)}, bf16[4,256,1536]{2,1,0:T(8,128)(2,1)}, u32[]{:S(2)}) copy-start(bf16[4,256,1536]{2,1,0:T(8,128)(2,1)} %get-tuple-element.79) | copy-start | bytes 9437188
  500.5 50.8 %copy-start.3 = (bf16[1536,1152]{1,0:T(8,128)(2,1)S(1)}, bf16[1536,1152]{1,0:T(8,128)(2,1)}, u32[]{:S(2)}) copy-start(bf16[1536,1152]{1,0:T(8,128)(2,1)} %convolution_convert_fusion) | copy-start | bytes 10616836
  554.4 131.8 %reduce-scatter.12.cloned.1.call-start = ((), (), s32[]{:S(2)}) async-start(), calls=%async_computation.13 | async-start | bytes 2703360 | tf_op jit(solution)/shard_map/reduce_scatter | solution.py:122
  554.5 55.3 %copy-start.26 = (bf16[1536,384]{1,0:T(8,128)(2,1)S(1)}, bf16[1536,384]{1,0:T(8,128)(2,1)}, u32[]{:S(2)}) copy-start(bf16[1536,384]{1,0:T(8,128)(2,1)} %convolution_convert_fusion.3) | copy-start | bytes 3538948
  613.0 89.8 %reduce-scatter.14.cloned.1.call-start = ((), (), s32[]{:S(2)}) async-start(), calls=%async_computation.14 | async-start | bytes 1966080 | tf_op jit(solution)/shard_map/reduce_scatter | solution.py:122
  690.1 6.5 copy-start.27
  690.2 7.7 %copy-start.16 = (bf16[192,1408]{1,0:T(8,128)(2,1)S(1)}, bf16[192,1408]{1,0:T(8,128)(2,1)}, u32[]{:S(2)}) copy-start(bf16[192,1408]{1,0:T(8,128)(2,1)} %gate.6) | copy-start | bytes 1622020
  702.7 19.5 %copy-start.15 = (bf16[192,1024]{1,0:T(8,128)(2,1)S(1)}, bf16[192,1024]{1,0:T(8,128)(2,1)}, u32[]{:S(2)}) copy-start(bf16[192,1024]{1,0:T(8,128)(2,1)} %gate.7) | copy-start | bytes 1179652
  702.7 19.5 %copy-start.24 = (f32[1024,192]{0,1:T(8,128)S(1)}, f32[1024,192]{0,1:T(8,128)}, u32[]{:S(2)}) copy-start(f32[1024,192]{0,1:T(8,128)} %param.40) | copy-start | bytes 2359300
  (46 other events, 112.9 us)
Sparse Core Ops, SparseCore 0:
  10.2 42.3 all-gather.9
  54.7 46.0 all-gather.7
  102.9 39.0 all-gather.5
  143.9 35.9 all-gather.11
  181.9 114.1 all-gather.13
  432.6 33.4 reduce-scatter.5
  468.4 109.6 reduce-scatter.9
  580.5 38.9 reduce-scatter.7
  621.9 44.0 reduce-scatter.11
  668.1 34.6 reduce-scatter.13

commit v5 on v4

--- a/solution.py
+++ b/solution.py
@@ -200,7 +200,18 @@
 
 
 def remote_call(
-    kernel, name, number, operands, outs, scratch, carry=(), everyone=False, neighbour=False, after=()
+    kernel,
+    name,
+    number,
+    operands,
+    outs,
+    scratch,
+    carry=(),
+    everyone=False,
+    neighbour=False,
+    after=(),
+    late=(),
+    late_outs=(),
 ):
     copies = sum(array.shape[0] if len(array.shape) == 4 else 1 for array in carry)
     traded = [
@@ -213,10 +224,10 @@
 
     def run(*refs):
         refs = list(refs)
-        ins = [refs.pop(0) for _ in operands]
+        ins = [refs.pop(0) for _ in (*operands, *late)]
         sources = [refs.pop(0) for _ in carry]
         del refs[: len(after)]
-        results = [refs.pop(0) for _ in outs]
+        results = [refs.pop(0) for _ in (*outs, *late_outs)]
         targets = [refs.pop(0) for _ in carry]
         meet(everyone, neighbour or bool(carry))
         started = []
@@ -250,9 +261,9 @@
     anywhere = pl.BlockSpec(memory_space=pl.ANY)
     return pl.pallas_call(
         run,
-        out_shape=[*outs, *traded],
-        in_specs=[whole] * len(operands) + [anywhere] * (len(carry) + len(after)),
-        out_specs=[whole] * len(outs) + [anywhere] * len(carry),
+        out_shape=[*outs, *late_outs, *traded],
+        in_specs=[whole] * len(operands) + [anywhere] * (len(late) + len(carry) + len(after)),
+        out_specs=[whole] * len(outs) + [anywhere] * (len(late_outs) + len(carry)),
         scratch_shapes=[
             *scratch,
             *([pltpu.SemaphoreType.DMA((2, copies))] if carry else []),
@@ -262,7 +273,7 @@
         ),
         cost_estimate=pl.CostEstimate(flops=1 << 20, bytes_accessed=1 << 20, transcendentals=0),
         name=name,
-    )(*operands, *carry, *after)
+    )(*operands, *late, *carry, *after)
 
 
 def send_blocks(axis, pick, target, send_sem, recv_sem):
@@ -535,13 +546,28 @@
     share.settle()
 
 
+def begin_copies(pairs, sems):
+    copies = [
+        pltpu.make_async_copy(source, target, sems.at[i])
+        for i, (source, target) in enumerate(pairs)
+    ]
+    for copy in copies:
+        copy.start()
+    return copies
+
+
 def feed_kernel(
-    inputs, feed, down, middle, factor, chooser, choose, cotangent, gain,
-    gate_up, hidden, out, factor_grad, row_grad, gathered, *rest
+    inputs, feed, factor, chooser, choose, gain, down_far, middle_far, cotangent_far,
+    hidden, out, factor_grad, row_grad, gathered, gate_far, *rest
 ):
-    work, sems = rest[:-1], rest[-1]
+    gate_up, down, middle, cotangent, moves = rest[:5]
+    work, sems = rest[5:-1], rest[-1]
     size = middle.shape[0]
     units = hidden.shape[1]
+    loads = begin_copies(
+        [(down_far, down), (middle_far, middle), (cotangent_far, cotangent)], moves
+    )
+    saves = []
     factor_grad[...] = jnp.zeros_like(factor_grad)
     row_grad[...] = jnp.zeros_like(row_grad)
 
@@ -557,6 +583,14 @@
             gate_up[own, other] = second
             hidden[own, columns] = half(first * jax.nn.sigmoid(first) * second)
 
+        save = pltpu.make_async_copy(
+            gate_up.at[own], gate_far.at[own], moves.at[3 + len(saves)]
+        )
+        save.start()
+        saves.append(save)
+        for load in loads[:1] if len(saves) == 1 else loads[1:]:
+            load.wait()
+
         @tiles_of(down.shape[0], 512)
         def _(columns):
             base[:, columns] = dot(hidden[own, :], down[columns, :], 1, 1)
@@ -577,20 +611,38 @@
 
     sum_blocks(partial, finish, work, sems)
     share.settle()
+    for save in saves:
+        save.wait()
 
 
 def feed_back_kernel(
-    back, gate_up, feed, down, summed, middle, factor, chooser, choose, cotangent, gain,
-    pair, middle_grad, factor_grad, row_grad, gathered, *rest
+    back, down, factor, chooser, choose, gain, gate_far, feed_far, summed_far, middle_far,
+    cotangent_far, middle_grad, factor_grad, row_grad, gathered, pair_far, *rest
 ):
-    work, sems = rest[:-1], rest[-1]
+    gate_up, feed, summed, middle, cotangent, pair, moves = rest[:7]
+    work, sems = rest[7:-1], rest[-1]
     size = middle.shape[0]
     units = down.shape[1]
+    mine, _, far, _ = row_peers()
+    first_rows, last_rows = chip_rows(far // 2, size), chip_rows(mine // 2, size)
+    loads = begin_copies(
+        [
+            (gate_far.at[first_rows], gate_up.at[first_rows]),
+            (feed_far, feed),
+            (gate_far.at[last_rows], gate_up.at[last_rows]),
+            (summed_far, summed),
+            (middle_far, middle),
+            (cotangent_far, cotangent),
+        ],
+        moves,
+    )
+    saves = []
     factor_grad[...] = jnp.zeros_like(factor_grad)
     row_grad[...] = jnp.zeros_like(row_grad)
 
     def partial(chip, base, _):
         own = chip_rows(chip, size)
+        loads[2 if saves else 0].wait()
 
         @tiles_of(units, 512)
         def _(columns):
@@ -598,6 +650,12 @@
             grad = dot(back[own, :], down[:, columns], 1, 0)
             first, second = gate_up[own, columns], gate_up[own, other]
             pair[own, columns], pair[own, other] = pair_point(grad, first, second)
+
+        save = pltpu.make_async_copy(pair.at[own], pair_far.at[own], moves.at[6 + len(saves)])
+        save.start()
+        saves.append(save)
+        for load in loads[1:2] if len(saves) == 1 else loads[3:]:
+            load.wait()
 
         @tiles_of(feed.shape[0], 512)
         def _(columns):
@@ -626,6 +684,8 @@
 
     sum_blocks(partial, finish, work, sems)
     share.settle()
+    for save in saves:
+        save.wait()
 
 
 def enter_back_kernel(
@@ -1405,30 +1465,30 @@
         )
         feed_all = feed_all.reshape(row_tokens, width)
         down_full = join_near(down_line, down_other, rows)
-        gate_up, hidden, block_out, end_factor, end_row, feed_sum_grad = remote_call(
+        block = pltpu.VMEM((shard_rows, width), f32)
+        hidden, block_out, end_factor, end_row, feed_sum_grad, gate_up = remote_call(
             feed_kernel,
             "feed_forward",
             6,
+            [feed_all, feed_full, factor_row, chooser, choose, norm_gains],
             [
-                feed_all,
-                feed_full,
-                down_full,
-                middle,
-                factor_row,
-                chooser,
-                choose,
-                cotangent,
-                norm_gains,
-            ],
-            [
-                shape((row_tokens, 2 * units)),
                 shape((row_tokens, units), bf16),
                 shape((shard_rows, width)),
                 shape((1, per_row, width)),
                 shape((1, 8, width)),
                 gathered,
             ],
-            [*in_kernel, all_sems],
+            [
+                pltpu.VMEM((row_tokens, 2 * units), f32),
+                pltpu.VMEM((width, units), bf16),
+                block,
+                block,
+                pltpu.SemaphoreType.DMA((5,)),
+                *in_kernel,
+                all_sems,
+            ],
+            late=[down_full, middle, cotangent],
+            late_outs=[shape((row_tokens, 2 * units))],
         )
         feed_sum_grad = feed_sum_grad.reshape(row_tokens, width)
     else:
@@ -1460,38 +1520,37 @@
     feed_out_parts = feed_out_grad.reshape(dp_size // 2, 2, -1, units)
     if fused:
         (
-            pair_grad,
             middle_grad,
             middle_factor,
             middle_row,
             attn_sum_grad,
+            pair_grad,
             feed_out_other,
         ) = remote_call(
             feed_back_kernel,
             "feed_backward",
             7,
+            [feed_sum_grad, down_full, factor_row, chooser, choose, norm_gains],
             [
-                feed_sum_grad,
-                gate_up,
-                feed_full,
-                down_full,
-                attn_sum,
-                middle,
-                factor_row,
-                chooser,
-                choose,
-                cotangent,
-                norm_gains,
-            ],
-            [
-                shape((row_tokens, 2 * units), bf16),
                 shape((shard_rows, width)),
                 shape((2, per_row, width)),
                 shape((2, 8, width)),
                 gathered,
             ],
-            [*in_kernel, all_sems],
+            [
+                pltpu.VMEM((row_tokens, 2 * units), f32),
+                pltpu.VMEM((width, 2 * units), bf16),
+                block,
+                block,
+                block,
+                pltpu.VMEM((row_tokens, 2 * units), bf16),
+                pltpu.SemaphoreType.DMA((8,)),
+                *in_kernel,
+                all_sems,
+            ],
             [feed_out_parts],
+            late=[gate_up, feed_full, attn_sum, middle, cotangent],
+            late_outs=[shape((row_tokens, 2 * units), bf16)],
         )
         attn_sum_grad = attn_sum_grad.reshape(row_tokens, width)
     else:

time: 762 us -> 753 us (0.988)
  Pallas kernels: 590 us -> 581 us
    pallas_call x12, Pallas kernels: 525 us -> 516 us  [remote_call(): pl.pallas_call(run, out_shape=[*outs, *late_outs, *traded], in_specs=[who...]
  transfers between devices with their start and end apart: 10 -> 10, of which waited for: 0 -> 0; matrix products, arithmetic and copies ran while one was open for 12% -> 12% of each run, Pallas kernels for 62% -> 63%
where the time goes in v5:
time: 753 us; the launch traced here: 742 us
  Pallas kernels  581 us (77%)
  other arithmetic  62.2 us (8%)
  matrix products  42.8 us (6%)
  local copies, waits for them, and re-layouts  32 us (4%)
  between operations  22.5 us (3%)
    pallas_call x12, Pallas kernels, remote_call(): pl.pallas_call(run, out_shape=[*outs, *late_outs, *traded], in_specs=[who...  516 us
    pallas_call x4, Pallas kernels, attention_call(): pl.pallas_call(run, grid_spec=pltpu.PrefetchScalarGridSpec(num_scalar_pre...  64.9 us
    dot_general x6, matrix products, dot(): lax.dot_general(left, right, (((left_dim,), (right_dim,)), ((), ())), pre...  41 us
    sub x7, other arithmetic, adamw(): weight - rate * (step_size + decay * weight)  16.2 us
  transfers between devices with their start and end apart: 10, of which 0 were waited for; matrix products, arithmetic and copies ran while one was open for 12% of the time, Pallas kernels for 63%

profile of v5, /device:TPU:0, one launch (start us, length us, event | category | flops | bytes accessed | tf_op | source)
XLA Modules:
  0.0 741.6 jit_solution(1779493504530162472)
XLA Ops:
  15.9 33.1 %modulation_exchange.1 = (f32[4,8,16,192]{3,2,1,0:T(8,128)}, bf16[192,2048]{1,0:T(8,128)(2,1)}) custom-call(f32[8,16,192]{2,1,0:T(8,128)} %pad_maximum_fusion.13.refs_0_, bf16[192,2048]{1,0:T(8,128)(2,1)} %pad_maximum_fusion.7.refs_1_), custom_call_target="tpu_custom_call" | custom-call | flops 1048576 | bytes 1048576 | tf_op jit(solution)/shard_map/modulation_exchange/pallas_call | solution.py:262
  63.3 41.9 %enter.1 = (bf16[4,256,1536]{2,1,0:T(8,128)(2,1)}, bf16[768,1024]{1,0:T(8,128)(2,1)}) custom-call(bf16[256,1536]{1,0:T(8,128)(2,1)} %refs_2_.7, f32[8,6144]{1,0:T(8,128)} %reshape.480.refs_1_.refs_3_.refs_2_, f32[256,8]{1,0:T(8,128)} %fusion.21.refs_2_.refs_4_.refs_3_, f32[8,1536]{1,0:T(8,128)} %reshape.481.refs_3_.refs_5_.refs_7_, ...), custom_call_target="tpu_custom_call" | custom-call | flops 1048576 | bytes 1048576 | tf_op jit(solution)/shard_map/enter/pallas_call | solution.py:262
  109.2 54.4 %project.2 = (f32[384,2048]{1,0:T(8,128)}, bf16[768,1408]{1,0:T(8,128)(2,1)}) custom-call(bf16[1536,1024]{1,0:T(8,128)(2,1)} %bitcast.170, bf16[2048,1024]{1,0:T(8,128)(2,1)} %refs_1_.11, bf16[768,1408]{1,0:T(8,128)(2,1)} %all-gather.8.cloned.1.call-done.refs_2_), custom_call_target="tpu_custom_call" | custom-call | flops 1048576 | bytes 1048576 | tf_op jit(solution)/shard_map/project/pallas_call | solution.py:262
  167.8 45.9 %project.3 = (f32[384,2048]{1,0:T(8,128)}, bf16[768,1152]{1,0:T(8,128)(2,1)}) custom-call(bf16[1536,1024]{1,0:T(8,128)(2,1)} %bitcast.169, bf16[2048,1024]{1,0:T(8,128)(2,1)} %refs_1_.11, bf16[768,1152]{1,0:T(8,128)(2,1)} %all-gather.6.cloned.1.call-done.refs_2_), custom_call_target="tpu_custom_call" | custom-call | flops 1048576 | bytes 1048576 | tf_op jit(solution)/shard_map/project/pallas_call | solution.py:262
  218.7 6.0 fusion.44.refs_8_.refs_9_.refs_10_.refs_16_.refs_17_
  224.7 11.7 %self_forward.1 = (bf16[384,1024]{1,0:T(8,128)(2,1)}, bf16[384,1024]{1,0:T(8,128)(2,1)}, bf16[6,1024,64]{2,1,0:T(8,128)(2,1)}, bf16[6,1024,64]{2,1,0:T(8,128)(2,...) custom-call(s32[8]{0:T(128)} %reshape.479.refs_0_, s32[1,1024]{1,0:T(1,128)} %refs_1_.9, s32[1024,1]{1,0:T(8,128)} %copy.130.refs_2_, ...), custom_call_target="tpu_custom_call" | custom-call | flops 15000 | bytes 15000 | tf_op jit(solution)/shard_map/self_forward/pallas_call | solution.py:1189
  236.4 15.9 %cross_forward.1 = (bf16[384,2048]{1,0:T(8,128)(2,1)}, bf16[6,2048,64]{2,1,0:T(8,128)(2,1)}, bf16[6,2048,64]{2,1,0:T(8,128)(2,1)}, f32[384,1024]{1,0:T(8,128)}, ...) custom-call(s32[8]{0:T(128)} %reshape.477.refs_0_, s32[8]{0:T(128)} %bitcast.213, s32[1,1024]{1,0:T(1,128)} %refs_1_.9, ...), custom_call_target="tpu_custom_call" | custom-call | flops 18000 | bytes 18000 | tf_op jit(solution)/shard_map/cross_forward/pallas_call | solution.py:1189
  254.9 48.5 %attention_out.1 = (f32[256,1536]{1,0:T(8,128)}, f32[256,1536]{1,0:T(8,128)}, bf16[4,256,1536]{2,1,0:T(8,128)(2,1)}, bf16[768,1024]{1,0:T(8,128)(2,1)}) custom-call(bf16[384,1024]{1,0:T(8,128)(2,1)} %get-tuple-element.84.refs_0_, bf16[1536,384]{1,0:T(8,128)(2,1)} %bitcast.190, bf16[256,1536]{1,0:T(8,128)(2,1)} %refs_2_.7, ...), custom_call_target="tpu_custom_call" | custom-call | flops 1048576 | bytes 1048576 | tf_op jit(solution)/shard_map/attention_out/pallas_call | solution.py:262
  307.0 52.2 %feed_forward.1 = (bf16[1024,1024]{1,0:T(8,128)(2,1)}, f32[256,1536]{1,0:T(8,128)}, f32[1,8,1536]{2,1,0:T(8,128)}, f32[1,8,1536]{2,1,0:T(8,128)}, bf16[4,256,1536]{2,1,0:T(8,128)(2,1)}, /*index=5*/f32[1024,2048]{1,0:T(8,128)}) custom-call(bf16[1024,1536]{1,0:T(8,128)(2,1)} %bitcast.196, bf16[1536,2048]{1,0:T(8,128)(2,1)} %all-gather.14.cloned.1.call-done.refs_1_.refs_7_, ...), custom_call_target="tpu_custom_call" | custom-call | flops 1048576 | bytes 1048576 | tf_op jit(solution)/shard_map/feed_forward/pallas_call | solution.py:262
  359.2 7.6 %convolution_convert_fusion.2 = bf16[1536,1024]{1,0:T(8,128)(2,1)} fusion(bf16[1024,1536]{1,0:T(8,128)(2,1)} %bitcast.192, bf16[1024,1024]{1,0:T(8,128)(2,1)} %get-tuple-element.97), kind=kOutput, calls=%fused_computation.2 | convolution fusion | flops 3222798336 | bytes 8388608 | tf_op jit(solution)/shard_map/dot_general | solution.py:40
  366.8 53.5 %feed_backward.1 = (f32[256,1536]{1,0:T(8,128)}, f32[2,8,1536]{2,1,0:T(8,128)}, f32[2,8,1536]{2,1,0:T(8,128)}, bf16[4,256,1536]{2,1,0:T(8,128)(2,1)}, bf16[1024,...) custom-call(bf16[1024,1536]{1,0:T(8,128)(2,1)} %bitcast.193, bf16[1536,1024]{1,0:T(8,128)(2,1)} %bitcast.166, ...), custom_call_target="tpu_custom_call" | custom-call | flops 1048576 | bytes 1048576 | tf_op jit(solution)/shard_map/feed_backward/pallas_call | solution.py:262
  420.4 3.4 fusion.1
  423.8 11.3 %convolution_convert_fusion.1.after = bf16[1536,2048]{1,0:T(8,128)(2,1)} fusion(bf16[1024,1536]{1,0:T(8,128)(2,1)} %bitcast.197, bf16[1024,2048]{1,0:T(8,128)(2,1)} %get-tuple-element.99), kind=kOutput, calls=%fused_computation.1 | convolution fusion | flops 6445596672 | bytes 13631488 | tf_op jit(solution)/shard_map/dot_general | solution.py:40
  437.0 4.0 convolution_convert_fusion.3
  442.3 4.5 fusion.45.refs_10_.refs_14_
  446.8 20.5 %cross_backward.1 = (f32[384,1024]{1,0:T(8,128)}, bf16[384,2048]{1,0:T(8,128)(2,1)}, bf16[384,2048]{1,0:T(8,128)(2,1)}, f32[384,256]{1,0:T(8,128)}) custom-call(s32[8]{0:T(128)} %reshape.477.refs_0_, s32[8]{0:T(128)} %bitcast.214, s32[1,1024]{1,0:T(1,128)} %refs_1_.9, f32[384,4]{1,0:T(8,128)} %dynamic-slice_bitcast_fusion.refs_3_, ...), custom_call_target="tpu_custom_call" | custom-call | flops 25000 | bytes 25000 | tf_op jit(solution)/shard_map/cross_backward/pallas_call | solution.py:1189
  467.4 16.8 %self_backward.1 = (bf16[1152,1024]{1,0:T(8,128)(2,1)}, f32[384,256]{1,0:T(8,128)}) custom-call(s32[8]{0:T(128)} %reshape.479.refs_0_, s32[1,1024]{1,0:T(1,128)} %refs_1_.9, s32[1024,1]{1,0:T(8,128)} %copy.130.refs_2_, f32[384,4]{1,0:T(8,128)} %dynamic-slice_bitcast_fusion.refs_3_, f32[32,1024]{1,0:T(8,128)} %get-tuple-element.184.refs_4_.refs_6_, ...), custom_call_target="tpu_custom_call" | custom-call | flops 25000 | bytes 25000 | tf_op jit(solution)/shard_map/self_backward/pallas_call | solution.py:1189
  484.2 7.6 %convolution_convert_fusion = bf16[1536,1152]{1,0:T(8,128)(2,1)} fusion(bf16[1024,1536]{1,0:T(8,128)(2,1)S(1)} %bitcast.217, bf16[1152,1024]{1,0:T(8,128)(2,1)} %get-tuple-element.107.refs_0_), kind=kOutput, calls=%fused_computation | convolution fusion | flops 3625648128 | bytes 9043968 | tf_op jit(solution)/shard_map/dot_general | solution.py:40
  491.8 50.8 %enter_backward.1 = (f32[256,1536]{1,0:T(8,128)}, f32[1,8,1536]{2,1,0:T(8,128)}, f32[1,8,1536]{2,1,0:T(8,128)}, bf16[4,192,1152]{2,1,0:T(8,128)(2,1)}) custom-call(bf16[1152,1024]{1,0:T(8,128)(2,1)} %get-tuple-element.107.refs_0_, bf16[1536,1152]{1,0:T(8,128)(2,1)} %bitcast.168, bf16[256,1536]{1,0:T(8,128)(2,1)} %refs_2_.7, ...), custom_call_target="tpu_custom_call" | custom-call | flops 1048576 | bytes 1048576 | tf_op jit(solution)/shard_map/enter_backward/pallas_call | solution.py:262
  545.8 55.3 %text_gradient.2 = (bf16[4,192,1024]{2,1,0:T(8,128)(2,1)}, bf16[4,384,2048]{2,1,0:T(8,128)(2,1)}, bf16[4,192,384]{2,1,0:T(8,128)(2,1)}) custom-call(bf16[384,2048]{1,0:T(8,128)(2,1)} %get-tuple-element.120.refs_0_, bf16[2048,1024]{1,0:T(8,128)(2,1)} %refs_1_.11, bf16[4,2,192,384]{3,2,1,0:T(8,128)(2,1)} %bitcast.198, f32[256,1536]{1,0:T(8,128)} %get-tuple-element.218.refs_3_), custom_call_target="tpu_custom_call" | custom-call | flops 1048576 | bytes 1048576 | tf_op jit(solution)/shard_map/text_gradient/pallas_call | solution.py:262
  604.5 45.2 %text_gradient.3 = (bf16[4,192,1024]{2,1,0:T(8,128)(2,1)}, bf16[4,384,2048]{2,1,0:T(8,128)(2,1)}) custom-call(bf16[384,2048]{1,0:T(8,128)(2,1)} %get-tuple-element.124.refs_0_, bf16[2048,1024]{1,0:T(8,128)(2,1)} %refs_1_.11, bf16[384,2048]{1,0:T(8,128)(2,1)} %reduce-scatter.10.cloned.1.call-done.refs_2_, bf16[768,1024]{1,0:T(8,128)(2,1)} %bitcast.188), custom_call_target="tpu_custom_call" | custom-call | flops 1048576 | bytes 1048576 | tf_op jit(solution)/shard_map/text_gradient/pallas_call | solution.py:262
  652.9 24.6 %modulation_return.1 = (f32[8,16,192]{2,1,0:T(8,128)}, bf16[1,192,2048]{2,1,0:T(8,128)(2,1)}) custom-call(f32[4,8,16,192]{3,2,1,0:T(8,128)} %pad_maximum_fusion.10.refs_0_, bf16[1,2,192,2048]{3,2,1,0:T(8,128)(2,1)} %bitcast.171, bf16[192,1152]{1,0:T(8,128)(2,1)} %reduce-scatter.8.cloned.1.call-done.refs_2_.value), custom_call_target="tpu_custom_call" | custom-call | flops 1048576 | bytes 1048576 | tf_op jit(solution)/shard_map/modulation_return/pallas_call | solution.py:262
  681.4 3.3 multiply_reduce_fusion
  698.4 10.8 %norm_exchange.1 = f32[8,128]{1,0:T(8,128)} custom-call(f32[8,128]{1,0:T(8,128)} %broadcast_in_dim.22.refs_0_), custom_call_target="tpu_custom_call" | custom-call | flops 1048576 | bytes 1048576 | tf_op jit(solution)/shard_map/norm_exchange/pallas_call | solution.py:262
  (260 shorter events, 90.3 us)
Async XLA Ops:
  7.2 56.1 %all-gather.10.cloned.1.call-start = ((), (), s32[]{:S(2)}) async-start(), calls=%async_computation.7 | async-start | bytes 1966080 | tf_op jit(solution)/shard_map/all_gather | solution.py:93
  9.6 99.6 %all-gather.8.cloned.1.call-start = ((), (), s32[]{:S(2)}) async-start(), calls=%async_computation.6 | async-start | bytes 2703360 | tf_op jit(solution)/shard_map/all_gather | solution.py:93
  10.7 157.1 %all-gather.6.cloned.1.call-start = ((), (), s32[]{:S(2)}) async-start(), calls=%async_computation.5 | async-start | bytes 2211840 | tf_op jit(solution)/shard_map/all_gather | solution.py:93
  11.7 243.1 %all-gather.12.cloned.1.call-start = ((), (), s32[]{:S(2)}) async-start(), calls=%async_computation.8 | async-start | bytes 1966080 | tf_op jit(solution)/shard_map/all_gather | solution.py:93
  12.6 294.3 %all-gather.14.cloned.1.call-start = ((), (), s32[]{:S(2)}) async-start(), calls=%async_computation.9 | async-start | bytes 7864320 | tf_op jit(solution)/shard_map/all_gather | solution.py:93
  51.8 5.6 copy-start.57
  51.8 415.5 %reduce-scatter.6.cloned.1.call-start = ((), (), s32[]{:S(2)}) async-start(), calls=%async_computation.10 | async-start | bytes 1966080 | tf_op jit(solution)/shard_map/reduce_scatter | solution.py:122
  63.3 42.0 %copy-start.11 = (bf16[768,1024]{1,0:T(8,128)(2,1)S(1)}, bf16[768,1024]{1,0:T(8,128)(2,1)}, u32[]{:S(2)}) copy-start(bf16[768,1024]{1,0:T(8,128)(2,1)} %all-gather.10.cloned.1.call-done.refs_4_) | copy-start | bytes 4718596
  109.2 54.4 %copy-start.2 = (bf16[768,1408]{1,0:T(8,128)(2,1)S(1)}, bf16[768,1408]{1,0:T(8,128)(2,1)}, u32[]{:S(2)}) copy-start(bf16[768,1408]{1,0:T(8,128)(2,1)} %all-gather.8.cloned.1.call-done.refs_2_) | copy-start | bytes 6488068
  167.8 45.9 %copy-start.6 = (bf16[768,1152]{1,0:T(8,128)(2,1)S(1)}, bf16[768,1152]{1,0:T(8,128)(2,1)}, u32[]{:S(2)}) copy-start(bf16[768,1152]{1,0:T(8,128)(2,1)} %all-gather.6.cloned.1.call-done.refs_2_) | copy-start | bytes 5308420
  215.9 8.8 %copy-start = (bf16[4,2,192,1152]{3,2,1,0:T(8,128)(2,1)}, bf16[4,2,192,1152]{3,2,1,0:T(8,128)(2,1)S(1)}, u32[]{:S(2)}) copy-start(bf16[4,2,192,1152]{3,2,1,0:T(8,128)(2,1)S(1)} %pad_maximum_fusion) | copy-start | bytes 10616836
  254.9 48.5 %copy-start.10 = (bf16[768,1024]{1,0:T(8,128)(2,1)S(1)}, bf16[768,1024]{1,0:T(8,128)(2,1)}, u32[]{:S(2)}) copy-start(bf16[768,1024]{1,0:T(8,128)(2,1)} %all-gather.12.cloned.1.call-done.refs_6_) | copy-start | bytes 4718596
  366.8 53.6 %copy-start.4 = (bf16[1536,1024]{1,0:T(8,128)(2,1)S(1)}, bf16[1536,1024]{1,0:T(8,128)(2,1)}, u32[]{:S(2)}) copy-start(bf16[1536,1024]{1,0:T(8,128)(2,1)} %convolution_convert_fusion.2) | copy-start | bytes 9437188
  423.7 180.7 %reduce-scatter.10.cloned.1.call-start = ((), (), s32[]{:S(2)}) async-start(), calls=%async_computation.12 | async-start | bytes 7864320 | tf_op jit(solution)/shard_map/reduce_scatter | solution.py:1577
  435.1 217.7 %reduce-scatter.8.cloned.1.call-start = ((), (), s32[]{:S(2)}) async-start(), calls=%async_computation.11 | async-start | bytes 2211840 | tf_op jit(solution)/shard_map/reduce_scatter | solution.py:122
  467.4 16.8 %copy-start.59 = (bf16[4,256,1536]{2,1,0:T(8,128)(2,1)S(1)}, bf16[4,256,1536]{2,1,0:T(8,128)(2,1)}, u32[]{:S(2)}) copy-start(bf16[4,256,1536]{2,1,0:T(8,128)(2,1)} %get-tuple-element.79) | copy-start | bytes 9437188
  491.8 50.8 %copy-start.3 = (bf16[1536,1152]{1,0:T(8,128)(2,1)S(1)}, bf16[1536,1152]{1,0:T(8,128)(2,1)}, u32[]{:S(2)}) copy-start(bf16[1536,1152]{1,0:T(8,128)(2,1)} %convolution_convert_fusion) | copy-start | bytes 10616836
  545.7 131.8 %reduce-scatter.12.cloned.1.call-start = ((), (), s32[]{:S(2)}) async-start(), calls=%async_computation.13 | async-start | bytes 2703360 | tf_op jit(solution)/shard_map/reduce_scatter | solution.py:122
  545.8 55.3 %copy-start.26 = (bf16[1536,384]{1,0:T(8,128)(2,1)S(1)}, bf16[1536,384]{1,0:T(8,128)(2,1)}, u32[]{:S(2)}) copy-start(bf16[1536,384]{1,0:T(8,128)(2,1)} %convolution_convert_fusion.3) | copy-start | bytes 3538948
  604.2 89.8 %reduce-scatter.14.cloned.1.call-start = ((), (), s32[]{:S(2)}) async-start(), calls=%async_computation.14 | async-start | bytes 1966080 | tf_op jit(solution)/shard_map/reduce_scatter | solution.py:122
  681.4 6.4 copy-start.27
  681.4 7.7 %copy-start.16 = (bf16[192,1408]{1,0:T(8,128)(2,1)S(1)}, bf16[192,1408]{1,0:T(8,128)(2,1)}, u32[]{:S(2)}) copy-start(bf16[192,1408]{1,0:T(8,128)(2,1)} %gate.6) | copy-start | bytes 1622020
  694.0 19.4 %copy-start.15 = (bf16[192,1024]{1,0:T(8,128)(2,1)S(1)}, bf16[192,1024]{1,0:T(8,128)(2,1)}, u32[]{:S(2)}) copy-start(bf16[192,1024]{1,0:T(8,128)(2,1)} %gate.7) | copy-start | bytes 1179652
  694.0 19.4 %copy-start.24 = (f32[1024,192]{0,1:T(8,128)S(1)}, f32[1024,192]{0,1:T(8,128)}, u32[]{:S(2)}) copy-start(f32[1024,192]{0,1:T(8,128)} %param.40) | copy-start | bytes 2359300
  (46 other events, 113.0 us)
Sparse Core Ops, SparseCore 0:
  10.2 42.3 all-gather.9
  54.7 46.0 all-gather.7
  102.9 39.0 all-gather.5
  143.9 35.9 all-gather.11
  181.9 114.1 all-gather.13
  423.9 33.4 reduce-scatter.5
  459.7 109.6 reduce-scatter.9
  571.7 38.9 reduce-scatter.7
  613.1 44.0 reduce-scatter.11
  659.3 34.6 reduce-scatter.13

commit v6 on v5

--- a/solution.py
+++ b/solution.py
@@ -710,7 +710,10 @@
     sum_blocks(transposed_partial(triple, weight, lhs, latents.shape[0]), finish, work, sems)
 
 
-def text_kernel(own, captions, summed, gathered, kept, sent, arrived, sems):
+def text_kernel(
+    own, captions_far, summed, gathered, kept, sent, arrived, captions, moves, sems
+):
+    (load,) = begin_copies([(captions_far, captions)], moves)
     mine, near, far, both = row_peers()
     other = dp_neighbour()
     odd = 1 - other % 2
@@ -754,6 +757,7 @@
         gathered[mine, part(k), :] = own[part(k), :]
         begin(move(mine, k, 0, far))
         begin(move(mine, k, 1, near))
+    load.wait()
     for k in range(CHUNKS):
         work(mine, 0, k)
     for k in range(CHUNKS):
@@ -1694,21 +1698,25 @@
             parts = parts.reshape(dp_size // 2, 2, -1, columns)
             return (sum_half(parts, swap_half(parts)), *(swap_half(array) for array in carry))
         kept = (tensor_size, local // 2, columns)
-        summed, _, *others = remote_call(
+        summed, *others = remote_call(
             text_kernel,
             "text_gradient",
             number,
-            [grad, captions],
-            [shape(kept, bf16), shape((tensor_size, local, slots), bf16)],
+            [grad],
+            [shape(kept, bf16)],
             [
+                pltpu.VMEM((tensor_size, local, slots), bf16),
                 pltpu.VMEM(kept, f32),
                 pltpu.VMEM(kept, bf16),
                 pltpu.VMEM(kept, bf16),
+                pltpu.VMEM(captions.shape, bf16),
+                pltpu.SemaphoreType.DMA((1,)),
                 semaphores(5 * CHUNKS),
             ],
             carry,
             neighbour=True,
             after=after,
+            late=[captions],
         )
         return (flat(summed), *others)
 

time: 753 us -> 752 us (level)
    pallas_call x12, Pallas kernels: 516 us -> 502 us  [remote_call(): pl.pallas_call(run, out_shape=[*outs, *late_outs, *traded], in_specs=[who...]
  transfers between devices with their start and end apart: 10 -> 10, of which waited for: 0 -> 1; matrix products, arithmetic and copies ran while one was open for 12% -> 12% of each run, Pallas kernels for 63% -> 62%
where the time goes in v6:
time: 752 us; the launch traced here: 741 us
  Pallas kernels  574 us (76%)
  other arithmetic  62.2 us (8%)
  matrix products  42.6 us (6%)
  local copies, waits for them, and re-layouts  32 us (4%)
  between operations  22.5 us (3%)
    pallas_call x12, Pallas kernels, remote_call(): pl.pallas_call(run, out_shape=[*outs, *late_outs, *traded], in_specs=[who...  502 us
    pallas_call x4, Pallas kernels, attention_call(): pl.pallas_call(run, grid_spec=pltpu.PrefetchScalarGridSpec(num_scalar_pre...  72.2 us
    dot_general x6, matrix products, dot(): lax.dot_general(left, right, (((left_dim,), (right_dim,)), ((), ())), pre...  40.9 us
    sub x7, other arithmetic, adamw(): weight - rate * (step_size + decay * weight)  16.2 us
  transfers between devices with their start and end apart: 10, of which 1 were waited for; matrix products, arithmetic and copies ran while one was open for 12% of the time, Pallas kernels for 62%

profile of v6, /device:TPU:0, one launch (start us, length us, event | category | flops | bytes accessed | tf_op | source)
XLA Modules:
  0.0 740.9 jit_solution(1053562255360663296)
XLA Ops:
  15.9 33.1 %modulation_exchange.1 = (f32[4,8,16,192]{3,2,1,0:T(8,128)}, bf16[192,2048]{1,0:T(8,128)(2,1)}) custom-call(f32[8,16,192]{2,1,0:T(8,128)} %pad_maximum_fusion.13.refs_0_, bf16[192,2048]{1,0:T(8,128)(2,1)} %pad_maximum_fusion.7.refs_1_), custom_call_target="tpu_custom_call" | custom-call | flops 1048576 | bytes 1048576 | tf_op jit(solution)/shard_map/modulation_exchange/pallas_call | solution.py:262
  63.3 41.9 %enter.1 = (bf16[4,256,1536]{2,1,0:T(8,128)(2,1)}, bf16[768,1024]{1,0:T(8,128)(2,1)}) custom-call(bf16[256,1536]{1,0:T(8,128)(2,1)} %refs_2_.7, f32[8,6144]{1,0:T(8,128)} %reshape.480.refs_1_.refs_3_.refs_2_, f32[256,8]{1,0:T(8,128)} %fusion.21.refs_2_.refs_4_.refs_3_, f32[8,1536]{1,0:T(8,128)} %reshape.481.refs_3_.refs_5_.refs_7_, ...), custom_call_target="tpu_custom_call" | custom-call | flops 1048576 | bytes 1048576 | tf_op jit(solution)/shard_map/enter/pallas_call | solution.py:262
  109.1 54.4 %project.2 = (f32[384,2048]{1,0:T(8,128)}, bf16[768,1408]{1,0:T(8,128)(2,1)}) custom-call(bf16[1536,1024]{1,0:T(8,128)(2,1)} %bitcast.170, bf16[2048,1024]{1,0:T(8,128)(2,1)} %refs_1_.11, bf16[768,1408]{1,0:T(8,128)(2,1)} %all-gather.8.cloned.1.call-done.refs_2_), custom_call_target="tpu_custom_call" | custom-call | flops 1048576 | bytes 1048576 | tf_op jit(solution)/shard_map/project/pallas_call | solution.py:262
  167.8 45.9 %project.3 = (f32[384,2048]{1,0:T(8,128)}, bf16[768,1152]{1,0:T(8,128)(2,1)}) custom-call(bf16[1536,1024]{1,0:T(8,128)(2,1)} %bitcast.169, bf16[2048,1024]{1,0:T(8,128)(2,1)} %refs_1_.11, bf16[768,1152]{1,0:T(8,128)(2,1)} %all-gather.6.cloned.1.call-done.refs_2_), custom_call_target="tpu_custom_call" | custom-call | flops 1048576 | bytes 1048576 | tf_op jit(solution)/shard_map/project/pallas_call | solution.py:262
  218.7 6.0 fusion.44.refs_8_.refs_9_.refs_10_.refs_16_.refs_17_
  224.6 13.9 %self_forward.1 = (bf16[384,1024]{1,0:T(8,128)(2,1)}, bf16[384,1024]{1,0:T(8,128)(2,1)}, bf16[6,1024,64]{2,1,0:T(8,128)(2,1)}, bf16[6,1024,64]{2,1,0:T(8,128)(2,...) custom-call(s32[8]{0:T(128)} %reshape.479.refs_0_, s32[1,1024]{1,0:T(1,128)} %refs_1_.9, s32[1024,1]{1,0:T(8,128)} %copy.130.refs_2_, ...), custom_call_target="tpu_custom_call" | custom-call | flops 15000 | bytes 15000 | tf_op jit(solution)/shard_map/self_forward/pallas_call | solution.py:1193
  238.5 16.4 %cross_forward.1 = (bf16[384,2048]{1,0:T(8,128)(2,1)}, bf16[6,2048,64]{2,1,0:T(8,128)(2,1)}, bf16[6,2048,64]{2,1,0:T(8,128)(2,1)}, f32[384,1024]{1,0:T(8,128)}, ...) custom-call(s32[8]{0:T(128)} %reshape.477.refs_0_, s32[8]{0:T(128)} %bitcast.213, s32[1,1024]{1,0:T(1,128)} %refs_1_.9, ...), custom_call_target="tpu_custom_call" | custom-call | flops 18000 | bytes 18000 | tf_op jit(solution)/shard_map/cross_forward/pallas_call | solution.py:1193
  257.6 45.8 %attention_out.1 = (f32[256,1536]{1,0:T(8,128)}, f32[256,1536]{1,0:T(8,128)}, bf16[4,256,1536]{2,1,0:T(8,128)(2,1)}, bf16[768,1024]{1,0:T(8,128)(2,1)}) custom-call(bf16[384,1024]{1,0:T(8,128)(2,1)} %get-tuple-element.83.refs_0_, bf16[1536,384]{1,0:T(8,128)(2,1)} %bitcast.191, bf16[256,1536]{1,0:T(8,128)(2,1)} %refs_2_.7, ...), custom_call_target="tpu_custom_call" | custom-call | flops 1048576 | bytes 1048576 | tf_op jit(solution)/shard_map/attention_out/pallas_call | solution.py:262
  307.0 52.2 %feed_forward.1 = (bf16[1024,1024]{1,0:T(8,128)(2,1)}, f32[256,1536]{1,0:T(8,128)}, f32[1,8,1536]{2,1,0:T(8,128)}, f32[1,8,1536]{2,1,0:T(8,128)}, bf16[4,256,1536]{2,1,0:T(8,128)(2,1)}, /*index=5*/f32[1024,2048]{1,0:T(8,128)}) custom-call(bf16[1024,1536]{1,0:T(8,128)(2,1)} %bitcast.197, bf16[1536,2048]{1,0:T(8,128)(2,1)} %all-gather.14.cloned.1.call-done.refs_1_.refs_7_, ...), custom_call_target="tpu_custom_call" | custom-call | flops 1048576 | bytes 1048576 | tf_op jit(solution)/shard_map/feed_forward/pallas_call | solution.py:262
  359.2 7.6 %convolution_convert_fusion.2 = bf16[1536,1024]{1,0:T(8,128)(2,1)} fusion(bf16[1024,1536]{1,0:T(8,128)(2,1)} %bitcast.193, bf16[1024,1024]{1,0:T(8,128)(2,1)} %get-tuple-element.96), kind=kOutput, calls=%fused_computation.2 | convolution fusion | flops 3222798336 | bytes 8388608 | tf_op jit(solution)/shard_map/dot_general | solution.py:40
  366.8 53.5 %feed_backward.1 = (f32[256,1536]{1,0:T(8,128)}, f32[2,8,1536]{2,1,0:T(8,128)}, f32[2,8,1536]{2,1,0:T(8,128)}, bf16[4,256,1536]{2,1,0:T(8,128)(2,1)}, bf16[1024,...) custom-call(bf16[1024,1536]{1,0:T(8,128)(2,1)} %bitcast.194, bf16[1536,1024]{1,0:T(8,128)(2,1)} %bitcast.166, ...), custom_call_target="tpu_custom_call" | custom-call | flops 1048576 | bytes 1048576 | tf_op jit(solution)/shard_map/feed_backward/pallas_call | solution.py:262
  420.4 3.3 fusion.1
  423.8 11.3 %convolution_convert_fusion.1.after = bf16[1536,2048]{1,0:T(8,128)(2,1)} fusion(bf16[1024,1536]{1,0:T(8,128)(2,1)} %bitcast.198, bf16[1024,2048]{1,0:T(8,128)(2,1)} %get-tuple-element.98), kind=kOutput, calls=%fused_computation.1 | convolution fusion | flops 6445596672 | bytes 13631488 | tf_op jit(solution)/shard_map/dot_general | solution.py:40
  437.0 4.0 convolution_convert_fusion.3
  442.3 4.5 fusion.45.refs_10_.refs_14_
  446.8 21.4 %cross_backward.1 = (f32[384,1024]{1,0:T(8,128)}, bf16[384,2048]{1,0:T(8,128)(2,1)}, bf16[384,2048]{1,0:T(8,128)(2,1)}, f32[384,256]{1,0:T(8,128)}) custom-call(s32[8]{0:T(128)} %reshape.477.refs_0_, s32[8]{0:T(128)} %bitcast.214, s32[1,1024]{1,0:T(1,128)} %refs_1_.9, f32[384,4]{1,0:T(8,128)} %dynamic-slice_bitcast_fusion.refs_3_, ...), custom_call_target="tpu_custom_call" | custom-call | flops 25000 | bytes 25000 | tf_op jit(solution)/shard_map/cross_backward/pallas_call | solution.py:1193
  468.2 20.5 %self_backward.1 = (bf16[1152,1024]{1,0:T(8,128)(2,1)}, f32[384,256]{1,0:T(8,128)}) custom-call(s32[8]{0:T(128)} %reshape.479.refs_0_, s32[1,1024]{1,0:T(1,128)} %refs_1_.9, s32[1024,1]{1,0:T(8,128)} %copy.130.refs_2_, f32[384,4]{1,0:T(8,128)} %dynamic-slice_bitcast_fusion.refs_3_, f32[32,1024]{1,0:T(8,128)} %get-tuple-element.182.refs_4_.refs_6_, ...), custom_call_target="tpu_custom_call" | custom-call | flops 25000 | bytes 25000 | tf_op jit(solution)/shard_map/self_backward/pallas_call | solution.py:1193
  488.7 7.5 %convolution_convert_fusion = bf16[1536,1152]{1,0:T(8,128)(2,1)} fusion(bf16[1024,1536]{1,0:T(8,128)(2,1)S(1)} %bitcast.217, bf16[1152,1024]{1,0:T(8,128)(2,1)} %get-tuple-element.106.refs_0_), kind=kOutput, calls=%fused_computation | convolution fusion | flops 3625648128 | bytes 9043968 | tf_op jit(solution)/shard_map/dot_general | solution.py:40
  496.2 46.4 %enter_backward.1 = (f32[256,1536]{1,0:T(8,128)}, f32[1,8,1536]{2,1,0:T(8,128)}, f32[1,8,1536]{2,1,0:T(8,128)}, bf16[4,192,1152]{2,1,0:T(8,128)(2,1)}) custom-call(bf16[1152,1024]{1,0:T(8,128)(2,1)} %get-tuple-element.106.refs_0_, bf16[1536,1152]{1,0:T(8,128)(2,1)} %bitcast.168, bf16[256,1536]{1,0:T(8,128)(2,1)} %refs_2_.7, ...), custom_call_target="tpu_custom_call" | custom-call | flops 1048576 | bytes 1048576 | tf_op jit(solution)/shard_map/enter_backward/pallas_call | solution.py:262
  545.9 52.0 %text_gradient.2 = (bf16[4,192,1024]{2,1,0:T(8,128)(2,1)}, bf16[4,192,384]{2,1,0:T(8,128)(2,1)}) custom-call(bf16[384,2048]{1,0:T(8,128)(2,1)} %get-tuple-element.119.refs_0_, bf16[2048,1024]{1,0:T(8,128)(2,1)} %refs_1_.11, bf16[4,2,192,384]{3,2,1,0:T(8,128)(2,1)} %bitcast.199, f32[256,1536]{1,0:T(8,128)} %get-tuple-element.216.refs_3_), custom_call_target="tpu_custom_call" | custom-call | flops 1048576 | bytes 1048576 | tf_op jit(solution)/shard_map/text_gradient/pallas_call | solution.py:262
  601.3 42.2 %text_gradient.3 = bf16[4,192,1024]{2,1,0:T(8,128)(2,1)} custom-call(bf16[384,2048]{1,0:T(8,128)(2,1)} %get-tuple-element.123.refs_0_, bf16[2048,1024]{1,0:T(8,128)(2,1)} %refs_1_.11, bf16[384,2048]{1,0:T(8,128)(2,1)} %reduce-scatter.10.cloned.1.call-done.refs_2_, bf16[768,1024]{1,0:T(8,128)(2,1)} %bitcast.183), custom_call_target="tpu_custom_call" | custom-call | flops 1048576 | bytes 1048576 | tf_op jit(solution)/shard_map/text_gradient/pallas_call | solution.py:262
  646.7 23.3 %modulation_return.1 = (f32[8,16,192]{2,1,0:T(8,128)}, bf16[1,192,2048]{2,1,0:T(8,128)(2,1)}) custom-call(f32[4,8,16,192]{3,2,1,0:T(8,128)} %pad_maximum_fusion.10.refs_0_, bf16[1,2,192,2048]{3,2,1,0:T(8,128)(2,1)} %bitcast.171, bf16[192,1152]{1,0:T(8,128)(2,1)} %reduce-scatter.8.cloned.1.call-done.refs_2_.value), custom_call_target="tpu_custom_call" | custom-call | flops 1048576 | bytes 1048576 | tf_op jit(solution)/shard_map/modulation_return/pallas_call | solution.py:262
  686.6 6.7 reduce-scatter.14.cloned.1.call-done
  697.6 10.9 %norm_exchange.1 = f32[8,128]{1,0:T(8,128)} custom-call(f32[8,128]{1,0:T(8,128)} %broadcast_in_dim.22.refs_0_), custom_call_target="tpu_custom_call" | custom-call | flops 1048576 | bytes 1048576 | tf_op jit(solution)/shard_map/norm_exchange/pallas_call | solution.py:262
  (260 shorter events, 93.7 us)
Async XLA Ops:
  7.2 56.1 %all-gather.10.cloned.1.call-start = ((), (), s32[]{:S(2)}) async-start(), calls=%async_computation.7 | async-start | bytes 1966080 | tf_op jit(solution)/shard_map/all_gather | solution.py:93
  9.6 99.5 %all-gather.8.cloned.1.call-start = ((), (), s32[]{:S(2)}) async-start(), calls=%async_computation.6 | async-start | bytes 2703360 | tf_op jit(solution)/shard_map/all_gather | solution.py:93
  10.7 157.1 %all-gather.6.cloned.1.call-start = ((), (), s32[]{:S(2)}) async-start(), calls=%async_computation.5 | async-start | bytes 2211840 | tf_op jit(solution)/shard_map/all_gather | solution.py:93
  11.7 245.9 %all-gather.12.cloned.1.call-start = ((), (), s32[]{:S(2)}) async-start(), calls=%async_computation.8 | async-start | bytes 1966080 | tf_op jit(solution)/shard_map/all_gather | solution.py:93
  12.6 294.3 %all-gather.14.cloned.1.call-start = ((), (), s32[]{:S(2)}) async-start(), calls=%async_computation.9 | async-start | bytes 7864320 | tf_op jit(solution)/shard_map/all_gather | solution.py:93
  51.8 5.6 copy-start.57
  51.8 416.4 %reduce-scatter.6.cloned.1.call-start = ((), (), s32[]{:S(2)}) async-start(), calls=%async_computation.10 | async-start | bytes 1966080 | tf_op jit(solution)/shard_map/reduce_scatter | solution.py:122
  63.3 41.9 %copy-start.12 = (bf16[768,1024]{1,0:T(8,128)(2,1)S(1)}, bf16[768,1024]{1,0:T(8,128)(2,1)}, u32[]{:S(2)}) copy-start(bf16[768,1024]{1,0:T(8,128)(2,1)} %all-gather.10.cloned.1.call-done.refs_4_) | copy-start | bytes 4718596
  109.1 54.4 %copy-start.2 = (bf16[768,1408]{1,0:T(8,128)(2,1)S(1)}, bf16[768,1408]{1,0:T(8,128)(2,1)}, u32[]{:S(2)}) copy-start(bf16[768,1408]{1,0:T(8,128)(2,1)} %all-gather.8.cloned.1.call-done.refs_2_) | copy-start | bytes 6488068
  167.8 45.9 %copy-start.6 = (bf16[768,1152]{1,0:T(8,128)(2,1)S(1)}, bf16[768,1152]{1,0:T(8,128)(2,1)}, u32[]{:S(2)}) copy-start(bf16[768,1152]{1,0:T(8,128)(2,1)} %all-gather.6.cloned.1.call-done.refs_2_) | copy-start | bytes 5308420
  215.9 8.8 %copy-start = (bf16[4,2,192,1152]{3,2,1,0:T(8,128)(2,1)}, bf16[4,2,192,1152]{3,2,1,0:T(8,128)(2,1)S(1)}, u32[]{:S(2)}) copy-start(bf16[4,2,192,1152]{3,2,1,0:T(8,128)(2,1)S(1)} %pad_maximum_fusion) | copy-start | bytes 10616836
  257.6 45.8 %copy-start.11 = (bf16[768,1024]{1,0:T(8,128)(2,1)S(1)}, bf16[768,1024]{1,0:T(8,128)(2,1)}, u32[]{:S(2)}) copy-start(bf16[768,1024]{1,0:T(8,128)(2,1)} %all-gather.12.cloned.1.call-done.refs_6_) | copy-start | bytes 4718596
  366.8 53.5 %copy-start.4 = (bf16[1536,1024]{1,0:T(8,128)(2,1)S(1)}, bf16[1536,1024]{1,0:T(8,128)(2,1)}, u32[]{:S(2)}) copy-start(bf16[1536,1024]{1,0:T(8,128)(2,1)} %convolution_convert_fusion.2) | copy-start | bytes 9437188
  423.7 177.6 %reduce-scatter.10.cloned.1.call-start = ((), (), s32[]{:S(2)}) async-start(), calls=%async_computation.12 | async-start | bytes 7864320 | tf_op jit(solution)/shard_map/reduce_scatter | solution.py:1581
  435.1 211.6 %reduce-scatter.8.cloned.1.call-start = ((), (), s32[]{:S(2)}) async-start(), calls=%async_computation.11 | async-start | bytes 2211840 | tf_op jit(solution)/shard_map/reduce_scatter | solution.py:122
  468.2 20.5 %copy-start.59 = (bf16[4,256,1536]{2,1,0:T(8,128)(2,1)S(1)}, bf16[4,256,1536]{2,1,0:T(8,128)(2,1)}, u32[]{:S(2)}) copy-start(bf16[4,256,1536]{2,1,0:T(8,128)(2,1)} %get-tuple-element.78) | copy-start | bytes 9437188
  496.2 46.4 %copy-start.3 = (bf16[1536,1152]{1,0:T(8,128)(2,1)S(1)}, bf16[1536,1152]{1,0:T(8,128)(2,1)}, u32[]{:S(2)}) copy-start(bf16[1536,1152]{1,0:T(8,128)(2,1)} %convolution_convert_fusion) | copy-start | bytes 10616836
  545.8 124.3 %reduce-scatter.12.cloned.1.call-start = ((), (), s32[]{:S(2)}) async-start(), calls=%async_computation.13 | async-start | bytes 2703360 | tf_op jit(solution)/shard_map/reduce_scatter | solution.py:122
  545.9 52.0 %copy-start.26 = (bf16[1536,384]{1,0:T(8,128)(2,1)S(1)}, bf16[1536,384]{1,0:T(8,128)(2,1)}, u32[]{:S(2)}) copy-start(bf16[1536,384]{1,0:T(8,128)(2,1)} %convolution_convert_fusion.3) | copy-start | bytes 3538948
  601.1 92.2 %reduce-scatter.14.cloned.1.call-start = ((), (), s32[]{:S(2)}) async-start(), calls=%async_computation.14 | async-start | bytes 1966080 | tf_op jit(solution)/shard_map/reduce_scatter | solution.py:122
  674.0 6.5 copy-start.27
  674.0 7.7 %copy-start.16 = (bf16[192,1408]{1,0:T(8,128)(2,1)S(1)}, bf16[192,1408]{1,0:T(8,128)(2,1)}, u32[]{:S(2)}) copy-start(bf16[192,1408]{1,0:T(8,128)(2,1)} %gate.6) | copy-start | bytes 1622020
  686.6 26.1 %copy-start.15 = (bf16[192,1024]{1,0:T(8,128)(2,1)S(1)}, bf16[192,1024]{1,0:T(8,128)(2,1)}, u32[]{:S(2)}) copy-start(bf16[192,1024]{1,0:T(8,128)(2,1)} %gate.7) | copy-start | bytes 1179652
  686.6 26.1 %copy-start.24 = (f32[1024,192]{0,1:T(8,128)S(1)}, f32[1024,192]{0,1:T(8,128)}, u32[]{:S(2)}) copy-start(f32[1024,192]{0,1:T(8,128)} %param.40) | copy-start | bytes 2359300
  (46 other events, 113.0 us)
Sparse Core Ops, SparseCore 0:
  10.2 42.3 all-gather.9
  54.7 46.0 all-gather.7
  102.9 39.0 all-gather.5
  143.9 35.9 all-gather.11
  181.9 114.1 all-gather.13
  423.8 32.7 reduce-scatter.5
  458.9 109.7 reduce-scatter.9
  571.0 38.9 reduce-scatter.7
  612.4 44.0 reduce-scatter.11
  658.6 34.6 reduce-scatter.13
